TPU v7x, 32 devices: a whole 2x2x4 slice. The times are simulated.
32 devices in a mesh: tm: 2 (over y), wall: 4 (over x, core), span: 4 (over z).
Axes of the slice: x: 2, y: 2, z: 4, core: 2. Of those that a mesh axis runs over, the one named last changes fastest.
Arguments:
- starting_speed_vector: float32 [3, 2, 16, 128, 512], P(None, 'tm', None, 'wall', 'span'), may hold values from -6 to 6
- driving_source: float32 [3, 2, 16, 128, 512], P(None, 'tm', None, 'wall', 'span'), may hold values from -3 to 3
- viscosity: float32 [128], P('wall'), may hold values from 0.02 to 0.2
Outputs:
- orbit: float32 [3, 2, 16, 128, 512], P(None, 'tm', None, 'wall', 'span')
- residual: float32 [3, 2, 16, 128, 512], P(None, 'tm', None, 'wall', 'span')
All inputs are finite; a program needn't handle non-finite values.
Results may differ from a plain program's by a relative error of at most 0.0001.
Values sent between devices are 32-bit elements; how exact they have to be, the bound alone decides.
No kernel may reach another device: no remote copies, remote signals or barrier semaphores. Data moves between devices by JAX's collectives and lax.ppermute only.
A program may use at most 64 MiB of HBM per device.

v0:
```python
import jax
import jax.numpy as jnp
from jax import lax
from jax.sharding import PartitionSpec as P

ITERS = 2


step_rate = 0.05


def with_halo(cells, sides, width, closed):
    for axis, dim in sides:
        count = lax.axis_size(axis)
        ends = count if closed else count - 1
        head = lax.slice_in_dim(cells, 0, width, axis=dim)
        tail = lax.slice_in_dim(cells, cells.shape[dim] - width, cells.shape[dim], axis=dim)
        cells = jnp.concatenate(
            [
                lax.ppermute(tail, axis, [(i, (i + 1) % count) for i in range(ends)]),
                cells,
                lax.ppermute(head, axis, [((i + 1) % count, i) for i in range(ends)]),
            ],
            axis=dim,
        )
    return cells


def partner_2(value, axis, bit):
    mask = 2**bit
    pairs = [(source, source ^ mask) for source in range(lax.axis_size(axis))]
    return lax.ppermute(value, axis, pairs)


def time_pair(values):
    padded_state = with_halo(values, (("tm", 1),), 1, True)
    return (padded_state[:, 2:], padded_state[:, :-2])


def wall_pair(values):
    padded_state = with_halo(values, (("wall", 3),), 1, False)
    return (padded_state[:, :, :, 2:], padded_state[:, :, :, :-2])


def span_pair(values):
    padded_state = with_halo(values, (("span", 4),), 1, True)
    return (padded_state[:, :, :, :, 2:], padded_state[:, :, :, :, :-2])


def along_flow(values):
    return (jnp.roll(values, -1, 2), jnp.roll(values, 1, 2))


def reflect(values):
    stack_size = values.shape[0]
    sign_row = jnp.where(jnp.arange(stack_size) % 3 == 1, -1.0, 1.0).astype(jnp.float32)
    sign_row = sign_row.reshape(stack_size, 1, 1, 1, 1)
    wall_bits = lax.axis_size("wall").bit_length() - 1
    time_bits = lax.axis_size("tm").bit_length() - 1
    partner = values
    for bit_index in list(range(wall_bits)) + [wall_bits + time_bits - 1]:
        partner = partner_2(partner, ("tm", "wall"), bit_index)
    partner = partner[:, :, :, ::-1, :]
    return partner * sign_row


def residual_of(present_state, mirrored, driving_source, viscous):
    ahead_time, behind_time = time_pair(present_state)
    neighbours = (along_flow(present_state), wall_pair(present_state), span_pair(present_state))
    slopes = [0.5 * (ahead - behind) for ahead, behind in neighbours]
    advect = (
        present_state[0:1] * slopes[0]
        + present_state[1:2] * slopes[1]
        + present_state[2:3] * slopes[2]
    )
    laplace = neighbours[0][0] + neighbours[0][1] - 2.0 * present_state
    laplace = laplace + (neighbours[1][0] + neighbours[1][1] - 2.0 * present_state)
    laplace = laplace + (neighbours[2][0] + neighbours[2][1] - 2.0 * present_state)
    residual_now = (
        0.5 * (ahead_time - behind_time)
        + advect
        - viscous * laplace
        + 0.5 * (present_state - mirrored)
        - driving_source
    )
    return (residual_now, neighbours, slopes)


def descent_part(neighbours, slopes, residual_now, viscous):
    ahead_time, behind_time = time_pair(residual_now)
    scaled = viscous * residual_now
    wall_ahead, wall_behind = wall_pair(jnp.concatenate((residual_now, scaled), 0))
    flow_ahead, flow_behind = along_flow(residual_now)
    span_ahead, span_behind = span_pair(residual_now)
    residual_pairs = (
        (flow_ahead, flow_behind),
        (wall_ahead[:3], wall_behind[:3]),
        (span_ahead, span_behind),
    )
    transport = jnp.stack(
        [jnp.sum(residual_now * slopes[component], axis=0) for component in range(3)]
    )
    second = None
    for axis_id in range(3):
        ahead_u = neighbours[axis_id][0][axis_id : axis_id + 1]
        behind_u = neighbours[axis_id][1][axis_id : axis_id + 1]
        term = 0.5 * (ahead_u * residual_pairs[axis_id][0] - behind_u * residual_pairs[axis_id][1])
        second = term if second is None else second + term
    diffused = viscous * flow_ahead + viscous * flow_behind - 2.0 * scaled
    diffused = diffused + (wall_ahead[3:] + wall_behind[3:] - 2.0 * scaled)
    diffused = diffused + (viscous * span_ahead + viscous * span_behind - 2.0 * scaled)
    return -0.5 * (ahead_time - behind_time) + transport - second - diffused


def local(starting_speed_vector, driving_source, viscosity):
    viscous = viscosity[None, None, None, :, None]
    present_state = starting_speed_vector
    residual_now = starting_speed_vector
    mirrored = starting_speed_vector
    for iteration in range(ITERS):
        mirrored = reflect(present_state)
        residual_now, neighbours, slopes = residual_of(
            present_state, mirrored, driving_source, viscous
        )
        local_part = descent_part(neighbours, slopes, residual_now, viscous)
        mirror_residual = reflect(residual_now)
        present_state = present_state - step_rate * (
            local_part + 0.5 * (residual_now - mirror_residual)
        )
    return (present_state, residual_now)


def solution(mesh):
    placed = (P(None, "tm", None, "wall", "span"), P(None, "tm", None, "wall", "span"), P("wall"))
    return jax.shard_map(
        local,
        mesh=mesh,
        in_specs=placed,
        out_specs=(P(None, "tm", None, "wall", "span"), P(None, "tm", None, "wall", "span")),
        check_vma=False,
    )
```

profile of v0, /device:TPU:1, one launch (start us, length us, event | category | flops | bytes accessed | tf_op | source)
XLA Modules:
  0.0 253.3 jit_solution(6928495435831955603)
XLA Ops:
  0.8 2.4 collective-permute-done.6
  3.2 2.3 collective-permute-start.7
  7.0 1.7 fusion.67
  9.1 1.3 collective-permute-start.5
  10.8 2.1 collective-permute-start.4
  14.1 9.1 %collective-permute-done.7 = f32[3,1,16,32,128]{4,3,2,1,0:T(8,128)} collective-permute-done((f32[3,1,16,32,128]{4,3,2,1,0:T(8,128)S(1)}, f32[3,1,16,32,128]{4,3,2,1,0:T(8,128)}, u32[]{:S(2)}, u32[]{:S(2)}) %collective-permute-start.7) | collective-permute-done | bytes 786464 | tf_op jit(solution)/shard_map/ppermute | solution.py:32
  24.5 3.4 %collective-permute-start.2 = (f32[3,1,16,1,128]{4,2,3,1,0:T(8,128)S(1)}, f32[3,1,16,1,128]{4,2,3,1,0:T(8,128)S(1)}, u32[]{:S(2)}, u32[]{:S(2)}) collective-permute-start(f32[3,1,16,1,128]{4,2,3,1,0:T(8,128)S(1)} %bitcast.76), channel_id=1, source_target_pairs={{4,0},{8,4},{12,8},{5,1},{9,5},{13,9},{6,2},{10,6},{14,10},{7,3},{... | collective-permute-start | bytes 73736 | tf_op jit(solution)/shard_map/ppermute | solution.py:22
  27.9 3.0 %collective-permute-start.3 = (f32[3,1,16,1,128]{4,2,3,1,0:T(8,128)S(1)}, f32[3,1,16,1,128]{4,2,3,1,0:T(8,128)S(1)}, u32[]{:S(2)}, u32[]{:S(2)}) collective-permute-start(f32[3,1,16,1,128]{4,2,3,1,0:T(8,128)S(1)} %bitcast.74), channel_id=1, source_target_pairs={{0,4},{4,8},{8,12},{1,5},{5,9},{9,13},{2,6},{6,10},{10,14},{3,7},{... | collective-permute-start | bytes 73736 | tf_op jit(solution)/shard_map/ppermute | solution.py:20
  32.2 1.4 fusion.54
  33.6 24.3 %collective-permute-done.8 = f32[3,1,16,32,128]{4,3,2,1,0:T(8,128)S(1)} collective-permute-done((f32[3,1,16,32,128]{4,3,2,1,0:T(8,128)}, f32[3,1,16,32,128]{4,3,2,1,0:T(8,128)S(1)}, u32[]{:S(2)}, u32[]{:S(2)}) %collective-permute-start.8) | collective-permute-done | bytes 786464 | tf_op jit(solution)/shard_map/ppermute | solution.py:32
  59.0 4.5 %multiply_reduce_fusion.4 = (f32[16,32,128]{2,1,0:T(8,128)}, f32[16,32,128]{2,1,0:T(8,128)}, f32[16,32,128]{2,1,0:T(8,128)}, f32[3,1,16,32,128]{4,3,2,1,0:T(8,128)S(1)}) fusion(f32[3,1,16,1,128]{4,3,2,1,0:T(1,128)S(1)} %bitcast.67, f32[3,1,16,32,128]{4,3,2,1,0:T(8,128)S(1)} %copy-done, f32[3,1,16,1,128]{4,3,2,1,0:T(1,128)S(1)} %bitcast.71, ...), kind=kLoop, calls=%fused_computation.90 | loop fusion | flops 9240576 | bytes 7925900 | tf_op jit(solution)/shard_map/reduce_sum | solution.py:101
  63.5 1.5 collective-permute-start.15
  65.0 2.0 collective-permute-done.15
  68.0 1.5 collective-permute-start.10
  70.5 1.5 collective-permute-start.14
  72.0 2.1 collective-permute-start.13
  74.1 12.1 %collective-permute-done.16 = f32[3,1,16,32,128]{4,3,2,1,0:T(8,128)} collective-permute-done((f32[3,1,16,32,128]{4,3,2,1,0:T(8,128)}, f32[3,1,16,32,128]{4,3,2,1,0:T(8,128)}, u32[]{:S(2)}, u32[]{:S(2)}) %collective-permute-start.16) | collective-permute-done | bytes 786464 | tf_op jit(solution)/shard_map/ppermute | solution.py:32
  89.6 3.5 %collective-permute-start.12 = (f32[6,1,16,1,128]{4,2,3,1,0:T(8,128)}, f32[6,1,16,1,128]{4,2,3,1,0:T(8,128)S(1)}, u32[]{:S(2)}, u32[]{:S(2)}) collective-permute-start(f32[6,1,16,1,128]{4,2,3,1,0:T(8,128)} %bitcast.37), channel_id=1, source_target_pairs={{0,4},{4,8},{8,12},{1,5},{5,9},{9,13},{2,6},{6,10},{10,14},{3,7},{... | collective-permute-start | bytes 147464 | tf_op jit(solution)/shard_map/ppermute | solution.py:20
  93.8 1.9 collective-permute-start.11
  95.7 2.0 copy.91
  97.7 2.0 copy.93
  99.7 20.4 %collective-permute-done.17 = f32[3,1,16,32,128]{4,3,2,1,0:T(8,128)S(1)} collective-permute-done((f32[3,1,16,32,128]{4,3,2,1,0:T(8,128)}, f32[3,1,16,32,128]{4,3,2,1,0:T(8,128)S(1)}, u32[]{:S(2)}, u32[]{:S(2)}) %collective-permute-start.17) | collective-permute-done | bytes 786464 | tf_op jit(solution)/shard_map/ppermute | solution.py:32
  121.2 4.3 %fusion.28 = f32[3,1,16,32,128]{4,3,2,1,0:T(8,128)S(1)} fusion(f32[3,1,16,32,128]{4,3,2,1,0:T(8,128)S(1)} %copy-done, f32[6,1,16,1,128]{4,3,2,1,0:T(1,128)S(1)} %bitcast.72, f32[3,1,16,32,128]{4,3,2,1,0:T(8,128)S(1)} %broadcast_multiply_fusion.1, f32[3,1,16,32,128]{4,3,2,1,0:T(8,128)S(1)} %get-tuple-element.11, f32[6,1,16,1,128]{4,3,2,1,0:T(1,128)} %bitcast.11, ...), kind=kLoop, calls=%fused_computation.61 | loop fusion | flops 9437184 | bytes 9547916 | tf_op jit(solution)/shard_map/sub | solution.py:127
  125.6 1.6 collective-permute-start.24
  127.1 1.9 collective-permute-done.24
  129.0 1.4 collective-permute-start.25
  132.2 15.7 %collective-permute-done.25 = f32[3,1,16,32,128]{4,3,2,1,0:T(8,128)} collective-permute-done((f32[3,1,16,32,128]{4,3,2,1,0:T(8,128)S(1)}, f32[3,1,16,32,128]{4,3,2,1,0:T(8,128)}, u32[]{:S(2)}, u32[]{:S(2)}) %collective-permute-start.25) | collective-permute-done | bytes 786464 | tf_op jit(solution)/shard_map/ppermute | solution.py:32
  147.9 1.5 collective-permute-start.26
  152.7 2.1 collective-permute-start.22
  155.9 4.5 %collective-permute-start.20 = (f32[3,1,16,1,128]{4,2,3,1,0:T(8,128)S(1)}, f32[3,1,16,1,128]{4,2,3,1,0:T(8,128)S(1)}, u32[]{:S(2)}, u32[]{:S(2)}) collective-permute-start(f32[3,1,16,1,128]{4,2,3,1,0:T(8,128)S(1)} %bitcast.77), channel_id=1, source_target_pairs={{4,0},{8,4},{12,8},{5,1},{9,5},{13,9},{6,2},{10,6},{14,10},{7,3},{... | collective-permute-start | bytes 73736 | tf_op jit(solution)/shard_map/ppermute | solution.py:22
  160.5 3.0 %collective-permute-start.21 = (f32[3,1,16,1,128]{4,2,3,1,0:T(8,128)S(1)}, f32[3,1,16,1,128]{4,2,3,1,0:T(8,128)S(1)}, u32[]{:S(2)}, u32[]{:S(2)}) collective-permute-start(f32[3,1,16,1,128]{4,2,3,1,0:T(8,128)S(1)} %bitcast.75), channel_id=1, source_target_pairs={{0,4},{4,8},{8,12},{1,5},{5,9},{9,13},{2,6},{6,10},{10,14},{3,7},{... | collective-permute-start | bytes 73736 | tf_op jit(solution)/shard_map/ppermute | solution.py:20
  164.4 1.4 fusion.47
  165.8 16.9 %collective-permute-done.26 = f32[3,1,16,32,128]{4,3,2,1,0:T(8,128)} collective-permute-done((f32[3,1,16,32,128]{4,3,2,1,0:T(8,128)}, f32[3,1,16,32,128]{4,3,2,1,0:T(8,128)}, u32[]{:S(2)}, u32[]{:S(2)}) %collective-permute-start.26) | collective-permute-done | bytes 786464 | tf_op jit(solution)/shard_map/ppermute | solution.py:32
  182.7 1.9 rev.14
  184.7 4.5 %multiply_reduce_fusion.1 = (f32[16,32,128]{2,1,0:T(8,128)}, f32[16,32,128]{2,1,0:T(8,128)}, f32[16,32,128]{2,1,0:T(8,128)}, f32[3,1,16,32,128]{4,3,2,1,0:T(8,128)S(1)}) fusion(f32[3,1,16,1,128]{4,3,2,1,0:T(1,128)S(1)} %bitcast.65, f32[3,1,16,32,128]{4,3,2,1,0:T(8,128)S(1)} %fusion.28, f32[3,1,16,1,128]{4,3,2,1,0:T(1,128)S(1)} %bitcast.69, ...), kind=kLoop, calls=%fused_computation.85 | loop fusion | flops 9240576 | bytes 7925900 | tf_op jit(solution)/shard_map/reduce_sum | solution.py:101
  189.2 1.5 collective-permute-start.33
  190.7 2.0 collective-permute-done.33
  194.2 1.5 collective-permute-start.28
  196.7 1.5 collective-permute-start.32
  198.2 2.1 collective-permute-start.31
  200.3 11.5 %collective-permute-done.34 = f32[3,1,16,32,128]{4,3,2,1,0:T(8,128)} collective-permute-done((f32[3,1,16,32,128]{4,3,2,1,0:T(8,128)}, f32[3,1,16,32,128]{4,3,2,1,0:T(8,128)}, u32[]{:S(2)}, u32[]{:S(2)}) %collective-permute-start.34) | collective-permute-done | bytes 786464 | tf_op jit(solution)/shard_map/ppermute | solution.py:32
  213.2 1.3 fusion.55
  215.3 3.5 %collective-permute-start.30 = (f32[6,1,16,1,128]{4,2,3,1,0:T(8,128)}, f32[6,1,16,1,128]{4,2,3,1,0:T(8,128)S(1)}, u32[]{:S(2)}, u32[]{:S(2)}) collective-permute-start(f32[6,1,16,1,128]{4,2,3,1,0:T(8,128)} %bitcast.39), channel_id=1, source_target_pairs={{0,4},{4,8},{8,12},{1,5},{5,9},{9,13},{2,6},{6,10},{10,14},{3,7},{... | collective-permute-start | bytes 147464 | tf_op jit(solution)/shard_map/ppermute | solution.py:20
  219.4 1.9 collective-permute-start.29
  222.5 2.0 copy.109
  224.4 22.0 %collective-permute-done.35 = f32[3,1,16,32,128]{4,3,2,1,0:T(8,128)} collective-permute-done((f32[3,1,16,32,128]{4,3,2,1,0:T(8,128)}, f32[3,1,16,32,128]{4,3,2,1,0:T(8,128)}, u32[]{:S(2)}, u32[]{:S(2)}) %collective-permute-start.35) | collective-permute-done | bytes 786464 | tf_op jit(solution)/shard_map/ppermute | solution.py:32
  246.4 1.9 rev.15
  248.4 4.9 %fusion.15 = f32[3,1,16,32,128]{4,3,2,1,0:T(8,128)} fusion(f32[3,1,16,32,128]{4,3,2,1,0:T(8,128)S(1)} %fusion.28, f32[6,1,16,1,128]{4,3,2,1,0:T(1,128)S(1)} %bitcast.73, f32[3,1,16,32,128]{4,3,2,1,0:T(8,128)S(1)} %broadcast_multiply_fusion, f32[3,1,16,32,128]{4,3,2,1,0:T(8,128)S(1)} %get-tuple-element.10, f32[6,1,16,1,128]{4,3,2,1,0:T(1,128)} %bitcast.29, ...), kind=kLoop, calls=%fused_computation.40 | loop fusion | flops 9437184 | bytes 9547916 | tf_op jit(solution)/shard_map/sub | solution.py:127
  (96 shorter events, 27.7 us)
Async XLA Ops:
  0.6 2.6 %collective-permute-start.6 = (f32[3,1,16,32,128]{4,3,2,1,0:T(8,128)}, f32[3,1,16,32,128]{4,3,2,1,0:T(8,128)S(1)}, u32[]{:S(2)}, u32[]{:S(2)}) collective-permute-start(f32[3,1,16,32,128]{4,3,2,1,0:T(8,128)} %param.3), channel_id=1, source_target_pairs={{0,4},{4,0},{8,12},{12,8},{16,20},{20,16},{24,28},{28,24},{1,5},{5... | collective-permute-start | bytes 2359304 | tf_op jit(solution)/shard_map/ppermute | solution.py:32
  3.2 20.1 %collective-permute-start.7 = (f32[3,1,16,32,128]{4,3,2,1,0:T(8,128)S(1)}, f32[3,1,16,32,128]{4,3,2,1,0:T(8,128)}, u32[]{:S(2)}, u32[]{:S(2)}) collective-permute-start(f32[3,1,16,32,128]{4,3,2,1,0:T(8,128)S(1)} %collective-permute-done.6), channel_id=1, source_target_pairs={{0,8},{4,12},{8,0},{12,4},{16,24},{20,28},{24,16},{28,20},{1,9},{5... | collective-permute-start | bytes 2359304 | tf_op jit(solution)/shard_map/ppermute | solution.py:32
  5.5 53.5 %collective-permute-start.1 = (f32[3,1,16,32,128]{4,3,2,1,0:T(8,128)}, f32[3,1,16,32,128]{4,3,2,1,0:T(8,128)}, u32[]{:S(2)}, u32[]{:S(2)}) collective-permute-start(f32[3,1,16,32,128]{4,3,2,1,0:T(8,128)} %param.3), channel_id=1, source_target_pairs={{0,16},{16,0},{1,17},{17,1},{2,18},{18,2},{3,19},{19,3},{4,20},{20... | collective-permute-start | bytes 2359304 | tf_op jit(solution)/shard_map/ppermute | solution.py:20
  6.8 52.2 %collective-permute-start = (f32[3,1,16,32,128]{4,3,2,1,0:T(8,128)}, f32[3,1,16,32,128]{4,3,2,1,0:T(8,128)}, u32[]{:S(2)}, u32[]{:S(2)}) collective-permute-start(f32[3,1,16,32,128]{4,3,2,1,0:T(8,128)} %param.3), channel_id=1, source_target_pairs={{16,0},{0,16},{17,1},{1,17},{18,2},{2,18},{19,3},{3,19},{20,4},{4,... | collective-permute-start | bytes 2359304 | tf_op jit(solution)/shard_map/ppermute | solution.py:22
  8.7 4.1 %copy-start = (f32[3,1,16,32,128]{4,3,2,1,0:T(8,128)S(1)}, f32[3,1,16,32,128]{4,3,2,1,0:T(8,128)}, u32[]{:S(2)}) copy-start(f32[3,1,16,32,128]{4,3,2,1,0:T(8,128)} %param.3) | copy-start | bytes 2359300
  9.1 15.4 %collective-permute-start.5 = (f32[3,1,16,32,1]{3,2,4,1,0:T(8,128)S(1)}, f32[3,1,16,32,1]{3,2,4,1,0:T(8,128)S(1)}, u32[]{:S(2)}, u32[]{:S(2)}) collective-permute-start(f32[3,1,16,32,1]{3,2,4,1,0:T(8,128)S(1)} %copy.113), channel_id=1, source_target_pairs={{0,1},{1,2},{2,3},{3,0},{4,5},{5,6},{6,7},{7,4},{8,9},{9,10},{10,1... | collective-permute-start | bytes 18440 | tf_op jit(solution)/shard_map/ppermute | solution.py:20
  10.8 17.1 %collective-permute-start.4 = (f32[3,1,16,32,1]{3,2,4,1,0:T(8,128)S(1)}, f32[3,1,16,32,1]{3,2,4,1,0:T(8,128)S(1)}, u32[]{:S(2)}, u32[]{:S(2)}) collective-permute-start(f32[3,1,16,32,1]{3,2,4,1,0:T(8,128)S(1)} %copy.112), channel_id=1, source_target_pairs={{1,0},{2,1},{3,2},{0,3},{5,4},{6,5},{7,6},{4,7},{9,8},{10,9},{11,1... | collective-permute-start | bytes 18440 | tf_op jit(solution)/shard_map/ppermute | solution.py:22
  23.2 34.6 %collective-permute-start.8 = (f32[3,1,16,32,128]{4,3,2,1,0:T(8,128)}, f32[3,1,16,32,128]{4,3,2,1,0:T(8,128)S(1)}, u32[]{:S(2)}, u32[]{:S(2)}) collective-permute-start(f32[3,1,16,32,128]{4,3,2,1,0:T(8,128)} %collective-permute-done.7), channel_id=1, source_target_pairs={{0,16},{4,20},{8,24},{12,28},{16,0},{20,4},{24,8},{28,12},{1,17},{... | collective-permute-start | bytes 2359304 | tf_op jit(solution)/shard_map/ppermute | solution.py:32
  24.5 7.7 %collective-permute-start.2 = (f32[3,1,16,1,128]{4,2,3,1,0:T(8,128)S(1)}, f32[3,1,16,1,128]{4,2,3,1,0:T(8,128)S(1)}, u32[]{:S(2)}, u32[]{:S(2)}) collective-permute-start(f32[3,1,16,1,128]{4,2,3,1,0:T(8,128)S(1)} %bitcast.76), channel_id=1, source_target_pairs={{4,0},{8,4},{12,8},{5,1},{9,5},{13,9},{6,2},{10,6},{14,10},{7,3},{... | collective-permute-start | bytes 73736 | tf_op jit(solution)/shard_map/ppermute | solution.py:22
  27.9 4.3 %collective-permute-start.3 = (f32[3,1,16,1,128]{4,2,3,1,0:T(8,128)S(1)}, f32[3,1,16,1,128]{4,2,3,1,0:T(8,128)S(1)}, u32[]{:S(2)}, u32[]{:S(2)}) collective-permute-start(f32[3,1,16,1,128]{4,2,3,1,0:T(8,128)S(1)} %bitcast.74), channel_id=1, source_target_pairs={{0,4},{4,8},{8,12},{1,5},{5,9},{9,13},{2,6},{6,10},{10,14},{3,7},{... | collective-permute-start | bytes 73736 | tf_op jit(solution)/shard_map/ppermute | solution.py:20
  59.0 8.1 %copy-start.4 = (f32[3,1,15,32,128]{4,3,2,1,0:T(8,128)S(1)}, f32[3,1,15,32,128]{4,3,2,1,0:T(8,128)}, u32[]{:S(2)}) copy-start(f32[3,1,15,32,128]{4,3,2,1,0:T(8,128)} %get-tuple-element.50) | copy-start | bytes 2211844
  59.0 8.1 %copy-start.5 = (f32[3,1,15,32,128]{4,3,2,1,0:T(8,128)S(1)}, f32[3,1,15,32,128]{4,3,2,1,0:T(8,128)}, u32[]{:S(2)}) copy-start(f32[3,1,15,32,128]{4,3,2,1,0:T(8,128)} %get-tuple-element.51) | copy-start | bytes 2211844
  63.5 3.6 %collective-permute-start.15 = (f32[3,1,16,32,128]{4,3,2,1,0:T(8,128)S(1)}, f32[3,1,16,32,128]{4,3,2,1,0:T(8,128)}, u32[]{:S(2)}, u32[]{:S(2)}) collective-permute-start(f32[3,1,16,32,128]{4,3,2,1,0:T(8,128)S(1)} %get-tuple-element.11), channel_id=1, source_target_pairs={{0,4},{4,0},{8,12},{12,8},{16,20},{20,16},{24,28},{28,24},{1,5},{5... | collective-permute-start | bytes 2359304 | tf_op jit(solution)/shard_map/ppermute | solution.py:32
  67.1 19.1 %collective-permute-start.16 = (f32[3,1,16,32,128]{4,3,2,1,0:T(8,128)}, f32[3,1,16,32,128]{4,3,2,1,0:T(8,128)}, u32[]{:S(2)}, u32[]{:S(2)}) collective-permute-start(f32[3,1,16,32,128]{4,3,2,1,0:T(8,128)} %collective-permute-done.15), channel_id=1, source_target_pairs={{0,8},{4,12},{8,0},{12,4},{16,24},{20,28},{24,16},{28,20},{1,9},{5... | collective-permute-start | bytes 2359304 | tf_op jit(solution)/shard_map/ppermute | solution.py:32
  68.0 53.2 %collective-permute-start.10 = (f32[3,1,16,32,128]{4,3,2,1,0:T(8,128)S(1)}, f32[3,1,16,32,128]{4,3,2,1,0:T(8,128)}, u32[]{:S(2)}, u32[]{:S(2)}) collective-permute-start(f32[3,1,16,32,128]{4,3,2,1,0:T(8,128)S(1)} %get-tuple-element.11), channel_id=1, source_target_pairs={{0,16},{16,0},{1,17},{17,1},{2,18},{18,2},{3,19},{19,3},{4,20},{20... | collective-permute-start | bytes 2359304 | tf_op jit(solution)/shard_map/ppermute | solution.py:20
  69.4 51.8 %collective-permute-start.9 = (f32[3,1,16,32,128]{4,3,2,1,0:T(8,128)S(1)}, f32[3,1,16,32,128]{4,3,2,1,0:T(8,128)}, u32[]{:S(2)}, u32[]{:S(2)}) collective-permute-start(f32[3,1,16,32,128]{4,3,2,1,0:T(8,128)S(1)} %get-tuple-element.11), channel_id=1, source_target_pairs={{16,0},{0,16},{17,1},{1,17},{18,2},{2,18},{19,3},{3,19},{20,4},{4,... | collective-permute-start | bytes 2359304 | tf_op jit(solution)/shard_map/ppermute | solution.py:22
  69.8 17.6 %copy-start.10 = (f32[32]{0:T(128)S(1)}, f32[32]{0:T(128)}, u32[]{:S(2)}) copy-start(f32[32]{0:T(128)} %param.5) | copy-start | bytes 388
  70.5 19.1 %collective-permute-start.14 = (f32[3,1,16,32,1]{3,2,4,1,0:T(8,128)S(1)}, f32[3,1,16,32,1]{3,2,4,1,0:T(8,128)S(1)}, u32[]{:S(2)}, u32[]{:S(2)}) collective-permute-start(f32[3,1,16,32,1]{3,2,4,1,0:T(8,128)S(1)} %copy.92), channel_id=1, source_target_pairs={{0,1},{1,2},{2,3},{3,0},{4,5},{5,6},{6,7},{7,4},{8,9},{9,10},{10,1... | collective-permute-start | bytes 18440 | tf_op jit(solution)/shard_map/ppermute | solution.py:20
  72.0 21.1 %collective-permute-start.13 = (f32[3,1,16,32,1]{3,2,4,1,0:T(8,128)S(1)}, f32[3,1,16,32,1]{3,2,4,1,0:T(8,128)S(1)}, u32[]{:S(2)}, u32[]{:S(2)}) collective-permute-start(f32[3,1,16,32,1]{3,2,4,1,0:T(8,128)S(1)} %copy.90), channel_id=1, source_target_pairs={{1,0},{2,1},{3,2},{0,3},{5,4},{6,5},{7,6},{4,7},{9,8},{10,9},{11,1... | collective-permute-start | bytes 18440 | tf_op jit(solution)/shard_map/ppermute | solution.py:22
  86.2 33.9 %collective-permute-start.17 = (f32[3,1,16,32,128]{4,3,2,1,0:T(8,128)}, f32[3,1,16,32,128]{4,3,2,1,0:T(8,128)S(1)}, u32[]{:S(2)}, u32[]{:S(2)}) collective-permute-start(f32[3,1,16,32,128]{4,3,2,1,0:T(8,128)} %collective-permute-done.16), channel_id=1, source_target_pairs={{0,16},{4,20},{8,24},{12,28},{16,0},{20,4},{24,8},{28,12},{1,17},{... | collective-permute-start | bytes 2359304 | tf_op jit(solution)/shard_map/ppermute | solution.py:32
  89.6 3.6 %copy-start.6 = (f32[3,1,16,32,1]{3,2,4,1,0:T(8,128)}, f32[3,1,16,32,1]{3,2,4,1,0:T(8,128)S(1)}, u32[]{:S(2)}) copy-start(f32[3,1,16,32,1]{3,2,4,1,0:T(8,128)S(1)} %collective-permute-done.14) | copy-start | bytes 18436
  89.6 31.6 %collective-permute-start.12 = (f32[6,1,16,1,128]{4,2,3,1,0:T(8,128)}, f32[6,1,16,1,128]{4,2,3,1,0:T(8,128)S(1)}, u32[]{:S(2)}, u32[]{:S(2)}) collective-permute-start(f32[6,1,16,1,128]{4,2,3,1,0:T(8,128)} %bitcast.37), channel_id=1, source_target_pairs={{0,4},{4,8},{8,12},{1,5},{5,9},{9,13},{2,6},{6,10},{10,14},{3,7},{... | collective-permute-start | bytes 147464 | tf_op jit(solution)/shard_map/ppermute | solution.py:20
  93.1 0.6 copy-start.8
  93.8 27.4 %collective-permute-start.11 = (f32[6,1,16,1,128]{4,2,3,1,0:T(8,128)}, f32[6,1,16,1,128]{4,2,3,1,0:T(8,128)}, u32[]{:S(2)}, u32[]{:S(2)}) collective-permute-start(f32[6,1,16,1,128]{4,2,3,1,0:T(8,128)} %bitcast.36), channel_id=1, source_target_pairs={{4,0},{8,4},{12,8},{5,1},{9,5},{13,9},{6,2},{10,6},{14,10},{7,3},{... | collective-permute-start | bytes 147464 | tf_op jit(solution)/shard_map/ppermute | solution.py:22
  125.6 3.5 %collective-permute-start.24 = (f32[3,1,16,32,128]{4,3,2,1,0:T(8,128)S(1)}, f32[3,1,16,32,128]{4,3,2,1,0:T(8,128)S(1)}, u32[]{:S(2)}, u32[]{:S(2)}) collective-permute-start(f32[3,1,16,32,128]{4,3,2,1,0:T(8,128)S(1)} %fusion.28), channel_id=1, source_target_pairs={{0,4},{4,0},{8,12},{12,8},{16,20},{20,16},{24,28},{28,24},{1,5},{5... | collective-permute-start | bytes 2359304 | tf_op jit(solution)/shard_map/ppermute | solution.py:32
  129.0 18.9 %collective-permute-start.25 = (f32[3,1,16,32,128]{4,3,2,1,0:T(8,128)S(1)}, f32[3,1,16,32,128]{4,3,2,1,0:T(8,128)}, u32[]{:S(2)}, u32[]{:S(2)}) collective-permute-start(f32[3,1,16,32,128]{4,3,2,1,0:T(8,128)S(1)} %collective-permute-done.24), channel_id=1, source_target_pairs={{0,8},{4,12},{8,0},{12,4},{16,24},{20,28},{24,16},{28,20},{1,9},{5... | collective-permute-start | bytes 2359304 | tf_op jit(solution)/shard_map/ppermute | solution.py:32
  130.5 54.2 %collective-permute-start.19 = (f32[3,1,16,32,128]{4,3,2,1,0:T(8,128)S(1)}, f32[3,1,16,32,128]{4,3,2,1,0:T(8,128)}, u32[]{:S(2)}, u32[]{:S(2)}) collective-permute-start(f32[3,1,16,32,128]{4,3,2,1,0:T(8,128)S(1)} %fusion.28), channel_id=1, source_target_pairs={{0,16},{16,0},{1,17},{17,1},{2,18},{18,2},{3,19},{19,3},{4,20},{20... | collective-permute-start | bytes 2359304 | tf_op jit(solution)/shard_map/ppermute | solution.py:20
  131.7 53.0 %collective-permute-start.18 = (f32[3,1,16,32,128]{4,3,2,1,0:T(8,128)S(1)}, f32[3,1,16,32,128]{4,3,2,1,0:T(8,128)}, u32[]{:S(2)}, u32[]{:S(2)}) collective-permute-start(f32[3,1,16,32,128]{4,3,2,1,0:T(8,128)S(1)} %fusion.28), channel_id=1, source_target_pairs={{16,0},{0,16},{17,1},{1,17},{18,2},{2,18},{19,3},{3,19},{20,4},{4,... | collective-permute-start | bytes 2359304 | tf_op jit(solution)/shard_map/ppermute | solution.py:22
  147.9 34.8 %collective-permute-start.26 = (f32[3,1,16,32,128]{4,3,2,1,0:T(8,128)}, f32[3,1,16,32,128]{4,3,2,1,0:T(8,128)}, u32[]{:S(2)}, u32[]{:S(2)}) collective-permute-start(f32[3,1,16,32,128]{4,3,2,1,0:T(8,128)} %collective-permute-done.25), channel_id=1, source_target_pairs={{0,16},{4,20},{8,24},{12,28},{16,0},{20,4},{24,8},{28,12},{1,17},{... | collective-permute-start | bytes 2359304 | tf_op jit(solution)/shard_map/ppermute | solution.py:32
  151.4 4.6 %collective-permute-start.23 = (f32[3,1,16,32,1]{3,2,4,1,0:T(8,128)S(1)}, f32[3,1,16,32,1]{3,2,4,1,0:T(8,128)S(1)}, u32[]{:S(2)}, u32[]{:S(2)}) collective-permute-start(f32[3,1,16,32,1]{3,2,4,1,0:T(8,128)S(1)} %copy.100), channel_id=1, source_target_pairs={{0,1},{1,2},{2,3},{3,0},{4,5},{5,6},{6,7},{7,4},{8,9},{9,10},{10,1... | collective-permute-start | bytes 18440 | tf_op jit(solution)/shard_map/ppermute | solution.py:20
  152.7 7.8 %collective-permute-start.22 = (f32[3,1,16,32,1]{3,2,4,1,0:T(8,128)S(1)}, f32[3,1,16,32,1]{3,2,4,1,0:T(8,128)S(1)}, u32[]{:S(2)}, u32[]{:S(2)}) collective-permute-start(f32[3,1,16,32,1]{3,2,4,1,0:T(8,128)S(1)} %copy.98), channel_id=1, source_target_pairs={{1,0},{2,1},{3,2},{0,3},{5,4},{6,5},{7,6},{4,7},{9,8},{10,9},{11,1... | collective-permute-start | bytes 18440 | tf_op jit(solution)/shard_map/ppermute | solution.py:22
  155.9 8.3 %collective-permute-start.20 = (f32[3,1,16,1,128]{4,2,3,1,0:T(8,128)S(1)}, f32[3,1,16,1,128]{4,2,3,1,0:T(8,128)S(1)}, u32[]{:S(2)}, u32[]{:S(2)}) collective-permute-start(f32[3,1,16,1,128]{4,2,3,1,0:T(8,128)S(1)} %bitcast.77), channel_id=1, source_target_pairs={{4,0},{8,4},{12,8},{5,1},{9,5},{13,9},{6,2},{10,6},{14,10},{7,3},{... | collective-permute-start | bytes 73736 | tf_op jit(solution)/shard_map/ppermute | solution.py:22
  160.5 3.9 %collective-permute-start.21 = (f32[3,1,16,1,128]{4,2,3,1,0:T(8,128)S(1)}, f32[3,1,16,1,128]{4,2,3,1,0:T(8,128)S(1)}, u32[]{:S(2)}, u32[]{:S(2)}) collective-permute-start(f32[3,1,16,1,128]{4,2,3,1,0:T(8,128)S(1)} %bitcast.75), channel_id=1, source_target_pairs={{0,4},{4,8},{8,12},{1,5},{5,9},{9,13},{2,6},{6,10},{10,14},{3,7},{... | collective-permute-start | bytes 73736 | tf_op jit(solution)/shard_map/ppermute | solution.py:20
  184.7 8.1 %copy-start.3 = (f32[3,1,15,32,128]{4,3,2,1,0:T(8,128)S(1)}, f32[3,1,15,32,128]{4,3,2,1,0:T(8,128)}, u32[]{:S(2)}) copy-start(f32[3,1,15,32,128]{4,3,2,1,0:T(8,128)} %get-tuple-element.29) | copy-start | bytes 2211844
  189.2 59.3 %copy-start.1 = (f32[3,1,16,32,128]{4,3,2,1,0:T(8,128)}, f32[3,1,16,32,128]{4,3,2,1,0:T(8,128)S(1)}, u32[]{:S(2)}) copy-start(f32[3,1,16,32,128]{4,3,2,1,0:T(8,128)S(1)} %get-tuple-element.10) | copy-start | bytes 2359300
  189.2 4.3 %copy-start.2 = (f32[3,1,15,32,128]{4,3,2,1,0:T(8,128)S(1)}, f32[3,1,15,32,128]{4,3,2,1,0:T(8,128)}, u32[]{:S(2)}) copy-start(f32[3,1,15,32,128]{4,3,2,1,0:T(8,128)} %get-tuple-element.30) | copy-start | bytes 2211844
  189.2 3.6 %collective-permute-start.33 = (f32[3,1,16,32,128]{4,3,2,1,0:T(8,128)S(1)}, f32[3,1,16,32,128]{4,3,2,1,0:T(8,128)}, u32[]{:S(2)}, u32[]{:S(2)}) collective-permute-start(f32[3,1,16,32,128]{4,3,2,1,0:T(8,128)S(1)} %get-tuple-element.10), channel_id=1, source_target_pairs={{0,4},{4,0},{8,12},{12,8},{16,20},{20,16},{24,28},{28,24},{1,5},{5... | collective-permute-start | bytes 2359304 | tf_op jit(solution)/shard_map/ppermute | solution.py:32
  192.7 19.1 %collective-permute-start.34 = (f32[3,1,16,32,128]{4,3,2,1,0:T(8,128)}, f32[3,1,16,32,128]{4,3,2,1,0:T(8,128)}, u32[]{:S(2)}, u32[]{:S(2)}) collective-permute-start(f32[3,1,16,32,128]{4,3,2,1,0:T(8,128)} %collective-permute-done.33), channel_id=1, source_target_pairs={{0,8},{4,12},{8,0},{12,4},{16,24},{20,28},{24,16},{28,20},{1,9},{5... | collective-permute-start | bytes 2359304 | tf_op jit(solution)/shard_map/ppermute | solution.py:32
  194.2 54.2 %collective-permute-start.28 = (f32[3,1,16,32,128]{4,3,2,1,0:T(8,128)S(1)}, f32[3,1,16,32,128]{4,3,2,1,0:T(8,128)}, u32[]{:S(2)}, u32[]{:S(2)}) collective-permute-start(f32[3,1,16,32,128]{4,3,2,1,0:T(8,128)S(1)} %get-tuple-element.10), channel_id=1, source_target_pairs={{0,16},{16,0},{1,17},{17,1},{2,18},{18,2},{3,19},{19,3},{4,20},{20... | collective-permute-start | bytes 2359304 | tf_op jit(solution)/shard_map/ppermute | solution.py:20
  195.7 52.7 %collective-permute-start.27 = (f32[3,1,16,32,128]{4,3,2,1,0:T(8,128)S(1)}, f32[3,1,16,32,128]{4,3,2,1,0:T(8,128)}, u32[]{:S(2)}, u32[]{:S(2)}) collective-permute-start(f32[3,1,16,32,128]{4,3,2,1,0:T(8,128)S(1)} %get-tuple-element.10), channel_id=1, source_target_pairs={{16,0},{0,16},{17,1},{1,17},{18,2},{2,18},{19,3},{3,19},{20,4},{4,... | collective-permute-start | bytes 2359304 | tf_op jit(solution)/shard_map/ppermute | solution.py:22
  196.0 17.0 %copy-start.11 = (f32[32]{0:T(128)S(1)}, f32[32]{0:T(128)}, u32[]{:S(2)}) copy-start(f32[32]{0:T(128)} %param.5) | copy-start | bytes 388
  196.7 18.6 %collective-permute-start.32 = (f32[3,1,16,32,1]{3,2,4,1,0:T(8,128)S(1)}, f32[3,1,16,32,1]{3,2,4,1,0:T(8,128)S(1)}, u32[]{:S(2)}, u32[]{:S(2)}) collective-permute-start(f32[3,1,16,32,1]{3,2,4,1,0:T(8,128)S(1)} %copy.108), channel_id=1, source_target_pairs={{0,1},{1,2},{2,3},{3,0},{4,5},{5,6},{6,7},{7,4},{8,9},{9,10},{10,1... | collective-permute-start | bytes 18440 | tf_op jit(solution)/shard_map/ppermute | solution.py:20
  198.2 20.6 %collective-permute-start.31 = (f32[3,1,16,32,1]{3,2,4,1,0:T(8,128)S(1)}, f32[3,1,16,32,1]{3,2,4,1,0:T(8,128)S(1)}, u32[]{:S(2)}, u32[]{:S(2)}) collective-permute-start(f32[3,1,16,32,1]{3,2,4,1,0:T(8,128)S(1)} %copy.106), channel_id=1, source_target_pairs={{1,0},{2,1},{3,2},{0,3},{5,4},{6,5},{7,6},{4,7},{9,8},{10,9},{11,1... | collective-permute-start | bytes 18440 | tf_op jit(solution)/shard_map/ppermute | solution.py:22
  211.8 34.7 %collective-permute-start.35 = (f32[3,1,16,32,128]{4,3,2,1,0:T(8,128)}, f32[3,1,16,32,128]{4,3,2,1,0:T(8,128)}, u32[]{:S(2)}, u32[]{:S(2)}) collective-permute-start(f32[3,1,16,32,128]{4,3,2,1,0:T(8,128)} %collective-permute-done.34), channel_id=1, source_target_pairs={{0,16},{4,20},{8,24},{12,28},{16,0},{20,4},{24,8},{28,12},{1,17},{... | collective-permute-start | bytes 2359304 | tf_op jit(solution)/shard_map/ppermute | solution.py:32
  215.3 6.1 %copy-start.7 = (f32[3,1,16,32,1]{3,2,4,1,0:T(8,128)}, f32[3,1,16,32,1]{3,2,4,1,0:T(8,128)S(1)}, u32[]{:S(2)}) copy-start(f32[3,1,16,32,1]{3,2,4,1,0:T(8,128)S(1)} %collective-permute-done.32) | copy-start | bytes 18436
  215.3 33.1 %collective-permute-start.30 = (f32[6,1,16,1,128]{4,2,3,1,0:T(8,128)}, f32[6,1,16,1,128]{4,2,3,1,0:T(8,128)S(1)}, u32[]{:S(2)}, u32[]{:S(2)}) collective-permute-start(f32[6,1,16,1,128]{4,2,3,1,0:T(8,128)} %bitcast.39), channel_id=1, source_target_pairs={{0,4},{4,8},{8,12},{1,5},{5,9},{9,13},{2,6},{6,10},{10,14},{3,7},{... | collective-permute-start | bytes 147464 | tf_op jit(solution)/shard_map/ppermute | solution.py:20
  218.8 0.6 copy-start.9
  219.4 29.0 %collective-permute-start.29 = (f32[6,1,16,1,128]{4,2,3,1,0:T(8,128)}, f32[6,1,16,1,128]{4,2,3,1,0:T(8,128)}, u32[]{:S(2)}, u32[]{:S(2)}) collective-permute-start(f32[6,1,16,1,128]{4,2,3,1,0:T(8,128)} %bitcast.38), channel_id=1, source_target_pairs={{4,0},{8,4},{12,8},{5,1},{9,5},{13,9},{6,2},{10,6},{14,10},{7,3},{... | collective-permute-start | bytes 147464 | tf_op jit(solution)/shard_map/ppermute | solution.py:22
where the time goes:
time: 255 us; the launch traced here: 253 us
  waiting for transfers between devices  142 us (56%)
  starting transfers between devices  58.5 us (23%)
  local copies, waits for them, and re-layouts  26.6 us (10%)
  other arithmetic  25.5 us (10%)
    ppermute x12, waiting for transfers between devices, partner_2(): return lax.ppermute(value, axis, pairs)  140 us
    ppermute x12, starting transfers between devices, with_halo(): lax.ppermute(tail, axis, [(i, (i + 1) % count) for i in range(ends)])  24.2 us
    ppermute x12, starting transfers between devices, with_halo(): lax.ppermute(head, axis, [((i + 1) % count, i) for i in range(ends)])  20.6 us
    ppermute x12, starting transfers between devices, partner_2(): return lax.ppermute(value, axis, pairs)  13.7 us
    sub x2, other arithmetic, local(): present_state - step_rate * (local_part + 0.5 * (residual_now - mirror_re...  9.18 us
    reduce_sum x2, other arithmetic, descent_part(): jnp.sum(residual_now * slopes[component], axis=0)  8.98 us
    rev x4, local copies, waits for them, and re-layouts, reflect(): partner = partner[:, :, :, ::-1, :]  6.07 us
    slice x8, local copies, waits for them, and re-layouts, along_flow(): return (jnp.roll(values, -1, 2), jnp.roll(values, 1, 2))  5.32 us
  transfers between devices with their start and end apart: 36, of which 14 were waited for; matrix products, arithmetic and copies ran while one was open for 13% of the time, Pallas kernels for 0%

commit v1 on v0

--- a/solution.py
+++ b/solution.py
@@ -1,12 +1,26 @@
+import functools
+
 import jax
 import jax.numpy as jnp
 from jax import lax
+from jax.experimental import pallas as pl
+from jax.experimental.pallas import tpu as pltpu
 from jax.sharding import PartitionSpec as P
 
 ITERS = 2
 
 
 step_rate = 0.05
+LANES = 128
+SUBLANES = 8
+SIGNS = (1.0, -1.0, 1.0)
+
+
+def instant_weights(instants):
+    weights = {}
+    for offset, weight in ((1, 0.5), (-1, -0.5)):
+        weights[offset % instants] = weights.get(offset % instants, 0.0) + weight
+    return {offset: weight for offset, weight in weights.items() if weight != 0.0}
 
 
 def with_halo(cells, sides, width, closed):
@@ -26,15 +40,12 @@
     return cells
 
 
-def partner_2(value, axis, bit):
-    mask = 2**bit
-    pairs = [(source, source ^ mask) for source in range(lax.axis_size(axis))]
-    return lax.ppermute(value, axis, pairs)
-
-
-def time_pair(values):
+def time_slope(values):
+    instants = values.shape[1] * lax.axis_size("tm")
+    if not instant_weights(instants):
+        return jnp.zeros_like(values)
     padded_state = with_halo(values, (("tm", 1),), 1, True)
-    return (padded_state[:, 2:], padded_state[:, :-2])
+    return 0.5 * (padded_state[:, 2:] - padded_state[:, :-2])
 
 
 def wall_pair(values):
@@ -51,21 +62,22 @@
     return (jnp.roll(values, -1, 2), jnp.roll(values, 1, 2))
 
 
+def partner_pairs():
+    times, walls = lax.axis_size("tm"), lax.axis_size("wall")
+    return [
+        (time * walls + wall, ((time + times // 2) % times) * walls + walls - 1 - wall)
+        for time in range(times)
+        for wall in range(walls)
+    ]
+
+
 def reflect(values):
-    stack_size = values.shape[0]
-    sign_row = jnp.where(jnp.arange(stack_size) % 3 == 1, -1.0, 1.0).astype(jnp.float32)
-    sign_row = sign_row.reshape(stack_size, 1, 1, 1, 1)
-    wall_bits = lax.axis_size("wall").bit_length() - 1
-    time_bits = lax.axis_size("tm").bit_length() - 1
-    partner = values
-    for bit_index in list(range(wall_bits)) + [wall_bits + time_bits - 1]:
-        partner = partner_2(partner, ("tm", "wall"), bit_index)
-    partner = partner[:, :, :, ::-1, :]
-    return partner * sign_row
+    sign_row = jnp.array(SIGNS, jnp.float32).reshape(3, 1, 1, 1, 1)
+    partner = lax.ppermute(values, ("tm", "wall"), partner_pairs())
+    return partner[:, :, :, ::-1, :] * sign_row
 
 
 def residual_of(present_state, mirrored, driving_source, viscous):
-    ahead_time, behind_time = time_pair(present_state)
     neighbours = (along_flow(present_state), wall_pair(present_state), span_pair(present_state))
     slopes = [0.5 * (ahead - behind) for ahead, behind in neighbours]
     advect = (
@@ -77,7 +89,7 @@
     laplace = laplace + (neighbours[1][0] + neighbours[1][1] - 2.0 * present_state)
     laplace = laplace + (neighbours[2][0] + neighbours[2][1] - 2.0 * present_state)
     residual_now = (
-        0.5 * (ahead_time - behind_time)
+        time_slope(present_state)
         + advect
         - viscous * laplace
         + 0.5 * (present_state - mirrored)
@@ -87,7 +99,6 @@
 
 
 def descent_part(neighbours, slopes, residual_now, viscous):
-    ahead_time, behind_time = time_pair(residual_now)
     scaled = viscous * residual_now
     wall_ahead, wall_behind = wall_pair(jnp.concatenate((residual_now, scaled), 0))
     flow_ahead, flow_behind = along_flow(residual_now)
@@ -109,14 +120,13 @@
     diffused = viscous * flow_ahead + viscous * flow_behind - 2.0 * scaled
     diffused = diffused + (wall_ahead[3:] + wall_behind[3:] - 2.0 * scaled)
     diffused = diffused + (viscous * span_ahead + viscous * span_behind - 2.0 * scaled)
-    return -0.5 * (ahead_time - behind_time) + transport - second - diffused
-
-
-def local(starting_speed_vector, driving_source, viscosity):
+    return -time_slope(residual_now) + transport - second - diffused
+
+
+def staged(starting_speed_vector, driving_source, viscosity):
     viscous = viscosity[None, None, None, :, None]
     present_state = starting_speed_vector
     residual_now = starting_speed_vector
-    mirrored = starting_speed_vector
     for iteration in range(ITERS):
         mirrored = reflect(present_state)
         residual_now, neighbours, slopes = residual_of(
@@ -130,6 +140,296 @@
     return (present_state, residual_now)
 
 
+def to_tiles(rows_ref, first, planes, tile, depth):
+    block = rows_ref[pl.ds(first, planes), pl.ds(tile, SUBLANES, stride=depth), :]
+    return block.reshape(planes * SUBLANES, block.shape[-1]).T
+
+
+def extend_rows(target, source, before, after, offset, count, halo):
+    rows = source.shape[1]
+
+    def place(plane, carry):
+        target[plane, 0:halo] = before[offset + plane]
+        target[plane, halo : halo + rows] = source[plane]
+        target[plane, halo + rows : rows + 2 * halo] = after[offset + plane]
+        return carry
+
+    lax.fori_loop(0, count, place, 0)
+
+
+def prepare(planes, halo, speed, force, thickness, before, after, speed_tiles, force_tiles, thick_tiles, first, last, rows):
+    count = speed.shape[0]
+    cells = speed.shape[-1]
+    depth = rows.shape[1] // SUBLANES
+    for part, (source, target) in enumerate(((speed, speed_tiles), (force, force_tiles))):
+        extend_rows(rows, source, before, after, part * count, count, halo)
+        for component in range(3):
+            for tile in range(depth):
+                place = component * depth + tile
+                block = to_tiles(rows, component * planes, planes, tile, depth)
+                target[place] = block
+                first[part * 3 * depth + place] = block[:halo]
+                last[part * 3 * depth + place] = block[cells - halo :]
+    extend_rows(rows, thickness, before, after, 2 * count, 1, halo)
+    for tile in range(depth):
+        block = rows[0, pl.ds(tile, SUBLANES, stride=depth), :]
+        block = jnp.concatenate([block] * planes, axis=0).T
+        thick_tiles[tile] = block[:SUBLANES]
+
+
+def turn(block):
+    lanes = lax.broadcasted_iota(jnp.int32, block.shape, 1)
+    return jnp.take_along_axis(block, lanes ^ (SUBLANES - 1), axis=1)
+
+
+def wrap(field, cells):
+    ring = field.shape[1] - 2 * SUBLANES
+    field[:, SUBLANES - 1 : SUBLANES] = field[:, SUBLANES + ring - 1 : SUBLANES + ring]
+    field[:, SUBLANES + ring : SUBLANES + ring + 1] = field[:, SUBLANES : SUBLANES + 1]
+
+
+def row_ahead(tiles, tile):
+    return tiles[tile + 1] if tile + 1 < len(tiles) else pltpu.roll(tiles[0], LANES - 1, 1)
+
+
+def row_behind(tiles, tile):
+    return tiles[tile - 1] if tile > 0 else pltpu.roll(tiles[-1], 1, 1)
+
+
+def plane_ahead(tile):
+    return pltpu.roll(tile, LANES - SUBLANES, 1)
+
+
+def plane_behind(tile):
+    return pltpu.roll(tile, SUBLANES, 1)
+
+
+def load(field, component, depth, start):
+    return [field[component * depth + tile, pl.ds(start, SUBLANES), :] for tile in range(depth)]
+
+
+def residual_stage(speed, mirrored, force, thick, inside, residual, slopes, depth, steps):
+    def step(index, carry):
+        start = pl.multiple_of(SUBLANES + index * SUBLANES, SUBLANES)
+        tiles = [load(speed, component, depth, start) for component in range(3)]
+        for tile in range(depth):
+            thin = thick[tile]
+            half = [0.5 * tiles[component][tile] for component in range(3)]
+            for component in range(3):
+                place = component * depth + tile
+                here = tiles[component][tile]
+                pairs = (
+                    (plane_ahead(here), plane_behind(here)),
+                    (row_ahead(tiles[component], tile), row_behind(tiles[component], tile)),
+                    (
+                        speed[place, pl.ds(start + 1, SUBLANES), :],
+                        speed[place, pl.ds(start - 1, SUBLANES), :],
+                    ),
+                )
+                around = None
+                total = None
+                for axis_id, (ahead, behind) in enumerate(pairs):
+                    slope = ahead - behind
+                    if slopes is not None:
+                        slopes[axis_id * 3 * depth + place, pl.ds(start, SUBLANES), :] = slope
+                    both = ahead + behind
+                    around = both if around is None else around + both
+                    term = half[axis_id] * slope
+                    total = term if total is None else total + term
+                laplace = around - 6.0 * here
+                other = mirrored[place, pl.ds(start, SUBLANES), :]
+                total = total - thin * laplace + 0.5 * (here - other)
+                total = total - force[place, pl.ds(start, SUBLANES), :]
+                residual[place, pl.ds(start, SUBLANES), :] = total * inside[tile]
+        return carry
+
+    lax.fori_loop(0, steps, step, 0)
+
+
+def descent_stage(speed, residual, mirrored, thick, inside, slopes, following, depth, steps):
+    def step(index, carry):
+        start = pl.multiple_of(SUBLANES + index * SUBLANES, SUBLANES)
+        speeds = [load(speed, component, depth, start) for component in range(3)]
+        tiles = [load(residual, component, depth, start) for component in range(3)]
+        rises = []
+        falls = []
+        for tile in range(depth):
+            half = 0.5 * speeds[1][tile]
+            rises.append(half + thick[tile])
+            falls.append(half - thick[tile])
+        upper = [[rises[tile] * tiles[c][tile] for tile in range(depth)] for c in range(3)]
+        lower = [[falls[tile] * tiles[c][tile] for tile in range(depth)] for c in range(3)]
+        for tile in range(depth):
+            thin = thick[tile]
+            flow = 0.5 * speeds[0][tile]
+            flow_rise, flow_fall = flow + thin, flow - thin
+            span_rise = 0.5 * speed[2 * depth + tile, pl.ds(start + 1, SUBLANES), :] + thin
+            span_fall = 0.5 * speed[2 * depth + tile, pl.ds(start - 1, SUBLANES), :] - thin
+            half = [0.5 * tiles[component][tile] for component in range(3)]
+            middle = 6.0 * thin
+            rate = step_rate * inside[tile]
+            for component in range(3):
+                place = component * depth + tile
+                here = tiles[component][tile]
+                total = None
+                for inner in range(3):
+                    slope = slopes[
+                        (component * 3 + inner) * depth + tile, pl.ds(start, SUBLANES), :
+                    ]
+                    term = half[inner] * slope
+                    total = term if total is None else total + term
+                total = total - plane_ahead(flow_rise * here) + plane_behind(flow_fall * here)
+                total = total - row_ahead(upper[component], tile) + row_behind(lower[component], tile)
+                total = total - span_rise * residual[place, pl.ds(start + 1, SUBLANES), :]
+                total = total + span_fall * residual[place, pl.ds(start - 1, SUBLANES), :]
+                total = total + middle * here
+                other = mirrored[place, pl.ds(start, SUBLANES), :]
+                total = total + 0.5 * (here - other)
+                following[place, pl.ds(start, SUBLANES), :] = speeds[component][tile] - rate * total
+        return carry
+
+    lax.fori_loop(0, steps, step, 0)
+
+
+def iterate(planes, halo, wall, speed_tiles, force_tiles, thick_tiles, ahead_cells, behind_cells,
+            partner_speed, partner_force, partner_thick, partner_before, partner_after, partner_ahead, partner_behind,
+            speed_out, residual_out,
+            rows, own, own_force, own_residual, own_slopes, own_next,
+            far, far_force, far_residual, far_slopes, far_next, own_thick, far_thick, inside):
+    count, width, cells = partner_speed.shape
+    depth = rows.shape[1] // SUBLANES
+    blocks = 3 * depth
+    ring = own.shape[1] - 2 * SUBLANES
+    body = pl.ds(SUBLANES, cells)
+    ahead = pl.ds(SUBLANES + cells, halo)
+    behind = pl.ds(SUBLANES + cells + halo, halo)
+
+    for part, (field, source) in enumerate(((own, speed_tiles), (own_force, force_tiles))):
+        field[:, body] = source[...]
+        field[:, ahead] = ahead_cells[pl.ds(part * blocks, blocks)]
+        field[:, behind] = behind_cells[pl.ds(part * blocks, blocks)]
+        wrap(field, cells)
+    for part, (field, source) in enumerate(((far, partner_speed), (far_force, partner_force))):
+        extend_rows(rows, source, partner_before, partner_after, part * count, count, halo)
+        for component in range(3):
+            for tile in range(depth):
+                place = component * depth + depth - 1 - tile
+                block = to_tiles(rows, component * planes, planes, tile, depth)
+                field[place, body] = SIGNS[component] * turn(block)
+                got = part * blocks + component * depth + tile
+                field[place, ahead] = SIGNS[component] * turn(partner_ahead[got])
+                field[place, behind] = SIGNS[component] * turn(partner_behind[got])
+        wrap(field, cells)
+    lane = lax.broadcasted_iota(jnp.int32, (SUBLANES, LANES), 1) % SUBLANES
+    for tile in range(depth):
+        own_thick[tile] = thick_tiles[tile]
+        far_thick[tile] = turn(partner_thick[depth - 1 - tile])
+        row = wall[0] * width - halo + tile + depth * lane
+        inside[tile] = jnp.where((row >= 0) & (row < wall[1] * width), 1.0, 0.0).astype(jnp.float32)
+
+    steps = ring // SUBLANES
+    for iteration in range(ITERS):
+        final = iteration + 1 == ITERS
+        residual_stage(own, far, own_force, own_thick, inside, own_residual, own_slopes, depth, steps)
+        wrap(own_residual, cells)
+        residual_stage(far, own, far_force, far_thick, inside, far_residual, None if final else far_slopes, depth, steps)
+        descent_stage(own, own_residual, far_residual, own_thick, inside, own_slopes, own_next, depth,
+                      cells // SUBLANES if final else steps)
+        if not final:
+            wrap(far_residual, cells)
+            wrap(own_next, cells)
+            descent_stage(far, far_residual, own_residual, far_thick, inside, far_slopes, far_next, depth, steps)
+            wrap(far_next, cells)
+            own, own_next = own_next, own
+            far, far_next = far_next, far
+
+    for field, target in ((own_next, speed_out), (own_residual, residual_out)):
+        for component in range(3):
+            for tile in range(depth):
+                block = field[component * depth + tile, body].T
+                block = block.reshape(planes, SUBLANES, cells)
+                rows[pl.ds(component * planes, planes), pl.ds(tile, SUBLANES, stride=depth), :] = block
+        target[...] = rows[:, halo : halo + width]
+
+
+def carried(starting_speed_vector, driving_source, viscosity):
+    shape = starting_speed_vector.shape
+    _, _, planes, width, cells = shape
+    halo = 2 * ITERS
+    depth = (width + 2 * halo) // SUBLANES
+    blocks = 3 * depth
+    count = 3 * planes
+    whole = pl.BlockSpec(memory_space=pltpu.VMEM)
+    arrays = lambda *sizes: jax.ShapeDtypeStruct(sizes, jnp.float32)
+    speed = starting_speed_vector.reshape(count, width, cells)
+    force = driving_source.reshape(count, width, cells)
+    thickness = jnp.broadcast_to(viscosity[None, :, None], (1, width, cells))
+
+    to_partner = functools.partial(lax.ppermute, axis_name=("tm", "wall"), perm=partner_pairs())
+    walls, spans = lax.axis_size("wall"), lax.axis_size("span")
+    upward = [(i, i + 1) for i in range(walls - 1)]
+    downward = [(i + 1, i) for i in range(walls - 1)]
+    onward = [(i, (i + 1) % spans) for i in range(spans)]
+    backward = [((i + 1) % spans, i) for i in range(spans)]
+
+    partner_speed = to_partner(speed)
+    partner_force = to_partner(force)
+    stack = lambda part: jnp.concatenate([part(speed), part(force), part(thickness)])
+    before = lax.ppermute(stack(lambda a: a[:, width - halo :]), "wall", upward)
+    after = lax.ppermute(stack(lambda a: a[:, :halo]), "wall", downward)
+    speed_tiles, force_tiles, thick_tiles, first, last = pl.pallas_call(
+        functools.partial(prepare, planes, halo),
+        out_shape=(
+            arrays(blocks, cells, LANES),
+            arrays(blocks, cells, LANES),
+            arrays(depth, SUBLANES, LANES),
+            arrays(2 * blocks, halo, LANES),
+            arrays(2 * blocks, halo, LANES),
+        ),
+        in_specs=[whole] * 5,
+        out_specs=[whole] * 5,
+        scratch_shapes=[pltpu.VMEM((count, width + 2 * halo, cells), jnp.float32)],
+        compiler_params=pltpu.CompilerParams(vmem_limit_bytes=32 * 2**20),
+        name="prepare",
+    )(speed, force, thickness, before, after)
+    behind_cells = lax.ppermute(last, "span", onward)
+    ahead_cells = lax.ppermute(first, "span", backward)
+    partner_before = to_partner(before)
+    partner_after = to_partner(after)
+    partner_thick = to_partner(thick_tiles)
+    partner_ahead = to_partner(ahead_cells)
+    partner_behind = to_partner(behind_cells)
+
+    wall = jnp.stack([lax.axis_index("wall"), jnp.int32(walls)])
+    field = pltpu.VMEM((blocks, cells + 2 * halo + 2 * SUBLANES, LANES), jnp.float32)
+    slope = pltpu.VMEM((3 * blocks, cells + 2 * halo + 2 * SUBLANES, LANES), jnp.float32)
+    small = pltpu.VMEM((depth, SUBLANES, LANES), jnp.float32)
+    speed_out, residual_out = pl.pallas_call(
+        functools.partial(iterate, planes, halo),
+        out_shape=(arrays(count, width, cells), arrays(count, width, cells)),
+        in_specs=[pl.BlockSpec(memory_space=pltpu.SMEM)] + [whole] * 12,
+        out_specs=[whole] * 2,
+        scratch_shapes=[pltpu.VMEM((count, width + 2 * halo, cells), jnp.float32)]
+        + [field, field, field, slope, field] * 2
+        + [small] * 3,
+        compiler_params=pltpu.CompilerParams(vmem_limit_bytes=48 * 2**20),
+        name="iterate",
+    )(wall, speed_tiles, force_tiles, thick_tiles, ahead_cells, behind_cells,
+      partner_speed, partner_force, partner_thick, partner_before, partner_after, partner_ahead, partner_behind)
+    return speed_out.reshape(shape), residual_out.reshape(shape)
+
+
+def local(starting_speed_vector, driving_source, viscosity):
+    _, instants, planes, width, cells = starting_speed_vector.shape
+    times = lax.axis_size("tm") * instants
+    halo = 2 * ITERS
+    one_instant = instants == 1 and not instant_weights(times)
+    tiled = planes * SUBLANES == LANES and cells % LANES == 0 and (width + 2 * halo) % SUBLANES == 0
+    if one_instant and tiled and (2 * halo) % SUBLANES == 0 and halo <= width:
+        return carried(starting_speed_vector, driving_source, viscosity)
+    return staged(starting_speed_vector, driving_source, viscosity)
+
+
 def solution(mesh):
     placed = (P(None, "tm", None, "wall", "span"), P(None, "tm", None, "wall", "span"), P("wall"))
     return jax.shard_map(

time: 255 us -> 85.9 us (0.34)
  waiting for transfers between devices: 142 us -> 37.2 us
  starting transfers between devices: 58.5 us -> 21.1 us
  other arithmetic: 25.5 us -> 0.17 us
  local copies, waits for them, and re-layouts: 26.6 us -> 4.58 us
  Pallas kernels: 0 us -> 21.9 us
    ppermute x36 -> x11, waiting for transfers between devices: 142 us -> 37.2 us  [the longest x1 28.1 us: carried(): before = lax.ppermute(stack(lambda a: a[:, width - halo:]), 'wall', upward)]
    ppermute x36 -> x11, starting transfers between devices: 58.5 us -> 21.1 us  [the longest x1 3.62 us: carried(): partner_speed = to_partner(speed)]
    pallas_call x0 -> x2, Pallas kernels: none -> 21.9 us  [the longest x1 19.6 us: carried(): pl.pallas_call(functools.partial(iterate, planes, halo), out_shape=(array...]
    sub x2 -> x0, other arithmetic: 9.18 us -> none  [local(): present_state - step_rate * (local_part + 0.5 * (residual_now - mirror_re...]
    reduce_sum x2 -> x0, other arithmetic: 8.98 us -> none  [descent_part(): jnp.sum(residual_now * slopes[component], axis=0)]
    ppermute x8 -> x0, local copies, waits for them, and re-layouts: 8.5 us -> none  [the longest x4 4.69 us: with_halo(): lax.ppermute(tail, axis, [(i, (i + 1) % count) for i in range(ends)])]
    slice x20 -> x3, local copies, waits for them, and re-layouts: 10.1 us -> 3.03 us  [carried(): after = lax.ppermute(stack(lambda a: a[:, :halo]), 'wall', downward)]
    rev x4 -> x0, local copies, waits for them, and re-layouts: 6.07 us -> none  [reflect(): partner = partner[:, :, :, ::-1, :]]
  transfers between devices with their start and end apart: 36 -> 11, of which waited for: 14 -> 5; matrix products, arithmetic and copies ran while one was open for 13% -> 4% of each run, Pallas kernels for 0% -> 3%
where the time goes in v1:
time: 85.9 us; the launch traced here: 85.6 us
  waiting for transfers between devices  37.2 us (43%)
  Pallas kernels  21.9 us (25%)
  starting transfers between devices  21.1 us (25%)
  local copies, waits for them, and re-layouts  4.58 us (5%)
    ppermute x1, waiting for transfers between devices, carried(): before = lax.ppermute(stack(lambda a: a[:, width - halo:]), 'wall', upward)  28.1 us
    pallas_call x1, Pallas kernels, carried(): pl.pallas_call(functools.partial(iterate, planes, halo), out_shape=(array...  19.6 us
    ppermute x1, waiting for transfers between devices, carried(): partner_ahead = to_partner(ahead_cells)  4.35 us
    ppermute x1, starting transfers between devices, carried(): partner_speed = to_partner(speed)  3.62 us
    ppermute x1, starting transfers between devices, carried(): before = lax.ppermute(stack(lambda a: a[:, width - halo:]), 'wall', upward)  3.4 us
    ppermute x1, starting transfers between devices, carried(): ahead_cells = lax.ppermute(first, 'span', backward)  3.35 us
    slice x3, local copies, waits for them, and re-layouts, carried(): after = lax.ppermute(stack(lambda a: a[:, :halo]), 'wall', downward)  3.03 us
    ppermute x1, waiting for transfers between devices, carried(): partner_behind = to_partner(behind_cells)  2.46 us
  transfers between devices with their start and end apart: 11, of which 5 were waited for; matrix products, arithmetic and copies ran while one was open for 4% of the time, Pallas kernels for 3%

profile of v1, /device:TPU:1, one launch (start us, length us, event | category | flops | bytes accessed | tf_op | source)
XLA Modules:
  0.0 85.6 jit_solution(9941346858972082171)
XLA Ops:
  0.6 3.6 %collective-permute-start.4 = (f32[48,32,128]{2,1,0:T(8,128)}, f32[48,32,128]{2,1,0:T(8,128)}, u32[]{:S(2)}, u32[]{:S(2)}) collective-permute-start(f32[48,32,128]{2,1,0:T(8,128)} %bitcast.9), channel_id=1, source_target_pairs={{0,28},{4,24},{8,20},{12,16},{16,12},{20,8},{24,4},{28,0},{1,29},{... | collective-permute-start | bytes 2359304 | tf_op jit(solution)/shard_map/ppermute | solution.py:375
  4.3 0.0 copy-start
  4.3 0.0 copy-start.1
  4.3 0.1 collective-permute-start.5
  4.4 1.2 %fusion = (f32[48,4,128]{2,1,0:T(4,128)S(1)}, f32[48,4,128]{2,1,0:T(4,128)S(1)}) fusion(f32[48,32,128]{2,1,0:T(8,128)} %bitcast.10), kind=kLoop, calls=%fused_computation.3 | loop fusion | bytes 393216 | tf_op jit(solution)/shard_map/slice | solution.py:379
  5.5 1.1 %fusion.1 = (f32[48,4,128]{2,1,0:T(4,128)S(1)}, f32[48,4,128]{2,1,0:T(4,128)S(1)}) fusion(f32[48,32,128]{2,1,0:T(8,128)} %bitcast.13), kind=kLoop, calls=%fused_computation.4 | loop fusion | bytes 393216 | tf_op jit(solution)/shard_map/slice | solution.py:379
  6.6 0.8 fusion.2
  7.4 0.1 broadcast_in_dim.11
  7.5 3.4 %collective-permute-start = (f32[97,4,128]{2,1,0:T(4,128)S(1)}, f32[97,4,128]{2,1,0:T(4,128)}, u32[]{:S(2)}, u32[]{:S(2)}) collective-permute-start(f32[97,4,128]{2,1,0:T(4,128)S(1)} %pad_maximum_fusion), channel_id=1, source_target_pairs={{0,4},{4,8},{8,12},{1,5},{5,9},{9,13},{2,6},{6,10},{10,14},{3,7},{... | collective-permute-start | bytes 595976 | tf_op jit(solution)/shard_map/ppermute | solution.py:378
  10.9 0.1 broadcast_in_dim.12
  11.0 0.0 copy-start.4
  11.0 1.9 %collective-permute-start.1 = (f32[97,4,128]{2,1,0:T(4,128)S(1)}, f32[97,4,128]{2,1,0:T(4,128)}, u32[]{:S(2)}, u32[]{:S(2)}) collective-permute-start(f32[97,4,128]{2,1,0:T(4,128)S(1)} %pad_maximum_fusion.1), channel_id=1, source_target_pairs={{4,0},{8,4},{12,8},{5,1},{9,5},{13,9},{6,2},{10,6},{14,10},{7,3},{... | collective-permute-start | bytes 595976 | tf_op jit(solution)/shard_map/ppermute | solution.py:379
  13.0 28.1 %collective-permute-done.before = f32[97,4,128]{2,1,0:T(4,128)} collective-permute-done((f32[97,4,128]{2,1,0:T(4,128)S(1)}, f32[97,4,128]{2,1,0:T(4,128)}, u32[]{:S(2)}, u32[]{:S(2)}) %collective-permute-start) | collective-permute-done | bytes 198688 | tf_op jit(solution)/shard_map/ppermute | solution.py:378
  41.0 0.8 collective-permute-done.1.after
  41.8 0.0 copy-done.4
  41.8 0.1 broadcast_in_dim.10.thickness
  41.9 0.0 copy-done
  41.9 0.0 copy-done.1
  41.9 2.4 %prepare.1 = (f32[15,128,128]{2,1,0:T(8,128)S(1)}, f32[15,128,128]{2,1,0:T(8,128)S(1)}, f32[5,8,128]{2,1,0:T(8,128)S(1)}, f32[30,4,128]{2,1,0:T(4,128)S(1)}, f32[30,4,128]{2,1,0:T(4,128)S(1)}) custom-call(f32[48,32,128]{2,1,0:T(8,128)S(1)} %bitcast.11, f32[48,32,128]{2,1,0:T(8,128)S(1)} %bitcast.14, f32[1,32,128]{2,1,0:T(8,128)S(1)} %broadcast_in_dim.10.thickness, ...), custom_call_target="tpu_custom_call" | custom-call | tf_op jit(solution)/shard_map/prepare/pallas_call | solution.py:380
  44.3 3.4 %collective-permute-start.2 = (f32[30,4,128]{2,1,0:T(4,128)S(1)}, f32[30,4,128]{2,1,0:T(4,128)S(1)}, u32[]{:S(2)}, u32[]{:S(2)}) collective-permute-start(f32[30,4,128]{2,1,0:T(4,128)S(1)} %get-tuple-element.12), channel_id=1, source_target_pairs={{1,0},{2,1},{3,2},{0,3},{5,4},{6,5},{7,6},{4,7},{9,8},{10,9},{11,1... | collective-permute-start | bytes 184328 | tf_op jit(solution)/shard_map/ppermute | solution.py:396
  47.6 0.0 collective-permute-start.3
  47.6 2.0 %collective-permute-start.6 = (f32[5,8,128]{2,1,0:T(8,128)S(1)}, f32[5,8,128]{2,1,0:T(8,128)S(1)}, u32[]{:S(2)}, u32[]{:S(2)}) collective-permute-start(f32[5,8,128]{2,1,0:T(8,128)S(1)} %get-tuple-element.11.thick_tiles), channel_id=1, source_target_pairs={{0,28},{4,24},{8,20},{12,16},{16,12},{20,8},{24,4},{28,0},{1,29},{... | collective-permute-start | bytes 61448 | tf_op jit(solution)/shard_map/ppermute | solution.py:399
  49.6 0.0 copy-start.2
  49.6 0.6 copy-done.2
  50.2 1.5 %collective-permute-done.6.partner_thick = f32[5,8,128]{2,1,0:T(8,128)S(1)} collective-permute-done((f32[5,8,128]{2,1,0:T(8,128)S(1)}, f32[5,8,128]{2,1,0:T(8,128)S(1)}, u32[]{:S(2)}, u32[]{:S(2)}) %collective-permute-start.6) | collective-permute-done | bytes 20512 | tf_op jit(solution)/shard_map/ppermute | solution.py:399
  51.7 2.0 %collective-permute-start.7 = (f32[97,4,128]{2,1,0:T(4,128)}, f32[97,4,128]{2,1,0:T(4,128)S(1)}, u32[]{:S(2)}, u32[]{:S(2)}) collective-permute-start(f32[97,4,128]{2,1,0:T(4,128)} %collective-permute-done.before), channel_id=1, source_target_pairs={{0,28},{4,24},{8,20},{12,16},{16,12},{20,8},{24,4},{28,0},{1,29},{... | collective-permute-start | bytes 595976 | tf_op jit(solution)/shard_map/ppermute | solution.py:397
  53.7 0.0 collective-permute-done.2.ahead_cells
  53.7 0.6 collective-permute-start.8
  54.4 0.0 collective-permute-done.3.behind_cells
  54.4 2.0 %collective-permute-start.9 = (f32[30,4,128]{2,1,0:T(4,128)S(1)}, f32[30,4,128]{2,1,0:T(4,128)S(1)}, u32[]{:S(2)}, u32[]{:S(2)}) collective-permute-start(f32[30,4,128]{2,1,0:T(4,128)S(1)} %collective-permute-done.2.ahead_cells), channel_id=1, source_target_pairs={{0,28},{4,24},{8,20},{12,16},{16,12},{20,8},{24,4},{28,0},{1,29},{... | collective-permute-start | bytes 184328 | tf_op jit(solution)/shard_map/ppermute | solution.py:400
  56.4 4.3 %collective-permute-done.9.partner_ahead = f32[30,4,128]{2,1,0:T(4,128)S(1)} collective-permute-done((f32[30,4,128]{2,1,0:T(4,128)S(1)}, f32[30,4,128]{2,1,0:T(4,128)S(1)}, u32[]{:S(2)}, u32[]{:S(2)}) %collective-permute-start.9) | collective-permute-done | bytes 61472 | tf_op jit(solution)/shard_map/ppermute | solution.py:400
  60.7 2.0 %collective-permute-start.10 = (f32[30,4,128]{2,1,0:T(4,128)S(1)}, f32[30,4,128]{2,1,0:T(4,128)S(1)}, u32[]{:S(2)}, u32[]{:S(2)}) collective-permute-start(f32[30,4,128]{2,1,0:T(4,128)S(1)} %collective-permute-done.3.behind_cells), channel_id=1, source_target_pairs={{0,28},{4,24},{8,20},{12,16},{16,12},{20,8},{24,4},{28,0},{1,29},{... | collective-permute-start | bytes 184328 | tf_op jit(solution)/shard_map/ppermute | solution.py:401
  62.8 0.1 pad_add_fusion.wall
  62.8 2.5 %collective-permute-done.10.partner_behind = f32[30,4,128]{2,1,0:T(4,128)S(1)} collective-permute-done((f32[30,4,128]{2,1,0:T(4,128)S(1)}, f32[30,4,128]{2,1,0:T(4,128)S(1)}, u32[]{:S(2)}, u32[]{:S(2)}) %collective-permute-start.10) | collective-permute-done | bytes 61472 | tf_op jit(solution)/shard_map/ppermute | solution.py:401
  65.3 0.0 collective-permute-done.7.partner_before
  65.3 0.0 collective-permute-done.8.partner_after
  65.3 0.0 collective-permute-done.4.partner_speed
  65.3 0.0 collective-permute-done.5.partner_force
  65.3 0.0 copy-start.3
  65.3 0.7 copy-done.3
  66.0 19.6 %iterate.1 = (f32[48,32,128]{2,1,0:T(8,128)}, f32[48,32,128]{2,1,0:T(8,128)}) custom-call(s32[2]{0:T(128)S(1)} %pad_add_fusion.wall, f32[15,128,128]{2,1,0:T(8,128)S(1)} %get-tuple-element.9.speed_tiles, f32[15,128,128]{2,1,0:T(8,128)S(1)} %get-tuple-element.10.force_tiles, f32[5,8,128]{2,1,0:T(8,128)S(1)} %copy-done.3, ...), custom_call_target="tpu_custom_call" | custom-call | tf_op jit(solution)/shard_map/iterate/pallas_call | solution.py:407
  (2 shorter events, 0.1 us)
Async XLA Ops:
  0.6 64.7 %collective-permute-start.4 = (f32[48,32,128]{2,1,0:T(8,128)}, f32[48,32,128]{2,1,0:T(8,128)}, u32[]{:S(2)}, u32[]{:S(2)}) collective-permute-start(f32[48,32,128]{2,1,0:T(8,128)} %bitcast.9), channel_id=1, source_target_pairs={{0,28},{4,24},{8,20},{12,16},{16,12},{20,8},{24,4},{28,0},{1,29},{... | collective-permute-start | bytes 2359304 | tf_op jit(solution)/shard_map/ppermute | solution.py:375
  4.3 37.6 %copy-start = (f32[3,1,16,32,128]{4,3,2,1,0:T(8,128)S(1)}, f32[3,1,16,32,128]{4,3,2,1,0:T(8,128)}, u32[]{:S(2)}) copy-start(f32[3,1,16,32,128]{4,3,2,1,0:T(8,128)} %param.3) | copy-start | bytes 2359300
  4.3 37.6 %copy-start.1 = (f32[3,1,16,32,128]{4,3,2,1,0:T(8,128)S(1)}, f32[3,1,16,32,128]{4,3,2,1,0:T(8,128)}, u32[]{:S(2)}) copy-start(f32[3,1,16,32,128]{4,3,2,1,0:T(8,128)} %param.4) | copy-start | bytes 2359300
  4.3 61.1 %collective-permute-start.5 = (f32[48,32,128]{2,1,0:T(8,128)}, f32[48,32,128]{2,1,0:T(8,128)}, u32[]{:S(2)}, u32[]{:S(2)}) collective-permute-start(f32[48,32,128]{2,1,0:T(8,128)} %bitcast.12), channel_id=1, source_target_pairs={{0,28},{4,24},{8,20},{12,16},{16,12},{20,8},{24,4},{28,0},{1,29},{... | collective-permute-start | bytes 2359304 | tf_op jit(solution)/shard_map/ppermute | solution.py:376
  7.5 33.5 %collective-permute-start = (f32[97,4,128]{2,1,0:T(4,128)S(1)}, f32[97,4,128]{2,1,0:T(4,128)}, u32[]{:S(2)}, u32[]{:S(2)}) collective-permute-start(f32[97,4,128]{2,1,0:T(4,128)S(1)} %pad_maximum_fusion), channel_id=1, source_target_pairs={{0,4},{4,8},{8,12},{1,5},{5,9},{9,13},{2,6},{6,10},{10,14},{3,7},{... | collective-permute-start | bytes 595976 | tf_op jit(solution)/shard_map/ppermute | solution.py:378
  11.0 30.8 %copy-start.4 = (f32[32]{0:T(128)S(1)}, f32[32]{0:T(128)}, u32[]{:S(2)}) copy-start(f32[32]{0:T(128)} %param.5) | copy-start | bytes 388
  11.0 30.8 %collective-permute-start.1 = (f32[97,4,128]{2,1,0:T(4,128)S(1)}, f32[97,4,128]{2,1,0:T(4,128)}, u32[]{:S(2)}, u32[]{:S(2)}) collective-permute-start(f32[97,4,128]{2,1,0:T(4,128)S(1)} %pad_maximum_fusion.1), channel_id=1, source_target_pairs={{4,0},{8,4},{12,8},{5,1},{9,5},{13,9},{6,2},{10,6},{14,10},{7,3},{... | collective-permute-start | bytes 595976 | tf_op jit(solution)/shard_map/ppermute | solution.py:379
  44.3 9.5 %collective-permute-start.2 = (f32[30,4,128]{2,1,0:T(4,128)S(1)}, f32[30,4,128]{2,1,0:T(4,128)S(1)}, u32[]{:S(2)}, u32[]{:S(2)}) collective-permute-start(f32[30,4,128]{2,1,0:T(4,128)S(1)} %get-tuple-element.12), channel_id=1, source_target_pairs={{1,0},{2,1},{3,2},{0,3},{5,4},{6,5},{7,6},{4,7},{9,8},{10,9},{11,1... | collective-permute-start | bytes 184328 | tf_op jit(solution)/shard_map/ppermute | solution.py:396
  47.6 6.8 %collective-permute-start.3 = (f32[30,4,128]{2,1,0:T(4,128)S(1)}, f32[30,4,128]{2,1,0:T(4,128)S(1)}, u32[]{:S(2)}, u32[]{:S(2)}) collective-permute-start(f32[30,4,128]{2,1,0:T(4,128)S(1)} %get-tuple-element.13), channel_id=1, source_target_pairs={{0,1},{1,2},{2,3},{3,0},{4,5},{5,6},{6,7},{7,4},{8,9},{9,10},{10,1... | collective-permute-start | bytes 184328 | tf_op jit(solution)/shard_map/ppermute | solution.py:395
  47.6 4.1 %collective-permute-start.6 = (f32[5,8,128]{2,1,0:T(8,128)S(1)}, f32[5,8,128]{2,1,0:T(8,128)S(1)}, u32[]{:S(2)}, u32[]{:S(2)}) collective-permute-start(f32[5,8,128]{2,1,0:T(8,128)S(1)} %get-tuple-element.11.thick_tiles), channel_id=1, source_target_pairs={{0,28},{4,24},{8,20},{12,16},{16,12},{20,8},{24,4},{28,0},{1,29},{... | collective-permute-start | bytes 61448 | tf_op jit(solution)/shard_map/ppermute | solution.py:399
  49.6 0.6 copy-start.2
  51.7 13.6 %collective-permute-start.7 = (f32[97,4,128]{2,1,0:T(4,128)}, f32[97,4,128]{2,1,0:T(4,128)S(1)}, u32[]{:S(2)}, u32[]{:S(2)}) collective-permute-start(f32[97,4,128]{2,1,0:T(4,128)} %collective-permute-done.before), channel_id=1, source_target_pairs={{0,28},{4,24},{8,20},{12,16},{16,12},{20,8},{24,4},{28,0},{1,29},{... | collective-permute-start | bytes 595976 | tf_op jit(solution)/shard_map/ppermute | solution.py:397
  53.7 11.6 %collective-permute-start.8 = (f32[97,4,128]{2,1,0:T(4,128)}, f32[97,4,128]{2,1,0:T(4,128)S(1)}, u32[]{:S(2)}, u32[]{:S(2)}) collective-permute-start(f32[97,4,128]{2,1,0:T(4,128)} %collective-permute-done.1.after), channel_id=1, source_target_pairs={{0,28},{4,24},{8,20},{12,16},{16,12},{20,8},{24,4},{28,0},{1,29},{... | collective-permute-start | bytes 595976 | tf_op jit(solution)/shard_map/ppermute | solution.py:398
  54.4 6.4 %collective-permute-start.9 = (f32[30,4,128]{2,1,0:T(4,128)S(1)}, f32[30,4,128]{2,1,0:T(4,128)S(1)}, u32[]{:S(2)}, u32[]{:S(2)}) collective-permute-start(f32[30,4,128]{2,1,0:T(4,128)S(1)} %collective-permute-done.2.ahead_cells), channel_id=1, source_target_pairs={{0,28},{4,24},{8,20},{12,16},{16,12},{20,8},{24,4},{28,0},{1,29},{... | collective-permute-start | bytes 184328 | tf_op jit(solution)/shard_map/ppermute | solution.py:400
  60.7 4.5 %collective-permute-start.10 = (f32[30,4,128]{2,1,0:T(4,128)S(1)}, f32[30,4,128]{2,1,0:T(4,128)S(1)}, u32[]{:S(2)}, u32[]{:S(2)}) collective-permute-start(f32[30,4,128]{2,1,0:T(4,128)S(1)} %collective-permute-done.3.behind_cells), channel_id=1, source_target_pairs={{0,28},{4,24},{8,20},{12,16},{16,12},{20,8},{24,4},{28,0},{1,29},{... | collective-permute-start | bytes 184328 | tf_op jit(solution)/shard_map/ppermute | solution.py:401
  65.3 0.7 copy-start.3

commit v2 on v1

v2 whole, which is shorter than its diff:
```python
import functools

import jax
import jax.numpy as jnp
from jax import lax
from jax.experimental import pallas as pl
from jax.experimental.pallas import tpu as pltpu
from jax.sharding import PartitionSpec as P

ITERS = 2


step_rate = 0.05
LANES = 128
SUBLANES = 8
SIGNS = (1.0, -1.0, 1.0)


def instant_weights(instants):
    weights = {}
    for offset, weight in ((1, 0.5), (-1, -0.5)):
        weights[offset % instants] = weights.get(offset % instants, 0.0) + weight
    return {offset: weight for offset, weight in weights.items() if weight != 0.0}


def with_halo(cells, sides, width, closed):
    for axis, dim in sides:
        count = lax.axis_size(axis)
        ends = count if closed else count - 1
        head = lax.slice_in_dim(cells, 0, width, axis=dim)
        tail = lax.slice_in_dim(cells, cells.shape[dim] - width, cells.shape[dim], axis=dim)
        cells = jnp.concatenate(
            [
                lax.ppermute(tail, axis, [(i, (i + 1) % count) for i in range(ends)]),
                cells,
                lax.ppermute(head, axis, [((i + 1) % count, i) for i in range(ends)]),
            ],
            axis=dim,
        )
    return cells


def time_slope(values):
    instants = values.shape[1] * lax.axis_size("tm")
    if not instant_weights(instants):
        return jnp.zeros_like(values)
    padded_state = with_halo(values, (("tm", 1),), 1, True)
    return 0.5 * (padded_state[:, 2:] - padded_state[:, :-2])


def wall_pair(values):
    padded_state = with_halo(values, (("wall", 3),), 1, False)
    return (padded_state[:, :, :, 2:], padded_state[:, :, :, :-2])


def span_pair(values):
    padded_state = with_halo(values, (("span", 4),), 1, True)
    return (padded_state[:, :, :, :, 2:], padded_state[:, :, :, :, :-2])


def along_flow(values):
    return (jnp.roll(values, -1, 2), jnp.roll(values, 1, 2))


def partner_pairs():
    times, walls = lax.axis_size("tm"), lax.axis_size("wall")
    return [
        (time * walls + wall, ((time + times // 2) % times) * walls + walls - 1 - wall)
        for time in range(times)
        for wall in range(walls)
    ]


def reflect(values):
    sign_row = jnp.array(SIGNS, jnp.float32).reshape(3, 1, 1, 1, 1)
    partner = lax.ppermute(values, ("tm", "wall"), partner_pairs())
    return partner[:, :, :, ::-1, :] * sign_row


def residual_of(present_state, mirrored, driving_source, viscous):
    neighbours = (along_flow(present_state), wall_pair(present_state), span_pair(present_state))
    slopes = [0.5 * (ahead - behind) for ahead, behind in neighbours]
    advect = (
        present_state[0:1] * slopes[0]
        + present_state[1:2] * slopes[1]
        + present_state[2:3] * slopes[2]
    )
    laplace = neighbours[0][0] + neighbours[0][1] - 2.0 * present_state
    laplace = laplace + (neighbours[1][0] + neighbours[1][1] - 2.0 * present_state)
    laplace = laplace + (neighbours[2][0] + neighbours[2][1] - 2.0 * present_state)
    residual_now = (
        time_slope(present_state)
        + advect
        - viscous * laplace
        + 0.5 * (present_state - mirrored)
        - driving_source
    )
    return (residual_now, neighbours, slopes)


def descent_part(neighbours, slopes, residual_now, viscous):
    scaled = viscous * residual_now
    wall_ahead, wall_behind = wall_pair(jnp.concatenate((residual_now, scaled), 0))
    flow_ahead, flow_behind = along_flow(residual_now)
    span_ahead, span_behind = span_pair(residual_now)
    residual_pairs = (
        (flow_ahead, flow_behind),
        (wall_ahead[:3], wall_behind[:3]),
        (span_ahead, span_behind),
    )
    transport = jnp.stack(
        [jnp.sum(residual_now * slopes[component], axis=0) for component in range(3)]
    )
    second = None
    for axis_id in range(3):
        ahead_u = neighbours[axis_id][0][axis_id : axis_id + 1]
        behind_u = neighbours[axis_id][1][axis_id : axis_id + 1]
        term = 0.5 * (ahead_u * residual_pairs[axis_id][0] - behind_u * residual_pairs[axis_id][1])
        second = term if second is None else second + term
    diffused = viscous * flow_ahead + viscous * flow_behind - 2.0 * scaled
    diffused = diffused + (wall_ahead[3:] + wall_behind[3:] - 2.0 * scaled)
    diffused = diffused + (viscous * span_ahead + viscous * span_behind - 2.0 * scaled)
    return -time_slope(residual_now) + transport - second - diffused


def staged(starting_speed_vector, driving_source, viscosity):
    viscous = viscosity[None, None, None, :, None]
    present_state = starting_speed_vector
    residual_now = starting_speed_vector
    for iteration in range(ITERS):
        mirrored = reflect(present_state)
        residual_now, neighbours, slopes = residual_of(
            present_state, mirrored, driving_source, viscous
        )
        local_part = descent_part(neighbours, slopes, residual_now, viscous)
        mirror_residual = reflect(residual_now)
        present_state = present_state - step_rate * (
            local_part + 0.5 * (residual_now - mirror_residual)
        )
    return (present_state, residual_now)


GROUP = 17


def sweep(steps, step):
    rounds = steps // GROUP

    def several(index, carry):
        for inner in range(GROUP):
            step(pl.multiple_of((index * GROUP + inner + 1) * SUBLANES, SUBLANES))
        return carry

    if rounds > 1:
        lax.fori_loop(0, rounds, several, 0)
    done = rounds * GROUP if rounds > 1 else 0
    for index in range(done, steps):
        step((index + 1) * SUBLANES)


def edges(halo, speed_first, speed_last, force_first, force_last, thickness, own_first, own_last):
    count = speed_first.shape[0] // SUBLANES
    fields = ((speed_first, speed_last, halo), (force_first, force_last, halo - 1))
    at = 0
    for first, last, held in fields:
        for row in range(held):
            for plane in range(0, count, SUBLANES):
                start = plane * SUBLANES
                own_first[at : at + SUBLANES] = first[pl.ds(start + row, SUBLANES, stride=SUBLANES), :]
                own_last[at : at + SUBLANES] = last[pl.ds(start + SUBLANES - 1 - row, SUBLANES, stride=SUBLANES), :]
                at += SUBLANES
    spread = jnp.broadcast_to(thickness[...], (SUBLANES, LANES))
    own_first[at : at + SUBLANES] = spread
    own_last[at : at + SUBLANES] = spread


def planes_of(*parts):
    return [part.at[plane] for part in parts for plane in range(part.shape[0])]


def extend_rows(rows, source, before, after, offset, held, halo):
    count, width = len(source), source[0].shape[0]
    extended = width + 2 * halo
    for plane in range(count):
        rows[pl.ds(plane * extended + halo, width), :] = source[plane][...]
    for row in range(halo):
        for plane in range(0, count, SUBLANES):
            at = offset + row * count + plane
            for edge, place in ((before, halo - 1 - row), (after, halo + width + row)):
                block = edge[pl.ds(at, SUBLANES), :] if row < held else jnp.zeros((SUBLANES, LANES), jnp.float32)
                rows[pl.ds(plane * extended + place, SUBLANES, stride=extended), :] = block


def to_tiles(rows, component, planes, tile, depth):
    extended = depth * SUBLANES
    blocks = [
        rows[pl.ds((component * planes + plane) * extended + tile, SUBLANES, stride=depth), :]
        for plane in range(planes)
    ]
    return jnp.concatenate(blocks, axis=0).T


def prepare(planes, halo, speed, force, before, after, speed_tiles, force_tiles, first, last, rows):
    count, width, cells = speed.shape
    depth = (width + 2 * halo) // SUBLANES
    blocks = 3 * depth
    fields = ((speed, speed_tiles, halo, 0), (force, force_tiles, halo - 1, halo * count))
    for part, (source, target, held, offset) in enumerate(fields):
        extend_rows(rows, planes_of(source), before, after, offset, held, halo)
        for component in range(3):
            for tile in range(depth):
                place = component * depth + tile
                block = to_tiles(rows, component, planes, tile, depth)
                target[place] = block
                first[part * blocks + place] = block[:halo]
                last[part * blocks + place] = block[cells - halo :]


def far_sizes(count, blocks, halo):
    rows = (2 * halo - 3) * count
    cells = -(-(2 * halo - 3) * blocks // SUBLANES) * SUBLANES
    return (0, rows, 2 * rows, 2 * rows + cells, 2 * rows + 2 * cells, 2 * rows + 2 * cells + SUBLANES)


def bundle(count, width, halo, before, after, ahead_cells, behind_cells, thickness, pack):
    blocks = ahead_cells.shape[0] // 2
    starts = far_sizes(count, blocks, halo)
    speed_rows = (halo - 1) * count
    force_rows = (halo - 2) * count
    for source, start in ((before, starts[0]), (after, starts[1])):
        pack[start : start + speed_rows] = source[:speed_rows]
        pack[start + speed_rows : start + speed_rows + force_rows] = source[halo * count : halo * count + force_rows]
    for source, start, last in ((ahead_cells, starts[2], False), (behind_cells, starts[3], True)):
        at = start
        for part, held in ((0, halo - 1), (1, halo - 2)):
            for cell in range(held):
                from_edge = halo - 1 - cell if last else cell
                for place in range(blocks):
                    pack[at : at + 1] = source[part * blocks + place, from_edge : from_edge + 1]
                    at += 1
    held = before.shape[0] - SUBLANES
    lane = lax.broadcasted_iota(jnp.int32, (SUBLANES, LANES), 1)
    spread = jnp.broadcast_to(thickness[...], (SUBLANES, LANES))
    parts = jnp.where(lane < width, before[held : held + SUBLANES], pltpu.roll(spread, width, 1))
    parts = jnp.where(lane < 2 * width, parts, pltpu.roll(after[held : held + SUBLANES], 2 * width, 1))
    pack[starts[4] : starts[5]] = parts


def hold(*refs):
    pass


def turn(block):
    lanes = lax.broadcasted_iota(jnp.int32, block.shape, 1)
    return jnp.take_along_axis(block, lanes ^ (SUBLANES - 1), axis=1)


def wrap(field):
    ring = field.shape[1] - 2 * SUBLANES
    field[:, SUBLANES - 1 : SUBLANES] = field[:, SUBLANES + ring - 1 : SUBLANES + ring]
    field[:, SUBLANES + ring : SUBLANES + ring + 1] = field[:, SUBLANES : SUBLANES + 1]


def turned_tiles(field, source, pack, part, planes, halo, rows):
    count = len(source)
    width, cells = source[0].shape
    depth = (width + 2 * halo) // SUBLANES
    blocks = 3 * depth
    starts = far_sizes(count, blocks, halo)
    held = halo - 1 - part
    extend_rows(rows, source, pack.at[starts[0] : starts[1]], pack.at[starts[1] : starts[2]], part * (halo - 1) * count, held, halo)
    for component in range(3):
        for tile in range(depth):
            place = component * depth + depth - 1 - tile
            block = turn(to_tiles(rows, component, planes, tile, depth))
            field[place, SUBLANES : SUBLANES + cells] = -block if SIGNS[component] < 0 else block
    offset = part * (halo - 1) * blocks
    for start, end, base, way in (
        (starts[2], starts[3], SUBLANES + cells, 1),
        (starts[3], starts[4], SUBLANES + cells + 2 * halo - 1, -1),
    ):
        edge = turn(pack[start:end])
        for cell in range(halo):
            for component in range(3):
                for tile in range(depth):
                    place = component * depth + depth - 1 - tile
                    at = offset + cell * blocks + component * depth + tile
                    line = edge[at : at + 1] if cell < held else jnp.zeros((1, LANES), jnp.float32)
                    field[place, base + way * cell : base + way * cell + 1] = -line if SIGNS[component] < 0 else line
    wrap(field)


def row_ahead(tiles, tile):
    return tiles[tile + 1] if tile + 1 < len(tiles) else pltpu.roll(tiles[0], LANES - 1, 1)


def row_behind(tiles, tile):
    return tiles[tile - 1] if tile > 0 else pltpu.roll(tiles[-1], 1, 1)


def plane_ahead(tile):
    return pltpu.roll(tile, LANES - SUBLANES, 1)


def plane_behind(tile):
    return pltpu.roll(tile, SUBLANES, 1)


def load(field, component, depth, start):
    return [field[component * depth + tile, pl.ds(start, SUBLANES), :] for tile in range(depth)]


def residual_stage(speed, mirrored, force, thick, inside, residual, slopes, steps):
    depth = thick.shape[0]

    def step(start):
        tiles = [load(speed, component, depth, start) for component in range(3)]
        for tile in range(depth):
            thin = thick[tile]
            middle = 6.0 * thin + 0.5
            half = [0.5 * tiles[component][tile] for component in range(3)]
            for component in range(3):
                place = component * depth + tile
                here = tiles[component][tile]
                pairs = (
                    (plane_ahead(here), plane_behind(here)),
                    (row_ahead(tiles[component], tile), row_behind(tiles[component], tile)),
                    (
                        speed[place, pl.ds(start + 1, SUBLANES), :],
                        speed[place, pl.ds(start - 1, SUBLANES), :],
                    ),
                )
                around = None
                total = None
                for axis_id, (ahead, behind) in enumerate(pairs):
                    slope = ahead - behind
                    if slopes is not None:
                        slopes[axis_id * 3 * depth + place, pl.ds(start, SUBLANES), :] = slope
                    both = ahead + behind
                    around = both if around is None else around + both
                    term = half[axis_id] * slope
                    total = term if total is None else total + term
                total = total - thin * around + middle * here
                total = total - 0.5 * mirrored[place, pl.ds(start, SUBLANES), :]
                if force is not None:
                    total = (total - force[place, pl.ds(start, SUBLANES), :]) * inside[tile]
                residual[place, pl.ds(start, SUBLANES), :] = total

    sweep(steps, step)


def descent_stage(speed, residual, mirrored, thick, inside, slopes, following, steps):
    depth = thick.shape[0]

    def step(start):
        speeds = [load(speed, component, depth, start) for component in range(3)]
        tiles = [load(residual, component, depth, start) for component in range(3)]
        rises = []
        falls = []
        for tile in range(depth):
            half = 0.5 * speeds[1][tile]
            rises.append(half + thick[tile])
            falls.append(half - thick[tile])
        upper = [[rises[tile] * tiles[c][tile] for tile in range(depth)] for c in range(3)]
        lower = [[falls[tile] * tiles[c][tile] for tile in range(depth)] for c in range(3)]
        for tile in range(depth):
            thin = thick[tile]
            flow = 0.5 * speeds[0][tile]
            flow_rise, flow_fall = flow + thin, flow - thin
            span_rise = 0.5 * speed[2 * depth + tile, pl.ds(start + 1, SUBLANES), :] + thin
            span_fall = 0.5 * speed[2 * depth + tile, pl.ds(start - 1, SUBLANES), :] - thin
            half = [0.5 * tiles[component][tile] for component in range(3)]
            middle = 6.0 * thin + 0.5
            rate = step_rate * inside[tile]
            for component in range(3):
                place = component * depth + tile
                here = tiles[component][tile]
                total = middle * here
                for inner in range(3):
                    slope = slopes[
                        (component * 3 + inner) * depth + tile, pl.ds(start, SUBLANES), :
                    ]
                    total = total + half[inner] * slope
                total = total - plane_ahead(flow_rise * here) + plane_behind(flow_fall * here)
                total = total - row_ahead(upper[component], tile) + row_behind(lower[component], tile)
                total = total - span_rise * residual[place, pl.ds(start + 1, SUBLANES), :]
                total = total + span_fall * residual[place, pl.ds(start - 1, SUBLANES), :]
                if mirrored is not None:
                    total = total - 0.5 * mirrored[place, pl.ds(start, SUBLANES), :]
                following[place, pl.ds(start, SUBLANES), :] = speeds[component][tile] - rate * total

    sweep(steps, step)


def before_force(planes, halo, wall, thickness, before, after, speed_tiles, force_tiles, ahead_cells, behind_cells,
                 partner_1, pack,
                 own_force, far, own_residual, far_open, own_open, far_slopes, own_thick, far_thick, inside,
                 own, own_slopes, rows):
    count = 3 * planes
    _, width, cells = partner_1.shape
    depth = own_thick.shape[0]
    blocks = 3 * depth
    for part, (field, source) in enumerate(((own, speed_tiles), (own_force, force_tiles))):
        field[:, SUBLANES : SUBLANES + cells] = source[...]
        field[:, SUBLANES + cells : SUBLANES + cells + halo] = ahead_cells[part * blocks : part * blocks + blocks]
        field[:, SUBLANES + cells + halo : SUBLANES + cells + 2 * halo] = behind_cells[part * blocks : part * blocks + blocks]
    wrap(own)
    lane = lax.broadcasted_iota(jnp.int32, (SUBLANES, LANES), 1)
    starts = far_sizes(count, blocks, halo)
    far_spread = pack[starts[4] : starts[5]]
    held = before.shape[0] - SUBLANES
    spread = jnp.broadcast_to(thickness[...], (SUBLANES, LANES))
    own_spread = jnp.where(lane < width, before[held : held + SUBLANES], pltpu.roll(spread, width, 1))
    own_spread = jnp.where(lane < 2 * width, own_spread, pltpu.roll(after[held : held + SUBLANES], 2 * width, 1))
    for tile in range(depth):
        row = tile - halo + depth * (lane % SUBLANES)
        own_thick[tile] = jnp.take_along_axis(own_spread, width + row, axis=1)
        far_thick[tile] = jnp.take_along_axis(far_spread, 2 * width - 1 - row, axis=1)
        row = wall[0] * width + row
        inside[tile] = jnp.where((row >= 0) & (row < wall[1] * width), 1.0, 0.0).astype(jnp.float32)
    turned_tiles(far, planes_of(partner_1), pack, 0, planes, halo, rows)
    steps = (cells + 2 * halo) // SUBLANES
    residual_stage(own, far, own_force, own_thick, inside, own_residual, own_slopes, steps)
    wrap(own_residual)
    residual_stage(far, own, None, far_thick, inside, far_open, far_slopes, steps)
    descent_stage(own, own_residual, None, own_thick, inside, own_slopes, own_open, steps)


def with_force(planes, halo, partner_2, partner_3, pack,
               own_force, far, own_residual, far_open, own_open, far_slopes, own_thick, far_thick, inside,
               speed_out, residual_out,
               rows, far_force, far_residual, next_residual, own, next_own, next_far, own_slopes):
    count = 3 * planes
    _, width, cells = partner_3.shape
    depth = own_thick.shape[0]
    blocks = 3 * depth
    turned_tiles(far_force, planes_of(partner_2, partner_3), pack, 1, planes, halo, rows)
    steps = (cells + 2 * halo) // SUBLANES

    def close(start):
        for place in range(blocks):
            at = pl.ds(start, SUBLANES)
            now = (far_open[place, at, :] - far_force[place, at, :]) * inside[place % depth]
            far_residual[place, at, :] = now
            own[place, at, :] = own_open[place, at, :] + (0.5 * step_rate) * now

    sweep(steps, close)
    wrap(far_residual)
    wrap(own)
    descent_stage(far, far_residual, own_residual, far_thick, inside, far_slopes, next_far, steps)
    wrap(next_far)
    far = next_far
    residual_stage(own, far, own_force, own_thick, inside, next_residual, own_slopes, steps)
    wrap(next_residual)
    residual_stage(far, own, far_force, far_thick, inside, far_residual, None, cells // SUBLANES)
    descent_stage(own, next_residual, far_residual, own_thick, inside, own_slopes, next_own, cells // SUBLANES)

    extended = depth * SUBLANES
    for field, target in ((next_residual, residual_out), (next_own, speed_out)):
        for component in range(3):
            for tile in range(depth):
                block = field[component * depth + tile, SUBLANES : SUBLANES + cells].T
                for plane in range(planes):
                    at = (component * planes + plane) * extended + tile
                    rows[pl.ds(at, SUBLANES, stride=depth), :] = block[plane * SUBLANES : (plane + 1) * SUBLANES]
        for plane in range(count):
            target[plane] = rows[pl.ds(plane * extended + halo, width), :]


def carried(starting_speed_vector, driving_source, viscosity):
    shape = starting_speed_vector.shape
    _, _, planes, width, cells = shape
    halo = 2 * ITERS
    depth = (width + 2 * halo) // SUBLANES
    blocks = 3 * depth
    count = 3 * planes
    whole = pl.BlockSpec(memory_space=pltpu.VMEM)
    arrays = lambda *sizes: jax.ShapeDtypeStruct(sizes, jnp.float32)
    grant = lambda mega: pltpu.CompilerParams(vmem_limit_bytes=mega * 2**20)
    tall = cells + 2 * halo + 2 * SUBLANES
    rows = pltpu.VMEM((count * (width + 2 * halo), cells), jnp.float32)
    field = pltpu.VMEM((blocks, tall, LANES), jnp.float32)
    slope = pltpu.VMEM((3 * blocks, tall, LANES), jnp.float32)
    speed = starting_speed_vector.reshape(count, width, cells)
    force = driving_source.reshape(count, width, cells)

    walls, spans = lax.axis_size("wall"), lax.axis_size("span")
    upward = [(i, i + 1) for i in range(walls - 1)]
    downward = [(i + 1, i) for i in range(walls - 1)]
    onward = [(i, (i + 1) % spans) for i in range(spans)]
    backward = [((i + 1) % spans, i) for i in range(spans)]
    to_partner = functools.partial(lax.ppermute, axis_name=("tm", "wall"), perm=partner_pairs())

    cut = count * 17 // 24
    partner_1 = to_partner(speed)
    sent_2 = force[:cut]
    sent_3 = force[cut:]
    any_place = pl.BlockSpec(memory_space=pl.ANY)
    after_all = lambda held, *others: pl.pallas_call(
        hold,
        out_shape=arrays(*held.shape),
        in_specs=[any_place] * (1 + len(others)),
        out_specs=any_place,
        input_output_aliases={0: 0},
        name="hold",
    )(held, *others)

    thickness = jnp.pad(viscosity, (0, LANES - width)).reshape(1, LANES)
    tops = pl.BlockSpec((count, SUBLANES, cells), lambda i: (0, 0, 0))
    ends = pl.BlockSpec((count, SUBLANES, cells), lambda i: (0, width // SUBLANES - 1, 0))
    lines = (2 * halo - 1) * count + SUBLANES
    flat = lambda ref: ref.reshape(count * SUBLANES, cells)
    own_first, own_last = pl.pallas_call(
        lambda a, b, c, d, *rest: edges(halo, flat(a), flat(b), flat(c), flat(d), *rest),
        out_shape=(arrays(lines, cells),) * 2,
        grid=(1,),
        in_specs=[tops, ends, tops, ends, pl.BlockSpec((1, LANES), lambda i: (0, 0))],
        out_specs=[pl.BlockSpec((lines, cells), lambda i: (0, 0))] * 2,
        compiler_params=grant(8),
        name="edges",
    )(speed, speed, force, force, thickness)
    before = lax.ppermute(own_last, "wall", upward)
    after = lax.ppermute(own_first, "wall", downward)
    partner_2 = to_partner(after_all(sent_2, before, after))
    speed_tiles, force_tiles, first, last = pl.pallas_call(
        functools.partial(prepare, planes, halo),
        out_shape=(arrays(blocks, cells, LANES),) * 2 + (arrays(2 * blocks, halo, LANES),) * 2,
        in_specs=[whole] * 4,
        out_specs=[whole] * 4,
        scratch_shapes=[rows],
        compiler_params=grant(12),
        name="prepare",
    )(speed, force, before, after)
    behind_cells = lax.ppermute(last, "span", onward)
    ahead_cells = lax.ppermute(first, "span", backward)
    pack = pl.pallas_call(
        functools.partial(bundle, count, width, halo),
        out_shape=arrays(far_sizes(count, blocks, halo)[-1], LANES),
        in_specs=[whole] * 5,
        out_specs=whole,
        compiler_params=grant(8),
        name="bundle",
    )(before, after, ahead_cells, behind_cells, thickness)
    far_pack = to_partner(pack)
    partner_3 = to_partner(after_all(sent_3, far_pack))

    wall = jnp.stack([lax.axis_index("wall"), jnp.int32(walls)])
    early = pl.pallas_call(
        functools.partial(before_force, planes, halo),
        out_shape=(arrays(blocks, tall, LANES),) * 5
        + (arrays(3 * blocks, tall, LANES),)
        + (arrays(depth, SUBLANES, LANES),) * 3,
        in_specs=[pl.BlockSpec(memory_space=pltpu.SMEM)] + [whole] * 9,
        out_specs=[whole] * 9,
        scratch_shapes=[field, slope, rows],
        compiler_params=grant(24),
        name="before_force",
    )(wall, thickness, before, after, speed_tiles, force_tiles, ahead_cells, behind_cells,
      partner_1, far_pack)
    speed_out, residual_out = pl.pallas_call(
        functools.partial(with_force, planes, halo),
        out_shape=(arrays(count, width, cells), arrays(count, width, cells)),
        in_specs=[whole] * 12,
        out_specs=[whole] * 2,
        scratch_shapes=[rows] + [field] * 6 + [slope],
        compiler_params=grant(32),
        name="with_force",
    )(partner_2, partner_3, far_pack, *early)
    return speed_out.reshape(shape), residual_out.reshape(shape)


def local(starting_speed_vector, driving_source, viscosity):
    _, instants, planes, width, cells = starting_speed_vector.shape
    times = lax.axis_size("tm") * instants
    halo = 2 * ITERS
    one_instant = ITERS == 2 and instants == 1 and not instant_weights(times)
    tiled = planes * SUBLANES == LANES and cells == LANES and (width + 2 * halo) % SUBLANES == 0
    rows_fit = halo <= width and 3 * width <= LANES and (2 * halo) % SUBLANES == 0
    if one_instant and tiled and rows_fit:
        return carried(starting_speed_vector, driving_source, viscosity)
    return staged(starting_speed_vector, driving_source, viscosity)


def solution(mesh):
    placed = (P(None, "tm", None, "wall", "span"), P(None, "tm", None, "wall", "span"), P("wall"))
    return jax.shard_map(
        local,
        mesh=mesh,
        in_specs=placed,
        out_specs=(P(None, "tm", None, "wall", "span"), P(None, "tm", None, "wall", "span")),
        check_vma=False,
    )
```

time: 85.9 us -> 62.9 us (0.73)
  waiting for transfers between devices: 37.2 us -> 23.1 us
  starting transfers between devices: 21.1 us -> 15.6 us
  Pallas kernels: 21.9 us -> 16.5 us
  local copies, waits for them, and re-layouts: 4.58 us -> 6.5 us
    ppermute x9 -> x6, waiting for transfers between devices: 37.2 us -> 18.2 us  [the longest x1 8.56 us: carried(): far_pack = to_partner(pack)]
    ppermute x9 -> x6, starting transfers between devices: 17.7 us -> 12.2 us  [the longest x1 4.51 us: carried(): before = lax.ppermute(own_last, 'wall', upward)]
    pallas_call x1 -> x6, Pallas kernels: 19.6 us -> 14.7 us  [the longest x1 7.4 us: carried(): pl.pallas_call(functools.partial(with_force, planes, halo), out_shape=(ar...]
    ppermute x1, waiting for transfers between devices: 0.01 us -> 3.58 us  [carried(): behind_cells = lax.ppermute(last, 'span', onward)]
    unnamed x10 -> x22, local copies, waits for them, and re-layouts: 1.34 us -> 4.3 us
    slice x3 -> x2, local copies, waits for them, and re-layouts: 3.03 us -> 1.54 us  [the longest x1 0.84 us: carried(): sent_2 = force[:cut]]
    ppermute x1, waiting for transfers between devices: 0.01 us -> 1.29 us  [carried(): ahead_cells = lax.ppermute(first, 'span', backward)]
  transfers between devices with their start and end apart: 11 -> 8, of which waited for: 5 -> 6; matrix products, arithmetic and copies ran while one was open for 4% -> 3% of each run, Pallas kernels for 3% -> 13%
where the time goes in v2:
time: 62.9 us; the launch traced here: 62.5 us
  waiting for transfers between devices  23.1 us (37%)
  Pallas kernels  16.5 us (26%)
  starting transfers between devices  15.6 us (25%)
  local copies, waits for them, and re-layouts  6.5 us (10%)
  between operations  0.69 us (1%)
    ppermute x1, waiting for transfers between devices, carried(): far_pack = to_partner(pack)  8.56 us
    pallas_call x1, Pallas kernels, carried(): pl.pallas_call(functools.partial(with_force, planes, halo), out_shape=(ar...  7.4 us
    pallas_call x1, Pallas kernels, carried(): pl.pallas_call(functools.partial(before_force, planes, halo), out_shape=(...  5.31 us
    ppermute x1, starting transfers between devices, carried(): before = lax.ppermute(own_last, 'wall', upward)  4.51 us
    ppermute x1, waiting for transfers between devices, carried(): after = lax.ppermute(own_first, 'wall', downward)  4.41 us
    unnamed x22, local copies, waits for them, and re-layouts  4.3 us
    ppermute x1, waiting for transfers between devices, carried(): behind_cells = lax.ppermute(last, 'span', onward)  3.58 us
    ppermute x1, starting transfers between devices, carried(): ahead_cells = lax.ppermute(first, 'span', backward)  3.37 us
  transfers between devices with their start and end apart: 8, of which 6 were waited for; matrix products, arithmetic and copies ran while one was open for 3% of the time, Pallas kernels for 13%

profile of v2, /device:TPU:1, one launch (start us, length us, event | category | flops | bytes accessed | tf_op | source)
XLA Modules:
  0.0 62.5 jit_solution(4212264340460371165)
XLA Ops:
  0.6 0.7 %pad_bitcast_fusion.rest_0_.thickness = f32[1,128]{1,0:T(1,128)S(1)} fusion(f32[32]{0:T(128)} %param.5), kind=kLoop, calls=%fused_computation.1 | loop fusion | bytes 640 | tf_op jit(solution)/shard_map/reshape | solution.py:508
  1.3 0.0 copy-start
  1.3 1.1 %copy-done = f32[3,1,16,32,128]{4,3,2,1,0:T(8,128)S(1)} copy-done((f32[3,1,16,32,128]{4,3,2,1,0:T(8,128)S(1)}, f32[3,1,16,32,128]{4,3,2,1,0:T(8,128)}, u32[]{:S(2)}) %copy-start) | copy-done | bytes 786456
  2.4 0.0 copy-start.1
  2.4 1.2 %edges.1 = (f32[344,128]{1,0:T(8,128)S(1)}, f32[344,128]{1,0:T(8,128)S(1)}) custom-call(f32[48,32,128]{2,1,0:T(8,128)} %bitcast.1.a.b.speed, f32[48,32,128]{2,1,0:T(8,128)} %bitcast.1.a.b.speed, f32[48,32,128]{2,1,0:T(8,128)S(1)} %bitcast.11, f32[48,32,128]{2,1,0:T(8,128)S(1)} %bitcast.12, f32[1,128]{1,0:T(1,128)S(1)} %pad_bitcast_fusion.rest_0_.thickness), custom_call_target="tpu_custom_call" | custom-call | tf_op jit(solution)/shard_map/edges/pallas_call | solution.py:513
  3.6 4.5 %collective-permute-start = (f32[344,128]{1,0:T(8,128)S(1)}, f32[344,128]{1,0:T(8,128)S(1)}, u32[]{:S(2)}, u32[]{:S(2)}) collective-permute-start(f32[344,128]{1,0:T(8,128)S(1)} %get-tuple-element.19), channel_id=1, source_target_pairs={{0,4},{4,8},{8,12},{1,5},{5,9},{9,13},{2,6},{6,10},{10,14},{3,7},{... | collective-permute-start | bytes 528392 | tf_op jit(solution)/shard_map/ppermute | solution.py:522
  8.1 1.9 %collective-permute-start.1 = (f32[344,128]{1,0:T(8,128)S(1)}, f32[344,128]{1,0:T(8,128)S(1)}, u32[]{:S(2)}, u32[]{:S(2)}) collective-permute-start(f32[344,128]{1,0:T(8,128)S(1)} %get-tuple-element.20), channel_id=1, source_target_pairs={{4,0},{8,4},{12,8},{5,1},{9,5},{13,9},{6,2},{10,6},{14,10},{7,3},{... | collective-permute-start | bytes 528392 | tf_op jit(solution)/shard_map/ppermute | solution.py:523
  10.0 2.8 %collective-permute-start.7 = (f32[48,32,128]{2,1,0:T(8,128)}, f32[48,32,128]{2,1,0:T(8,128)}, u32[]{:S(2)}, u32[]{:S(2)}) collective-permute-start(f32[48,32,128]{2,1,0:T(8,128)} %bitcast.1.a.b.speed), channel_id=1, source_target_pairs={{0,28},{4,24},{8,20},{12,16},{16,12},{20,8},{24,4},{28,0},{1,29},{... | collective-permute-start | bytes 2359304 | tf_op jit(solution)/shard_map/ppermute | solution.py:495
  12.8 0.0 collective-permute-done.refs_1_.before
  12.8 0.0 copy-start.5
  12.8 4.4 %collective-permute-done.1.refs_2_.after = f32[344,128]{1,0:T(8,128)S(1)} collective-permute-done((f32[344,128]{1,0:T(8,128)S(1)}, f32[344,128]{1,0:T(8,128)S(1)}, u32[]{:S(2)}, u32[]{:S(2)}) %collective-permute-start.1) | collective-permute-done | bytes 176160 | tf_op jit(solution)/shard_map/ppermute | solution.py:523
  17.2 0.0 copy-done.1
  17.2 0.0 copy-start.7
  17.2 1.8 %prepare.1 = (f32[15,128,128]{2,1,0:T(8,128)S(1)}, f32[15,128,128]{2,1,0:T(8,128)S(1)}, f32[30,4,128]{2,1,0:T(4,128)S(1)}, f32[30,4,128]{2,1,0:T(4,128)S(1)}) custom-call(f32[48,32,128]{2,1,0:T(8,128)} %bitcast.1.a.b.speed, f32[48,32,128]{2,1,0:T(8,128)S(1)} %bitcast.13, f32[344,128]{1,0:T(8,128)S(1)} %collective-permute-done.refs_1_.before, ...), custom_call_target="tpu_custom_call" | custom-call | tf_op jit(solution)/shard_map/prepare/pallas_call | solution.py:525
  19.1 3.4 %collective-permute-start.3 = (f32[30,4,128]{2,1,0:T(4,128)S(1)}, f32[30,4,128]{2,1,0:T(4,128)S(1)}, u32[]{:S(2)}, u32[]{:S(2)}) collective-permute-start(f32[30,4,128]{2,1,0:T(4,128)S(1)} %get-tuple-element.21), channel_id=1, source_target_pairs={{1,0},{2,1},{3,2},{0,3},{5,4},{6,5},{7,6},{4,7},{9,8},{10,9},{11,1... | collective-permute-start | bytes 184328 | tf_op jit(solution)/shard_map/ppermute | solution.py:535
  22.4 0.0 collective-permute-start.4
  22.4 1.3 %collective-permute-done.3.ahead_cells = f32[30,4,128]{2,1,0:T(4,128)S(1)} collective-permute-done((f32[30,4,128]{2,1,0:T(4,128)S(1)}, f32[30,4,128]{2,1,0:T(4,128)S(1)}, u32[]{:S(2)}, u32[]{:S(2)}) %collective-permute-start.3) | collective-permute-done | bytes 61472 | tf_op jit(solution)/shard_map/ppermute | solution.py:535
  23.7 3.6 %collective-permute-done.4.behind_cells = f32[30,4,128]{2,1,0:T(4,128)S(1)} collective-permute-done((f32[30,4,128]{2,1,0:T(4,128)S(1)}, f32[30,4,128]{2,1,0:T(4,128)S(1)}, u32[]{:S(2)}, u32[]{:S(2)}) %collective-permute-start.4) | collective-permute-done | bytes 61472 | tf_op jit(solution)/shard_map/ppermute | solution.py:534
  27.3 0.8 %bundle.1 = f32[648,128]{1,0:T(8,128)} custom-call(f32[344,128]{1,0:T(8,128)S(1)} %collective-permute-done.refs_1_.before, f32[344,128]{1,0:T(8,128)S(1)} %collective-permute-done.1.refs_2_.after, f32[30,4,128]{2,1,0:T(4,128)S(1)} %collective-permute-done.3.ahead_cells, f32[30,4,128]{2,1,0:T(4,128)S(1)} %collective-permute-done.4.behind_cells, ...), custom_call_target="tpu_custom_call" | custom-call | tf_op jit(solution)/shard_map/bundle/pallas_call | solution.py:536
  28.1 0.0 copy-done.5
  28.1 0.0 copy-done.7
  28.1 0.0 copy-start.9
  28.1 0.6 copy-done.9
  28.7 1.8 %collective-permute-start.5 = (f32[648,128]{1,0:T(8,128)}, f32[648,128]{1,0:T(8,128)S(1)}, u32[]{:S(2)}, u32[]{:S(2)}) collective-permute-start(f32[648,128]{1,0:T(8,128)} %bundle.1), channel_id=1, source_target_pairs={{0,28},{4,24},{8,20},{12,16},{16,12},{20,8},{24,4},{28,0},{1,29},{... | collective-permute-start | bytes 995336 | tf_op jit(solution)/shard_map/ppermute | solution.py:544
  30.6 0.8 %slice.8.refs_0_ = f32[34,32,128]{2,1,0:T(8,128)} slice(f32[48,32,128]{2,1,0:T(8,128)S(1)} %bitcast.14), slice={[0:34], [0:32], [0:128]} | slice | bytes 1114112 | tf_op jit(solution)/shard_map/slice | solution.py:496
  31.4 0.0 copy-start.6
  31.4 0.0 copy-start.8
  31.4 0.8 %collective-permute-start.2 = (f32[34,32,128]{2,1,0:T(8,128)}, f32[34,32,128]{2,1,0:T(8,128)}, u32[]{:S(2)}, u32[]{:S(2)}) collective-permute-start(f32[34,32,128]{2,1,0:T(8,128)} %hold.2), channel_id=1, source_target_pairs={{0,28},{4,24},{8,20},{12,16},{16,12},{20,8},{24,4},{28,0},{1,29},{... | collective-permute-start | bytes 1671176 | tf_op jit(solution)/shard_map/ppermute | solution.py:524
  32.2 0.7 %slice.9.refs_0_ = f32[14,32,128]{2,1,0:T(8,128)} slice(f32[48,32,128]{2,1,0:T(8,128)S(1)} %bitcast.15), slice={[34:48], [0:32], [0:128]} | slice | bytes 458752 | tf_op jit(solution)/shard_map/slice | solution.py:497
  32.9 8.6 %collective-permute-done.5.refs_1_.pack = f32[648,128]{1,0:T(8,128)S(1)} collective-permute-done((f32[648,128]{1,0:T(8,128)}, f32[648,128]{1,0:T(8,128)S(1)}, u32[]{:S(2)}, u32[]{:S(2)}) %collective-permute-start.5) | collective-permute-done | bytes 331808 | tf_op jit(solution)/shard_map/ppermute | solution.py:544
  41.5 0.0 copy-start.2
  41.5 0.7 %copy-done.2 = f32[648,128]{1,0:T(8,128)} copy-done((f32[648,128]{1,0:T(8,128)}, f32[648,128]{1,0:T(8,128)S(1)}, u32[]{:S(2)}) %copy-start.2) | copy-done | bytes 331800
  42.2 0.4 collective-permute-start.6
  42.6 0.1 pad_add_fusion.wall
  42.7 0.0 collective-permute-done.7.partner_1
  42.7 0.0 copy-done.6
  42.7 0.0 copy-done.8
  42.7 0.0 copy-start.3
  42.7 1.0 %copy-done.3 = f32[648,128]{1,0:T(8,128)S(1)} copy-done((f32[648,128]{1,0:T(8,128)S(1)}, f32[648,128]{1,0:T(8,128)}, u32[]{:S(2)}) %copy-start.3) | copy-done | bytes 331800
  43.6 0.0 copy-start.10
  43.6 0.8 %copy-done.10 = f32[30,4,128]{2,1,0:T(4,128)S(1)} copy-done((f32[30,4,128]{2,1,0:T(4,128)S(1)}, f32[30,4,128]{2,1,0:T(4,128)}, u32[]{:S(2)}) %copy-start.10) | copy-done | bytes 61464
  44.5 0.0 copy-start.4
  44.5 5.3 %before_force.1 = (f32[15,152,128]{2,1,0:T(8,128)S(1)}, f32[15,152,128]{2,1,0:T(8,128)S(1)}, f32[15,152,128]{2,1,0:T(8,128)S(1)}, f32[15,152,128]{2,1,0:T(8,128)...) custom-call(s32[2]{0:T(128)S(1)} %pad_add_fusion.wall, ...), custom_call_target="tpu_custom_call" | custom-call | tf_op jit(solution)/shard_map/before_force/pallas_call | solution.py:548
  49.8 2.9 %collective-permute-done.2.partner_2 = f32[34,32,128]{2,1,0:T(8,128)} collective-permute-done((f32[34,32,128]{2,1,0:T(8,128)}, f32[34,32,128]{2,1,0:T(8,128)}, u32[]{:S(2)}, u32[]{:S(2)}) %collective-permute-start.2) | collective-permute-done | bytes 557088 | tf_op jit(solution)/shard_map/ppermute | solution.py:524
  52.7 2.4 %collective-permute-done.6.partner_3 = f32[14,32,128]{2,1,0:T(8,128)S(1)} collective-permute-done((f32[14,32,128]{2,1,0:T(8,128)}, f32[14,32,128]{2,1,0:T(8,128)S(1)}, u32[]{:S(2)}, u32[]{:S(2)}) %collective-permute-start.6) | collective-permute-done | bytes 229408 | tf_op jit(solution)/shard_map/ppermute | solution.py:545
  55.1 0.0 copy-done.4
  55.1 7.4 %with_force.1 = (f32[48,32,128]{2,1,0:T(8,128)}, f32[48,32,128]{2,1,0:T(8,128)}) custom-call(f32[34,32,128]{2,1,0:T(8,128)} %collective-permute-done.2.partner_2, f32[14,32,128]{2,1,0:T(8,128)S(1)} %collective-permute-done.6.partner_3, f32[648,128]{1,0:T(8,128)S(1)} %copy-done.4, f32[15,152,128]{2,1,0:T(8,128)S(1)} %get-tuple-element.25.own_force, ...), custom_call_target="tpu_custom_call" | custom-call | tf_op jit(solution)/shard_map/with_force/pallas_call | solution.py:560
  (2 shorter events, 0.0 us)
Async XLA Ops:
  1.3 1.1 %copy-start = (f32[3,1,16,32,128]{4,3,2,1,0:T(8,128)S(1)}, f32[3,1,16,32,128]{4,3,2,1,0:T(8,128)}, u32[]{:S(2)}) copy-start(f32[3,1,16,32,128]{4,3,2,1,0:T(8,128)} %param.4) | copy-start | bytes 2359300
  2.4 14.8 %copy-start.1 = (f32[3,1,16,32,128]{4,3,2,1,0:T(8,128)S(1)}, f32[3,1,16,32,128]{4,3,2,1,0:T(8,128)}, u32[]{:S(2)}) copy-start(f32[3,1,16,32,128]{4,3,2,1,0:T(8,128)} %param.4) | copy-start | bytes 2359300
  3.6 9.2 %collective-permute-start = (f32[344,128]{1,0:T(8,128)S(1)}, f32[344,128]{1,0:T(8,128)S(1)}, u32[]{:S(2)}, u32[]{:S(2)}) collective-permute-start(f32[344,128]{1,0:T(8,128)S(1)} %get-tuple-element.19), channel_id=1, source_target_pairs={{0,4},{4,8},{8,12},{1,5},{5,9},{9,13},{2,6},{6,10},{10,14},{3,7},{... | collective-permute-start | bytes 528392 | tf_op jit(solution)/shard_map/ppermute | solution.py:522
  8.1 9.1 %collective-permute-start.1 = (f32[344,128]{1,0:T(8,128)S(1)}, f32[344,128]{1,0:T(8,128)S(1)}, u32[]{:S(2)}, u32[]{:S(2)}) collective-permute-start(f32[344,128]{1,0:T(8,128)S(1)} %get-tuple-element.20), channel_id=1, source_target_pairs={{4,0},{8,4},{12,8},{5,1},{9,5},{13,9},{6,2},{10,6},{14,10},{7,3},{... | collective-permute-start | bytes 528392 | tf_op jit(solution)/shard_map/ppermute | solution.py:523
  10.0 32.6 %collective-permute-start.7 = (f32[48,32,128]{2,1,0:T(8,128)}, f32[48,32,128]{2,1,0:T(8,128)}, u32[]{:S(2)}, u32[]{:S(2)}) collective-permute-start(f32[48,32,128]{2,1,0:T(8,128)} %bitcast.1.a.b.speed), channel_id=1, source_target_pairs={{0,28},{4,24},{8,20},{12,16},{16,12},{20,8},{24,4},{28,0},{1,29},{... | collective-permute-start | bytes 2359304 | tf_op jit(solution)/shard_map/ppermute | solution.py:495
  12.8 15.3 %copy-start.5 = (f32[344,128]{1,0:T(8,128)}, f32[344,128]{1,0:T(8,128)S(1)}, u32[]{:S(2)}) copy-start(f32[344,128]{1,0:T(8,128)S(1)} %collective-permute-done.refs_1_.before) | copy-start | bytes 528388
  17.2 10.9 %copy-start.7 = (f32[344,128]{1,0:T(8,128)}, f32[344,128]{1,0:T(8,128)S(1)}, u32[]{:S(2)}) copy-start(f32[344,128]{1,0:T(8,128)S(1)} %collective-permute-done.1.refs_2_.after) | copy-start | bytes 528388
  19.1 4.7 %collective-permute-start.3 = (f32[30,4,128]{2,1,0:T(4,128)S(1)}, f32[30,4,128]{2,1,0:T(4,128)S(1)}, u32[]{:S(2)}, u32[]{:S(2)}) collective-permute-start(f32[30,4,128]{2,1,0:T(4,128)S(1)} %get-tuple-element.21), channel_id=1, source_target_pairs={{1,0},{2,1},{3,2},{0,3},{5,4},{6,5},{7,6},{4,7},{9,8},{10,9},{11,1... | collective-permute-start | bytes 184328 | tf_op jit(solution)/shard_map/ppermute | solution.py:535
  22.4 4.9 %collective-permute-start.4 = (f32[30,4,128]{2,1,0:T(4,128)S(1)}, f32[30,4,128]{2,1,0:T(4,128)S(1)}, u32[]{:S(2)}, u32[]{:S(2)}) collective-permute-start(f32[30,4,128]{2,1,0:T(4,128)S(1)} %get-tuple-element.22), channel_id=1, source_target_pairs={{0,1},{1,2},{2,3},{3,0},{4,5},{5,6},{6,7},{7,4},{8,9},{9,10},{10,1... | collective-permute-start | bytes 184328 | tf_op jit(solution)/shard_map/ppermute | solution.py:534
  28.1 0.6 %copy-start.9 = (f32[30,4,128]{2,1,0:T(4,128)}, f32[30,4,128]{2,1,0:T(4,128)S(1)}, u32[]{:S(2)}) copy-start(f32[30,4,128]{2,1,0:T(4,128)S(1)} %collective-permute-done.4.behind_cells) | copy-start | bytes 184324
  28.7 12.8 %collective-permute-start.5 = (f32[648,128]{1,0:T(8,128)}, f32[648,128]{1,0:T(8,128)S(1)}, u32[]{:S(2)}, u32[]{:S(2)}) collective-permute-start(f32[648,128]{1,0:T(8,128)} %bundle.1), channel_id=1, source_target_pairs={{0,28},{4,24},{8,20},{12,16},{16,12},{20,8},{24,4},{28,0},{1,29},{... | collective-permute-start | bytes 995336 | tf_op jit(solution)/shard_map/ppermute | solution.py:544
  31.4 11.2 %copy-start.6 = (f32[344,128]{1,0:T(8,128)S(1)}, f32[344,128]{1,0:T(8,128)}, u32[]{:S(2)}) copy-start(f32[344,128]{1,0:T(8,128)} %copy-done.5) | copy-start | bytes 528388
  31.4 11.2 %copy-start.8 = (f32[344,128]{1,0:T(8,128)S(1)}, f32[344,128]{1,0:T(8,128)}, u32[]{:S(2)}) copy-start(f32[344,128]{1,0:T(8,128)} %copy-done.7) | copy-start | bytes 528388
  31.4 21.3 %collective-permute-start.2 = (f32[34,32,128]{2,1,0:T(8,128)}, f32[34,32,128]{2,1,0:T(8,128)}, u32[]{:S(2)}, u32[]{:S(2)}) collective-permute-start(f32[34,32,128]{2,1,0:T(8,128)} %hold.2), channel_id=1, source_target_pairs={{0,28},{4,24},{8,20},{12,16},{16,12},{20,8},{24,4},{28,0},{1,29},{... | collective-permute-start | bytes 1671176 | tf_op jit(solution)/shard_map/ppermute | solution.py:524
  41.5 0.7 %copy-start.2 = (f32[648,128]{1,0:T(8,128)}, f32[648,128]{1,0:T(8,128)S(1)}, u32[]{:S(2)}) copy-start(f32[648,128]{1,0:T(8,128)S(1)} %collective-permute-done.5.refs_1_.pack) | copy-start | bytes 995332
  42.2 12.8 %collective-permute-start.6 = (f32[14,32,128]{2,1,0:T(8,128)}, f32[14,32,128]{2,1,0:T(8,128)S(1)}, u32[]{:S(2)}, u32[]{:S(2)}) collective-permute-start(f32[14,32,128]{2,1,0:T(8,128)} %hold.3), channel_id=1, source_target_pairs={{0,28},{4,24},{8,20},{12,16},{16,12},{20,8},{24,4},{28,0},{1,29},{... | collective-permute-start | bytes 688136 | tf_op jit(solution)/shard_map/ppermute | solution.py:545
  42.7 1.0 %copy-start.3 = (f32[648,128]{1,0:T(8,128)S(1)}, f32[648,128]{1,0:T(8,128)}, u32[]{:S(2)}) copy-start(f32[648,128]{1,0:T(8,128)} %copy-done.2) | copy-start | bytes 995332
  43.6 0.8 %copy-start.10 = (f32[30,4,128]{2,1,0:T(4,128)S(1)}, f32[30,4,128]{2,1,0:T(4,128)}, u32[]{:S(2)}) copy-start(f32[30,4,128]{2,1,0:T(4,128)} %copy-done.9) | copy-start | bytes 184324
  44.5 10.6 %copy-start.4 = (f32[648,128]{1,0:T(8,128)S(1)}, f32[648,128]{1,0:T(8,128)}, u32[]{:S(2)}) copy-start(f32[648,128]{1,0:T(8,128)} %copy-done.2) | copy-start | bytes 995332

commit v3 on v2

--- a/solution.py
+++ b/solution.py
@@ -169,23 +169,29 @@
                 own_first[at : at + SUBLANES] = first[pl.ds(start + row, SUBLANES, stride=SUBLANES), :]
                 own_last[at : at + SUBLANES] = last[pl.ds(start + SUBLANES - 1 - row, SUBLANES, stride=SUBLANES), :]
                 at += SUBLANES
-    spread = jnp.broadcast_to(thickness[...], (SUBLANES, LANES))
+    spread = spread_of(thickness)
     own_first[at : at + SUBLANES] = spread
     own_last[at : at + SUBLANES] = spread
 
 
+def spread_of(thickness):
+    row = thickness[...]
+    row = jnp.concatenate([row, jnp.zeros((1, LANES - row.shape[1]), jnp.float32)], axis=1)
+    return jnp.broadcast_to(row, (SUBLANES, LANES))
+
+
 def planes_of(*parts):
     return [part.at[plane] for part in parts for plane in range(part.shape[0])]
 
 
-def extend_rows(rows, source, before, after, offset, held, halo):
+def extend_rows(rows, source, before, after, offset, held, halo, total=None, skip=0):
     count, width = len(source), source[0].shape[0]
     extended = width + 2 * halo
     for plane in range(count):
         rows[pl.ds(plane * extended + halo, width), :] = source[plane][...]
     for row in range(halo):
         for plane in range(0, count, SUBLANES):
-            at = offset + row * count + plane
+            at = offset + row * (total or count) + skip + plane
             for edge, place in ((before, halo - 1 - row), (after, halo + width + row)):
                 block = edge[pl.ds(at, SUBLANES), :] if row < held else jnp.zeros((SUBLANES, LANES), jnp.float32)
                 rows[pl.ds(plane * extended + place, SUBLANES, stride=extended), :] = block
@@ -200,7 +206,7 @@
     return jnp.concatenate(blocks, axis=0).T
 
 
-def prepare(planes, halo, speed, force, before, after, speed_tiles, force_tiles, first, last, rows):
+def prepare(planes, halo, speed, force, before, after, _, speed_tiles, force_tiles, first, last, rows):
     count, width, cells = speed.shape
     depth = (width + 2 * halo) // SUBLANES
     blocks = 3 * depth
@@ -240,7 +246,7 @@
                     at += 1
     held = before.shape[0] - SUBLANES
     lane = lax.broadcasted_iota(jnp.int32, (SUBLANES, LANES), 1)
-    spread = jnp.broadcast_to(thickness[...], (SUBLANES, LANES))
+    spread = spread_of(thickness)
     parts = jnp.where(lane < width, before[held : held + SUBLANES], pltpu.roll(spread, width, 1))
     parts = jnp.where(lane < 2 * width, parts, pltpu.roll(after[held : held + SUBLANES], 2 * width, 1))
     pack[starts[4] : starts[5]] = parts
@@ -261,33 +267,58 @@
     field[:, SUBLANES + ring : SUBLANES + ring + 1] = field[:, SUBLANES : SUBLANES + 1]
 
 
-def turned_tiles(field, source, pack, part, planes, halo, rows):
-    count = len(source)
+def turned_tiles(field, source, pack, part, planes, halo, rows, components=range(3)):
+    count = 3 * planes
     width, cells = source[0].shape
     depth = (width + 2 * halo) // SUBLANES
     blocks = 3 * depth
     starts = far_sizes(count, blocks, halo)
     held = halo - 1 - part
-    extend_rows(rows, source, pack.at[starts[0] : starts[1]], pack.at[starts[1] : starts[2]], part * (halo - 1) * count, held, halo)
-    for component in range(3):
+    before, after = pack.at[starts[0] : starts[1]], pack.at[starts[1] : starts[2]]
+    extend_rows(rows, source, before, after, part * (halo - 1) * count, held, halo, count, components[0] * planes)
+    offset = part * (halo - 1) * blocks
+    for number, component in enumerate(components):
         for tile in range(depth):
-            place = component * depth + depth - 1 - tile
-            block = turn(to_tiles(rows, component, planes, tile, depth))
+            block = turn(to_tiles(rows, number, planes, tile, depth))
+            place = number * depth + depth - 1 - tile
             field[place, SUBLANES : SUBLANES + cells] = -block if SIGNS[component] < 0 else block
-    offset = part * (halo - 1) * blocks
     for start, end, base, way in (
         (starts[2], starts[3], SUBLANES + cells, 1),
         (starts[3], starts[4], SUBLANES + cells + 2 * halo - 1, -1),
     ):
         edge = turn(pack[start:end])
         for cell in range(halo):
-            for component in range(3):
+            for number, component in enumerate(components):
                 for tile in range(depth):
-                    place = component * depth + depth - 1 - tile
+                    place = number * depth + depth - 1 - tile
                     at = offset + cell * blocks + component * depth + tile
                     line = edge[at : at + 1] if cell < held else jnp.zeros((1, LANES), jnp.float32)
                     field[place, base + way * cell : base + way * cell + 1] = -line if SIGNS[component] < 0 else line
     wrap(field)
+
+
+class Joined:
+    def __init__(self, *fields):
+        self.rows = [(field, place) for field in fields for place in range(field.shape[0])]
+
+    def __getitem__(self, at):
+        field, place = self.rows[at[0]]
+        return field[(place,) + at[1:]]
+
+
+def close_far(far_open, far_force, own_open, inside, far_residual, own, first, steps):
+    depth = inside.shape[0]
+
+    def close(start):
+        at = pl.ds(start, SUBLANES)
+        for place in range(far_force.shape[0]):
+            now = (far_open[first + place, at, :] - far_force[place, at, :]) * inside[place % depth]
+            far_residual[place, at, :] = now
+            own[place, at, :] = own_open[first + place, at, :] + (0.5 * step_rate) * now
+
+    sweep(steps, close)
+    wrap(far_residual)
+    wrap(own)
 
 
 def row_ahead(tiles, tile):
@@ -341,9 +372,12 @@
                     term = half[axis_id] * slope
                     total = term if total is None else total + term
                 total = total - thin * around + middle * here
-                total = total - 0.5 * mirrored[place, pl.ds(start, SUBLANES), :]
+                if mirrored is not None:
+                    total = total - 0.5 * mirrored[place, pl.ds(start, SUBLANES), :]
                 if force is not None:
-                    total = (total - force[place, pl.ds(start, SUBLANES), :]) * inside[tile]
+                    total = total - force[place, pl.ds(start, SUBLANES), :]
+                if inside is not None:
+                    total = total * inside[tile]
                 residual[place, pl.ds(start, SUBLANES), :] = total
 
     sweep(steps, step)
@@ -392,12 +426,11 @@
     sweep(steps, step)
 
 
-def before_force(planes, halo, wall, thickness, before, after, speed_tiles, force_tiles, ahead_cells, behind_cells,
-                 partner_1, pack,
-                 own_force, far, own_residual, far_open, own_open, far_slopes, own_thick, far_thick, inside,
-                 own, own_slopes, rows):
+def own_part(planes, halo, wall, thickness, before, after, speed_tiles, force_tiles, ahead_cells, behind_cells,
+             own, own_force, own_open, own_slopes, own_thick, inside):
     count = 3 * planes
-    _, width, cells = partner_1.shape
+    width = thickness.shape[1]
+    cells = speed_tiles.shape[1]
     depth = own_thick.shape[0]
     blocks = 3 * depth
     for part, (field, source) in enumerate(((own, speed_tiles), (own_force, force_tiles))):
@@ -406,65 +439,91 @@
         field[:, SUBLANES + cells + halo : SUBLANES + cells + 2 * halo] = behind_cells[part * blocks : part * blocks + blocks]
     wrap(own)
     lane = lax.broadcasted_iota(jnp.int32, (SUBLANES, LANES), 1)
-    starts = far_sizes(count, blocks, halo)
-    far_spread = pack[starts[4] : starts[5]]
     held = before.shape[0] - SUBLANES
-    spread = jnp.broadcast_to(thickness[...], (SUBLANES, LANES))
+    spread = spread_of(thickness)
     own_spread = jnp.where(lane < width, before[held : held + SUBLANES], pltpu.roll(spread, width, 1))
     own_spread = jnp.where(lane < 2 * width, own_spread, pltpu.roll(after[held : held + SUBLANES], 2 * width, 1))
     for tile in range(depth):
         row = tile - halo + depth * (lane % SUBLANES)
         own_thick[tile] = jnp.take_along_axis(own_spread, width + row, axis=1)
-        far_thick[tile] = jnp.take_along_axis(far_spread, 2 * width - 1 - row, axis=1)
         row = wall[0] * width + row
         inside[tile] = jnp.where((row >= 0) & (row < wall[1] * width), 1.0, 0.0).astype(jnp.float32)
+    residual_stage(own, None, own_force, own_thick, None, own_open, own_slopes, (cells + 2 * halo) // SUBLANES)
+
+
+def before_force(planes, halo, partner_1, partner_2, pack, own, own_partial, own_slopes, own_thick, inside,
+                 far, own_residual, far_open, own_open, far_slopes, far_thick, far_force, far_residual, own_next,
+                 rows):
+    count = 3 * planes
+    _, width, cells = partner_1.shape
+    depth = own_thick.shape[0]
+    blocks = 3 * depth
+    lane = lax.broadcasted_iota(jnp.int32, (SUBLANES, LANES), 1)
+    starts = far_sizes(count, blocks, halo)
+    far_spread = pack[starts[4] : starts[5]]
+    for tile in range(depth):
+        row = tile - halo + depth * (lane % SUBLANES)
+        far_thick[tile] = jnp.take_along_axis(far_spread, 2 * width - 1 - row, axis=1)
     turned_tiles(far, planes_of(partner_1), pack, 0, planes, halo, rows)
     steps = (cells + 2 * halo) // SUBLANES
-    residual_stage(own, far, own_force, own_thick, inside, own_residual, own_slopes, steps)
+
+    def close(start):
+        at = pl.ds(start, SUBLANES)
+        for place in range(blocks):
+            own_residual[place, at, :] = (own_partial[place, at, :] - 0.5 * far[place, at, :]) * inside[place % depth]
+
+    sweep(steps, close)
     wrap(own_residual)
-    residual_stage(far, own, None, far_thick, inside, far_open, far_slopes, steps)
+    residual_stage(far, own, None, far_thick, None, far_open, far_slopes, steps)
     descent_stage(own, own_residual, None, own_thick, inside, own_slopes, own_open, steps)
-
-
-def with_force(planes, halo, partner_2, partner_3, pack,
-               own_force, far, own_residual, far_open, own_open, far_slopes, own_thick, far_thick, inside,
+    turned_tiles(far_force, planes_of(partner_2), pack, 1, planes, halo, rows, range(2))
+    close_far(far_open, far_force, own_open, inside, far_residual, own_next, 0, steps)
+
+
+def with_force(planes, halo, partner_3, pack,
+               own_force, own_thick, inside, far, own_residual, far_open, own_open, far_slopes, far_thick,
+               far_force_1, far_residual_1, own_1,
                speed_out, residual_out,
-               rows, far_force, far_residual, next_residual, own, next_own, next_far, own_slopes):
+               speed_buffer, residual_buffer, sems, rows, far_force_2, far_residual_2, own_2,
+               far_mirror, next_residual, next_own, next_far, own_slopes):
     count = 3 * planes
     _, width, cells = partner_3.shape
     depth = own_thick.shape[0]
-    blocks = 3 * depth
-    turned_tiles(far_force, planes_of(partner_2, partner_3), pack, 1, planes, halo, rows)
     steps = (cells + 2 * halo) // SUBLANES
-
-    def close(start):
-        for place in range(blocks):
-            at = pl.ds(start, SUBLANES)
-            now = (far_open[place, at, :] - far_force[place, at, :]) * inside[place % depth]
-            far_residual[place, at, :] = now
-            own[place, at, :] = own_open[place, at, :] + (0.5 * step_rate) * now
-
-    sweep(steps, close)
-    wrap(far_residual)
-    wrap(own)
+    turned_tiles(far_force_2, planes_of(partner_3), pack, 1, planes, halo, rows, range(2, 3))
+    close_far(far_open, far_force_2, own_open, inside, far_residual_2, own_2, 2 * depth, steps)
+    far_force = Joined(far_force_1, far_force_2)
+    far_residual = Joined(far_residual_1, far_residual_2)
+    own = Joined(own_1, own_2)
     descent_stage(far, far_residual, own_residual, far_thick, inside, far_slopes, next_far, steps)
     wrap(next_far)
     far = next_far
     residual_stage(own, far, own_force, own_thick, inside, next_residual, own_slopes, steps)
     wrap(next_residual)
-    residual_stage(far, own, far_force, far_thick, inside, far_residual, None, cells // SUBLANES)
-    descent_stage(own, next_residual, far_residual, own_thick, inside, own_slopes, next_own, cells // SUBLANES)
-
+    residual_copies = send_out(next_residual, residual_buffer, residual_out, sems.at[0], rows, planes, depth, halo)
+    residual_stage(far, own, far_force, far_thick, inside, far_mirror, None, cells // SUBLANES)
+    descent_stage(own, next_residual, far_mirror, own_thick, inside, own_slopes, next_own, cells // SUBLANES)
+    speed_copies = send_out(next_own, speed_buffer, speed_out, sems.at[1], rows, planes, depth, halo)
+    for copy in residual_copies + speed_copies:
+        copy.wait()
+
+
+def send_out(field, buffer, target, sems, rows, planes, depth, halo):
+    _, width, cells = buffer.shape
     extended = depth * SUBLANES
-    for field, target in ((next_residual, residual_out), (next_own, speed_out)):
-        for component in range(3):
-            for tile in range(depth):
-                block = field[component * depth + tile, SUBLANES : SUBLANES + cells].T
-                for plane in range(planes):
-                    at = (component * planes + plane) * extended + tile
-                    rows[pl.ds(at, SUBLANES, stride=depth), :] = block[plane * SUBLANES : (plane + 1) * SUBLANES]
-        for plane in range(count):
-            target[plane] = rows[pl.ds(plane * extended + halo, width), :]
+    copies = []
+    for component in range(3):
+        for tile in range(depth):
+            block = field[component * depth + tile, SUBLANES : SUBLANES + cells].T
+            for plane in range(planes):
+                at = (component * planes + plane) * extended + tile
+                rows[pl.ds(at, SUBLANES, stride=depth), :] = block[plane * SUBLANES : (plane + 1) * SUBLANES]
+        for plane in range(component * planes, (component + 1) * planes):
+            buffer[plane] = rows[pl.ds(plane * extended + halo, width), :]
+        part = pl.ds(component * planes, planes)
+        copies.append(pltpu.make_async_copy(buffer.at[part], target.at[part], sems.at[component]))
+        copies[-1].start()
+    return copies
 
 
 def carried(starting_speed_vector, driving_source, viscosity):
@@ -491,7 +550,7 @@
     backward = [((i + 1) % spans, i) for i in range(spans)]
     to_partner = functools.partial(lax.ppermute, axis_name=("tm", "wall"), perm=partner_pairs())
 
-    cut = count * 17 // 24
+    cut = 2 * planes
     partner_1 = to_partner(speed)
     sent_2 = force[:cut]
     sent_3 = force[cut:]
@@ -502,10 +561,11 @@
         in_specs=[any_place] * (1 + len(others)),
         out_specs=any_place,
         input_output_aliases={0: 0},
+        compiler_params=grant(1),
         name="hold",
     )(held, *others)
 
-    thickness = jnp.pad(viscosity, (0, LANES - width)).reshape(1, LANES)
+    thickness = viscosity.reshape(1, width)
     tops = pl.BlockSpec((count, SUBLANES, cells), lambda i: (0, 0, 0))
     ends = pl.BlockSpec((count, SUBLANES, cells), lambda i: (0, width // SUBLANES - 1, 0))
     lines = (2 * halo - 1) * count + SUBLANES
@@ -514,7 +574,7 @@
         lambda a, b, c, d, *rest: edges(halo, flat(a), flat(b), flat(c), flat(d), *rest),
         out_shape=(arrays(lines, cells),) * 2,
         grid=(1,),
-        in_specs=[tops, ends, tops, ends, pl.BlockSpec((1, LANES), lambda i: (0, 0))],
+        in_specs=[tops, ends, tops, ends, pl.BlockSpec((1, width), lambda i: (0, 0))],
         out_specs=[pl.BlockSpec((lines, cells), lambda i: (0, 0))] * 2,
         compiler_params=grant(8),
         name="edges",
@@ -525,12 +585,12 @@
     speed_tiles, force_tiles, first, last = pl.pallas_call(
         functools.partial(prepare, planes, halo),
         out_shape=(arrays(blocks, cells, LANES),) * 2 + (arrays(2 * blocks, halo, LANES),) * 2,
-        in_specs=[whole] * 4,
+        in_specs=[whole] * 4 + [any_place],
         out_specs=[whole] * 4,
         scratch_shapes=[rows],
-        compiler_params=grant(12),
+        compiler_params=grant(8),
         name="prepare",
-    )(speed, force, before, after)
+    )(speed, force, before, after, partner_1)
     behind_cells = lax.ppermute(last, "span", onward)
     ahead_cells = lax.ppermute(first, "span", backward)
     pack = pl.pallas_call(
@@ -542,30 +602,43 @@
         name="bundle",
     )(before, after, ahead_cells, behind_cells, thickness)
     far_pack = to_partner(pack)
-    partner_3 = to_partner(after_all(sent_3, far_pack))
+    partner_3 = to_partner(after_all(sent_3, pack, partner_2))
 
     wall = jnp.stack([lax.axis_index("wall"), jnp.int32(walls)])
+    own, own_force, own_partial, own_slopes, own_thick, inside = pl.pallas_call(
+        functools.partial(own_part, planes, halo),
+        out_shape=(arrays(blocks, tall, LANES),) * 3
+        + (arrays(3 * blocks, tall, LANES),)
+        + (arrays(depth, SUBLANES, LANES),) * 2,
+        in_specs=[pl.BlockSpec(memory_space=pltpu.SMEM)] + [whole] * 7,
+        out_specs=[whole] * 6,
+        compiler_params=grant(14),
+        name="own_part",
+    )(wall, thickness, before, after, speed_tiles, force_tiles, ahead_cells, behind_cells)
     early = pl.pallas_call(
         functools.partial(before_force, planes, halo),
-        out_shape=(arrays(blocks, tall, LANES),) * 5
-        + (arrays(3 * blocks, tall, LANES),)
-        + (arrays(depth, SUBLANES, LANES),) * 3,
-        in_specs=[pl.BlockSpec(memory_space=pltpu.SMEM)] + [whole] * 9,
+        out_shape=(arrays(blocks, tall, LANES),) * 4
+        + (arrays(3 * blocks, tall, LANES), arrays(depth, SUBLANES, LANES))
+        + (arrays(2 * depth, tall, LANES),) * 3,
+        in_specs=[whole] * 8,
         out_specs=[whole] * 9,
-        scratch_shapes=[field, slope, rows],
-        compiler_params=grant(24),
+        scratch_shapes=[rows],
+        compiler_params=grant(20),
         name="before_force",
-    )(wall, thickness, before, after, speed_tiles, force_tiles, ahead_cells, behind_cells,
-      partner_1, far_pack)
+    )(partner_1, partner_2, far_pack, own, own_partial, own_slopes, own_thick, inside)
+    out = pltpu.VMEM((count, width, cells), jnp.float32)
     speed_out, residual_out = pl.pallas_call(
         functools.partial(with_force, planes, halo),
         out_shape=(arrays(count, width, cells), arrays(count, width, cells)),
-        in_specs=[whole] * 12,
-        out_specs=[whole] * 2,
-        scratch_shapes=[rows] + [field] * 6 + [slope],
-        compiler_params=grant(32),
+        in_specs=[whole] * 14,
+        out_specs=[any_place] * 2,
+        scratch_shapes=[out, out, pltpu.SemaphoreType.DMA((2, 3)), rows]
+        + [pltpu.VMEM((depth, tall, LANES), jnp.float32)] * 3
+        + [field] * 4
+        + [slope],
+        compiler_params=grant(30),
         name="with_force",
-    )(partner_2, partner_3, far_pack, *early)
+    )(partner_3, far_pack, own_force, own_thick, inside, *early)
     return speed_out.reshape(shape), residual_out.reshape(shape)
 
 

time: 62.9 us -> 58.8 us (0.935)
  Pallas kernels: 16.5 us -> 12.3 us
  local copies, waits for them, and re-layouts: 6.5 us -> 7.32 us
  waiting for transfers between devices: 23.1 us -> 22.3 us
    ppermute x1, waiting for transfers between devices: 0.01 us -> 13.6 us  [carried(): before = lax.ppermute(own_last, 'wall', upward)]
    ppermute x1, waiting for transfers between devices: 8.56 us -> 2.81 us  [carried(): far_pack = to_partner(pack)]
    ppermute x1, waiting for transfers between devices: 4.41 us -> 1.02 us  [carried(): after = lax.ppermute(own_first, 'wall', downward)]
    unnamed x22 -> x20, local copies, waits for them, and re-layouts: 4.3 us -> 7.27 us
    ppermute x1, waiting for transfers between devices: 2.9 us -> 0.01 us  [carried(): partner_2 = to_partner(after_all(sent_2, before, after))]
    ppermute x1, starting transfers between devices: 4.51 us -> 2.05 us  [carried(): before = lax.ppermute(own_last, 'wall', upward)]
    ppermute x1, waiting for transfers between devices: 2.35 us -> 0.01 us  [carried(): partner_3 = to_partner(after_all(sent_3, pack, partner_2))]
    pallas_call x0 -> x1, Pallas kernels: none -> 1.54 us  [carried(): pl.pallas_call(functools.partial(own_part, planes, halo), out_shape=(arra...]
  transfers between devices with their start and end apart: 8 -> 8, of which waited for: 6 -> 5; matrix products, arithmetic and copies ran while one was open for 3% -> 0% of each run, Pallas kernels for 13% -> 11%
where the time goes in v3:
time: 58.8 us; the launch traced here: 58.5 us
  waiting for transfers between devices  22.3 us (38%)
  starting transfers between devices  15.8 us (27%)
  Pallas kernels  12.3 us (21%)
  local copies, waits for them, and re-layouts  7.32 us (12%)
  between operations  0.74 us (1%)
    ppermute x1, waiting for transfers between devices, carried(): before = lax.ppermute(own_last, 'wall', upward)  13.6 us
    unnamed x20, local copies, waits for them, and re-layouts  7.27 us
    pallas_call x1, Pallas kernels, carried(): pl.pallas_call(functools.partial(with_force, planes, halo), out_shape=(ar...  5.99 us
    pallas_call x1, Pallas kernels, carried(): pl.pallas_call(functools.partial(before_force, planes, halo), out_shape=(...  3.89 us
    ppermute x1, starting transfers between devices, carried(): partner_1 = to_partner(speed)  3.62 us
    ppermute x1, waiting for transfers between devices, carried(): behind_cells = lax.ppermute(last, 'span', onward)  3.58 us
    ppermute x1, starting transfers between devices, carried(): ahead_cells = lax.ppermute(first, 'span', backward)  3.32 us
    ppermute x1, waiting for transfers between devices, carried(): far_pack = to_partner(pack)  2.81 us
  transfers between devices with their start and end apart: 8, of which 5 were waited for; matrix products, arithmetic and copies ran while one was open for 0% of the time, Pallas kernels for 11%

profile of v3, /device:TPU:1, one launch (start us, length us, event | category | flops | bytes accessed | tf_op | source)
XLA Modules:
  0.0 58.5 jit_solution(15183957686536821709)
XLA Ops:
  0.6 3.6 %collective-permute-start.2 = (f32[48,32,128]{2,1,0:T(8,128)}, f32[48,32,128]{2,1,0:T(8,128)S(1)}, u32[]{:S(2)}, u32[]{:S(2)}) collective-permute-start(f32[48,32,128]{2,1,0:T(8,128)} %bitcast.16), channel_id=1, source_target_pairs={{0,28},{4,24},{8,20},{12,16},{16,12},{20,8},{24,4},{28,0},{1,29},{... | collective-permute-start | bytes 2359304 | tf_op jit(solution)/shard_map/ppermute | solution.py:554
  4.3 0.0 copy-start
  4.3 1.1 %copy-done = f32[3,1,16,32,128]{4,3,2,1,0:T(8,128)S(1)} copy-done((f32[3,1,16,32,128]{4,3,2,1,0:T(8,128)S(1)}, f32[3,1,16,32,128]{4,3,2,1,0:T(8,128)}, u32[]{:S(2)}) %copy-start) | copy-done | bytes 786456
  5.4 0.0 copy-start.2
  5.4 1.1 %copy-done.2 = f32[3,1,16,32,128]{4,3,2,1,0:T(8,128)S(1)} copy-done((f32[3,1,16,32,128]{4,3,2,1,0:T(8,128)S(1)}, f32[3,1,16,32,128]{4,3,2,1,0:T(8,128)}, u32[]{:S(2)}) %copy-start.2) | copy-done | bytes 786456
  6.5 0.0 copy-start.8
  6.5 0.7 %copy-done.8 = f32[32]{0:T(128)S(1)} copy-done((f32[32]{0:T(128)S(1)}, f32[32]{0:T(128)}, u32[]{:S(2)}) %copy-start.8) | copy-done | bytes 152
  7.2 0.0 copy-start.1
  7.2 0.1 edges.1
  7.3 2.1 %collective-permute-start = (f32[344,128]{1,0:T(8,128)S(1)}, f32[344,128]{1,0:T(8,128)S(1)}, u32[]{:S(2)}, u32[]{:S(2)}) collective-permute-start(f32[344,128]{1,0:T(8,128)S(1)} %get-tuple-element.25), channel_id=1, source_target_pairs={{0,4},{4,8},{8,12},{1,5},{5,9},{9,13},{2,6},{6,10},{10,14},{3,7},{... | collective-permute-start | bytes 528392 | tf_op jit(solution)/shard_map/ppermute | solution.py:582
  9.4 0.0 copy-start.3
  9.4 2.5 %collective-permute-start.1 = (f32[344,128]{1,0:T(8,128)S(1)}, f32[344,128]{1,0:T(8,128)S(1)}, u32[]{:S(2)}, u32[]{:S(2)}) collective-permute-start(f32[344,128]{1,0:T(8,128)S(1)} %get-tuple-element.26), channel_id=1, source_target_pairs={{4,0},{8,4},{12,8},{5,1},{9,5},{13,9},{6,2},{10,6},{14,10},{7,3},{... | collective-permute-start | bytes 528392 | tf_op jit(solution)/shard_map/ppermute | solution.py:583
  11.9 0.0 copy-done.1
  12.0 13.6 %collective-permute-done.before.refs_1_ = f32[344,128]{1,0:T(8,128)S(1)} collective-permute-done((f32[344,128]{1,0:T(8,128)S(1)}, f32[344,128]{1,0:T(8,128)S(1)}, u32[]{:S(2)}, u32[]{:S(2)}) %collective-permute-start) | collective-permute-done | bytes 176160 | tf_op jit(solution)/shard_map/ppermute | solution.py:582
  25.6 1.0 %collective-permute-done.1.after.refs_2_ = f32[344,128]{1,0:T(8,128)S(1)} collective-permute-done((f32[344,128]{1,0:T(8,128)S(1)}, f32[344,128]{1,0:T(8,128)S(1)}, u32[]{:S(2)}, u32[]{:S(2)}) %collective-permute-start.1) | collective-permute-done | bytes 176160 | tf_op jit(solution)/shard_map/ppermute | solution.py:583
  26.6 0.0 copy-start.9
  26.6 1.4 %collective-permute-start.5 = (f32[32,32,128]{2,1,0:T(8,128)S(1)}, f32[32,32,128]{2,1,0:T(8,128)S(1)}, u32[]{:S(2)}, u32[]{:S(2)}) collective-permute-start(f32[32,32,128]{2,1,0:T(8,128)S(1)} %hold.2), channel_id=1, source_target_pairs={{0,28},{4,24},{8,20},{12,16},{16,12},{20,8},{24,4},{28,0},{1,29},{... | collective-permute-start | bytes 1572872 | tf_op jit(solution)/shard_map/ppermute | solution.py:584
  28.0 0.0 collective-permute-done.2._.partner_1
  28.0 0.0 copy-done.3
  28.0 0.6 %prepare.1 = (f32[15,128,128]{2,1,0:T(8,128)S(1)}, f32[15,128,128]{2,1,0:T(8,128)S(1)}, f32[30,4,128]{2,1,0:T(4,128)S(1)}, f32[30,4,128]{2,1,0:T(4,128)S(1)}) custom-call(f32[48,32,128]{2,1,0:T(8,128)S(1)} %bitcast.19, f32[48,32,128]{2,1,0:T(8,128)S(1)} %bitcast.15, f32[344,128]{1,0:T(8,128)S(1)} %collective-permute-done.before.refs_1_, ...), custom_call_target="tpu_custom_call" | custom-call | tf_op jit(solution)/shard_map/prepare/pallas_call | solution.py:585
  28.7 0.0 copy-start.4
  28.7 1.0 %copy-done.4 = f32[15,128,128]{2,1,0:T(8,128)} copy-done((f32[15,128,128]{2,1,0:T(8,128)}, f32[15,128,128]{2,1,0:T(8,128)S(1)}, u32[]{:S(2)}) %copy-start.4) | copy-done | bytes 983064
  29.6 0.0 copy-start.6
  29.6 1.0 %copy-done.6 = f32[15,128,128]{2,1,0:T(8,128)} copy-done((f32[15,128,128]{2,1,0:T(8,128)}, f32[15,128,128]{2,1,0:T(8,128)S(1)}, u32[]{:S(2)}) %copy-start.6) | copy-done | bytes 983064
  30.6 3.3 %collective-permute-start.3 = (f32[30,4,128]{2,1,0:T(4,128)S(1)}, f32[30,4,128]{2,1,0:T(4,128)S(1)}, u32[]{:S(2)}, u32[]{:S(2)}) collective-permute-start(f32[30,4,128]{2,1,0:T(4,128)S(1)} %get-tuple-element.27), channel_id=1, source_target_pairs={{1,0},{2,1},{3,2},{0,3},{5,4},{6,5},{7,6},{4,7},{9,8},{10,9},{11,1... | collective-permute-start | bytes 184328 | tf_op jit(solution)/shard_map/ppermute | solution.py:595
  33.9 0.0 collective-permute-start.4
  33.9 1.3 %collective-permute-done.3.ahead_cells = f32[30,4,128]{2,1,0:T(4,128)S(1)} collective-permute-done((f32[30,4,128]{2,1,0:T(4,128)S(1)}, f32[30,4,128]{2,1,0:T(4,128)S(1)}, u32[]{:S(2)}, u32[]{:S(2)}) %collective-permute-start.3) | collective-permute-done | bytes 61472 | tf_op jit(solution)/shard_map/ppermute | solution.py:595
  35.2 3.6 %collective-permute-done.4.behind_cells = f32[30,4,128]{2,1,0:T(4,128)S(1)} collective-permute-done((f32[30,4,128]{2,1,0:T(4,128)S(1)}, f32[30,4,128]{2,1,0:T(4,128)S(1)}, u32[]{:S(2)}, u32[]{:S(2)}) %collective-permute-start.4) | collective-permute-done | bytes 61472 | tf_op jit(solution)/shard_map/ppermute | solution.py:594
  38.8 0.0 copy-done.9
  38.8 0.1 bundle.1.refs_1_
  38.9 2.7 %collective-permute-start.7 = (f32[648,128]{1,0:T(8,128)S(1)}, f32[648,128]{1,0:T(8,128)S(1)}, u32[]{:S(2)}, u32[]{:S(2)}) collective-permute-start(f32[648,128]{1,0:T(8,128)S(1)} %bundle.1.refs_1_), channel_id=1, source_target_pairs={{0,28},{4,24},{8,20},{12,16},{16,12},{20,8},{24,4},{28,0},{1,29},{... | collective-permute-start | bytes 995336 | tf_op jit(solution)/shard_map/ppermute | solution.py:604
  41.6 0.0 collective-permute-done.5.refs_2_.partner_2
  41.7 0.1 collective-permute-start.6
  41.7 0.1 pad_add_fusion.wall
  41.8 0.0 copy-start.5
  41.8 1.2 %copy-done.5 = f32[15,128,128]{2,1,0:T(8,128)S(1)} copy-done((f32[15,128,128]{2,1,0:T(8,128)S(1)}, f32[15,128,128]{2,1,0:T(8,128)}, u32[]{:S(2)}) %copy-start.5) | copy-done | bytes 983064
  43.0 0.0 copy-start.7
  43.0 1.2 %copy-done.7 = f32[15,128,128]{2,1,0:T(8,128)S(1)} copy-done((f32[15,128,128]{2,1,0:T(8,128)S(1)}, f32[15,128,128]{2,1,0:T(8,128)}, u32[]{:S(2)}) %copy-start.7) | copy-done | bytes 983064
  44.2 1.5 %own_part.1 = (f32[15,152,128]{2,1,0:T(8,128)S(1)}, f32[15,152,128]{2,1,0:T(8,128)S(1)}, f32[15,152,128]{2,1,0:T(8,128)S(1)}, f32[45,152,128]{2,1,0:T(8,128)S(1)...) custom-call(s32[2]{0:T(128)S(1)} %pad_add_fusion.wall, f32[1,32]{1,0:T(1,128)S(1)} %bitcast.23, ...), custom_call_target="tpu_custom_call" | custom-call | tf_op jit(solution)/shard_map/own_part/pallas_call | solution.py:608
  45.8 2.8 %collective-permute-done.7.pack = f32[648,128]{1,0:T(8,128)S(1)} collective-permute-done((f32[648,128]{1,0:T(8,128)S(1)}, f32[648,128]{1,0:T(8,128)S(1)}, u32[]{:S(2)}, u32[]{:S(2)}) %collective-permute-start.7) | collective-permute-done | bytes 331808 | tf_op jit(solution)/shard_map/ppermute | solution.py:604
  48.6 3.9 %before_force.1 = (f32[15,152,128]{2,1,0:T(8,128)S(1)}, f32[15,152,128]{2,1,0:T(8,128)S(1)}, f32[15,152,128]{2,1,0:T(8,128)S(1)}, f32[15,152,128]{2,1,0:T(8,128)...) custom-call(f32[48,32,128]{2,1,0:T(8,128)S(1)} %collective-permute-d, ...), custom_call_target="tpu_custom_call" | custom-call | tf_op jit(solution)/shard_map/before_force/pallas_call | solution.py:618
  52.5 0.0 collective-permute-done.6.partner_3
  52.5 6.0 %with_force.1 = (f32[48,32,128]{2,1,0:T(8,128)}, f32[48,32,128]{2,1,0:T(8,128)}) custom-call(f32[16,32,128]{2,1,0:T(8,128)S(1)} %collective-permute-done.6.partner_3, f32[648,128]{1,0:T(8,128)S(1)} %collective-permute-done.7.pack, f32[15,152,128]{2,1,0:T(8,128)S(1)} %get-tuple-element.31.own_force, f32[5,8,128]{2,1,0:T(8,128)S(1)} %get-tuple-element.32.own_thick, ...), custom_call_target="tpu_custom_call" | custom-call | tf_op jit(solution)/shard_map/with_force/pallas_call | solution.py:630
  (4 shorter events, 0.1 us)
Async XLA Ops:
  0.6 27.4 %collective-permute-start.2 = (f32[48,32,128]{2,1,0:T(8,128)}, f32[48,32,128]{2,1,0:T(8,128)S(1)}, u32[]{:S(2)}, u32[]{:S(2)}) collective-permute-start(f32[48,32,128]{2,1,0:T(8,128)} %bitcast.16), channel_id=1, source_target_pairs={{0,28},{4,24},{8,20},{12,16},{16,12},{20,8},{24,4},{28,0},{1,29},{... | collective-permute-start | bytes 2359304 | tf_op jit(solution)/shard_map/ppermute | solution.py:554
  4.3 1.1 %copy-start = (f32[3,1,16,32,128]{4,3,2,1,0:T(8,128)S(1)}, f32[3,1,16,32,128]{4,3,2,1,0:T(8,128)}, u32[]{:S(2)}) copy-start(f32[3,1,16,32,128]{4,3,2,1,0:T(8,128)} %param.4) | copy-start | bytes 2359300
  5.4 1.1 %copy-start.2 = (f32[3,1,16,32,128]{4,3,2,1,0:T(8,128)S(1)}, f32[3,1,16,32,128]{4,3,2,1,0:T(8,128)}, u32[]{:S(2)}) copy-start(f32[3,1,16,32,128]{4,3,2,1,0:T(8,128)} %param.3) | copy-start | bytes 2359300
  6.5 0.7 %copy-start.8 = (f32[32]{0:T(128)S(1)}, f32[32]{0:T(128)}, u32[]{:S(2)}) copy-start(f32[32]{0:T(128)} %param.5) | copy-start | bytes 388
  7.2 4.8 %copy-start.1 = (f32[3,1,16,32,128]{4,3,2,1,0:T(8,128)S(1)}, f32[3,1,16,32,128]{4,3,2,1,0:T(8,128)}, u32[]{:S(2)}) copy-start(f32[3,1,16,32,128]{4,3,2,1,0:T(8,128)} %param.4) | copy-start | bytes 2359300
  7.3 18.3 %collective-permute-start = (f32[344,128]{1,0:T(8,128)S(1)}, f32[344,128]{1,0:T(8,128)S(1)}, u32[]{:S(2)}, u32[]{:S(2)}) collective-permute-start(f32[344,128]{1,0:T(8,128)S(1)} %get-tuple-element.25), channel_id=1, source_target_pairs={{0,4},{4,8},{8,12},{1,5},{5,9},{9,13},{2,6},{6,10},{10,14},{3,7},{... | collective-permute-start | bytes 528392 | tf_op jit(solution)/shard_map/ppermute | solution.py:582
  9.4 18.7 %copy-start.3 = (f32[3,1,16,32,128]{4,3,2,1,0:T(8,128)S(1)}, f32[3,1,16,32,128]{4,3,2,1,0:T(8,128)}, u32[]{:S(2)}) copy-start(f32[3,1,16,32,128]{4,3,2,1,0:T(8,128)} %param.3) | copy-start | bytes 2359300
  9.4 17.2 %collective-permute-start.1 = (f32[344,128]{1,0:T(8,128)S(1)}, f32[344,128]{1,0:T(8,128)S(1)}, u32[]{:S(2)}, u32[]{:S(2)}) collective-permute-start(f32[344,128]{1,0:T(8,128)S(1)} %get-tuple-element.26), channel_id=1, source_target_pairs={{4,0},{8,4},{12,8},{5,1},{9,5},{13,9},{6,2},{10,6},{14,10},{7,3},{... | collective-permute-start | bytes 528392 | tf_op jit(solution)/shard_map/ppermute | solution.py:583
  26.6 12.2 %copy-start.9 = (f32[32]{0:T(128)S(1)}, f32[32]{0:T(128)}, u32[]{:S(2)}) copy-start(f32[32]{0:T(128)} %param.5) | copy-start | bytes 388
  26.6 15.0 %collective-permute-start.5 = (f32[32,32,128]{2,1,0:T(8,128)S(1)}, f32[32,32,128]{2,1,0:T(8,128)S(1)}, u32[]{:S(2)}, u32[]{:S(2)}) collective-permute-start(f32[32,32,128]{2,1,0:T(8,128)S(1)} %hold.2), channel_id=1, source_target_pairs={{0,28},{4,24},{8,20},{12,16},{16,12},{20,8},{24,4},{28,0},{1,29},{... | collective-permute-start | bytes 1572872 | tf_op jit(solution)/shard_map/ppermute | solution.py:584
  28.7 1.0 %copy-start.4 = (f32[15,128,128]{2,1,0:T(8,128)}, f32[15,128,128]{2,1,0:T(8,128)S(1)}, u32[]{:S(2)}) copy-start(f32[15,128,128]{2,1,0:T(8,128)S(1)} %get-tuple-element.29.speed_tiles) | copy-start | bytes 2949124
  29.6 1.0 %copy-start.6 = (f32[15,128,128]{2,1,0:T(8,128)}, f32[15,128,128]{2,1,0:T(8,128)S(1)}, u32[]{:S(2)}) copy-start(f32[15,128,128]{2,1,0:T(8,128)S(1)} %get-tuple-element.30.force_tiles) | copy-start | bytes 2949124
  30.6 4.6 %collective-permute-start.3 = (f32[30,4,128]{2,1,0:T(4,128)S(1)}, f32[30,4,128]{2,1,0:T(4,128)S(1)}, u32[]{:S(2)}, u32[]{:S(2)}) collective-permute-start(f32[30,4,128]{2,1,0:T(4,128)S(1)} %get-tuple-element.27), channel_id=1, source_target_pairs={{1,0},{2,1},{3,2},{0,3},{5,4},{6,5},{7,6},{4,7},{9,8},{10,9},{11,1... | collective-permute-start | bytes 184328 | tf_op jit(solution)/shard_map/ppermute | solution.py:595
  33.9 4.9 %collective-permute-start.4 = (f32[30,4,128]{2,1,0:T(4,128)S(1)}, f32[30,4,128]{2,1,0:T(4,128)S(1)}, u32[]{:S(2)}, u32[]{:S(2)}) collective-permute-start(f32[30,4,128]{2,1,0:T(4,128)S(1)} %get-tuple-element.28), channel_id=1, source_target_pairs={{0,1},{1,2},{2,3},{3,0},{4,5},{5,6},{6,7},{7,4},{8,9},{9,10},{10,1... | collective-permute-start | bytes 184328 | tf_op jit(solution)/shard_map/ppermute | solution.py:594
  38.9 9.7 %collective-permute-start.7 = (f32[648,128]{1,0:T(8,128)S(1)}, f32[648,128]{1,0:T(8,128)S(1)}, u32[]{:S(2)}, u32[]{:S(2)}) collective-permute-start(f32[648,128]{1,0:T(8,128)S(1)} %bundle.1.refs_1_), channel_id=1, source_target_pairs={{0,28},{4,24},{8,20},{12,16},{16,12},{20,8},{24,4},{28,0},{1,29},{... | collective-permute-start | bytes 995336 | tf_op jit(solution)/shard_map/ppermute | solution.py:604
  41.7 10.8 %collective-permute-start.6 = (f32[16,32,128]{2,1,0:T(8,128)S(1)}, f32[16,32,128]{2,1,0:T(8,128)S(1)}, u32[]{:S(2)}, u32[]{:S(2)}) collective-permute-start(f32[16,32,128]{2,1,0:T(8,128)S(1)} %hold.3), channel_id=1, source_target_pairs={{0,28},{4,24},{8,20},{12,16},{16,12},{20,8},{24,4},{28,0},{1,29},{... | collective-permute-start | bytes 786440 | tf_op jit(solution)/shard_map/ppermute | solution.py:605
  41.8 1.2 %copy-start.5 = (f32[15,128,128]{2,1,0:T(8,128)S(1)}, f32[15,128,128]{2,1,0:T(8,128)}, u32[]{:S(2)}) copy-start(f32[15,128,128]{2,1,0:T(8,128)} %copy-done.4) | copy-start | bytes 2949124
  43.0 1.2 %copy-start.7 = (f32[15,128,128]{2,1,0:T(8,128)S(1)}, f32[15,128,128]{2,1,0:T(8,128)}, u32[]{:S(2)}) copy-start(f32[15,128,128]{2,1,0:T(8,128)} %copy-done.6) | copy-start | bytes 2949124

commit v4 on v3

--- a/solution.py
+++ b/solution.py
@@ -206,20 +206,27 @@
     return jnp.concatenate(blocks, axis=0).T
 
 
-def prepare(planes, halo, speed, force, before, after, _, speed_tiles, force_tiles, first, last, rows):
-    count, width, cells = speed.shape
+def tile_fields(planes, halo, speed, force, before, after, rows):
+    count, width, _ = speed.shape
     depth = (width + 2 * halo) // SUBLANES
-    blocks = 3 * depth
-    fields = ((speed, speed_tiles, halo, 0), (force, force_tiles, halo - 1, halo * count))
-    for part, (source, target, held, offset) in enumerate(fields):
+    for part, (source, held, offset) in enumerate(((speed, halo, 0), (force, halo - 1, halo * count))):
         extend_rows(rows, planes_of(source), before, after, offset, held, halo)
         for component in range(3):
             for tile in range(depth):
-                place = component * depth + tile
-                block = to_tiles(rows, component, planes, tile, depth)
-                target[place] = block
-                first[part * blocks + place] = block[:halo]
-                last[part * blocks + place] = block[cells - halo :]
+                yield (part * 3 + component) * depth + tile, to_tiles(rows, component, planes, tile, depth)
+
+
+def edge_cells(planes, halo, speed, force, before, after, _, first, last, rows):
+    cells = speed.shape[-1]
+    for place, block in tile_fields(planes, halo, speed, force, before, after, rows):
+        first[place] = block[:halo]
+        last[place] = block[cells - halo :]
+
+
+def own_tiles(planes, halo, speed, force, before, after, _, speed_tiles, force_tiles, rows):
+    blocks = speed_tiles.shape[0]
+    for place, block in tile_fields(planes, halo, speed, force, before, after, rows):
+        (speed_tiles if place < blocks else force_tiles)[place % blocks] = block
 
 
 def far_sizes(count, blocks, halo):
@@ -228,7 +235,7 @@
     return (0, rows, 2 * rows, 2 * rows + cells, 2 * rows + 2 * cells, 2 * rows + 2 * cells + SUBLANES)
 
 
-def bundle(count, width, halo, before, after, ahead_cells, behind_cells, thickness, pack):
+def bundle(count, width, halo, before, after, ahead_cells, behind_cells, thickness, _, pack):
     blocks = ahead_cells.shape[0] // 2
     starts = far_sizes(count, blocks, halo)
     speed_rows = (halo - 1) * count
@@ -582,25 +589,34 @@
     before = lax.ppermute(own_last, "wall", upward)
     after = lax.ppermute(own_first, "wall", downward)
     partner_2 = to_partner(after_all(sent_2, before, after))
-    speed_tiles, force_tiles, first, last = pl.pallas_call(
-        functools.partial(prepare, planes, halo),
-        out_shape=(arrays(blocks, cells, LANES),) * 2 + (arrays(2 * blocks, halo, LANES),) * 2,
+    first, last = pl.pallas_call(
+        functools.partial(edge_cells, planes, halo),
+        out_shape=(arrays(2 * blocks, halo, LANES),) * 2,
         in_specs=[whole] * 4 + [any_place],
-        out_specs=[whole] * 4,
+        out_specs=[whole] * 2,
         scratch_shapes=[rows],
         compiler_params=grant(8),
-        name="prepare",
+        name="edge_cells",
     )(speed, force, before, after, partner_1)
+    speed_tiles, force_tiles = pl.pallas_call(
+        functools.partial(own_tiles, planes, halo),
+        out_shape=(arrays(blocks, cells, LANES),) * 2,
+        in_specs=[whole] * 4 + [any_place],
+        out_specs=[whole] * 2,
+        scratch_shapes=[rows],
+        compiler_params=grant(8),
+        name="own_tiles",
+    )(speed, force, before, after, first)
     behind_cells = lax.ppermute(last, "span", onward)
     ahead_cells = lax.ppermute(first, "span", backward)
     pack = pl.pallas_call(
         functools.partial(bundle, count, width, halo),
         out_shape=arrays(far_sizes(count, blocks, halo)[-1], LANES),
-        in_specs=[whole] * 5,
+        in_specs=[whole] * 5 + [any_place],
         out_specs=whole,
         compiler_params=grant(8),
         name="bundle",
-    )(before, after, ahead_cells, behind_cells, thickness)
+    )(before, after, ahead_cells, behind_cells, thickness, force_tiles)
     far_pack = to_partner(pack)
     partner_3 = to_partner(after_all(sent_3, pack, partner_2))
 

time: 58.8 us -> 57.3 us (0.974)
  waiting for transfers between devices: 22.3 us -> 18.2 us
  starting transfers between devices: 15.8 us -> 18.2 us
  Pallas kernels: 12.3 us -> 13.9 us
  local copies, waits for them, and re-layouts: 7.32 us -> 5.86 us
    ppermute x1, waiting for transfers between devices: 3.58 us -> 0.02 us  [carried(): behind_cells = lax.ppermute(last, 'span', onward)]
    ppermute x1, starting transfers between devices: 0.08 us -> 2.44 us  [carried(): partner_3 = to_partner(after_all(sent_3, pack, partner_2))]
    unnamed x20 -> x16, local copies, waits for them, and re-layouts: 7.27 us -> 5.1 us
    ppermute x1, waiting for transfers between devices: 0.01 us -> 1.59 us  [carried(): partner_2 = to_partner(after_all(sent_2, before, after))]
    ppermute x1, starting transfers between devices: 0.01 us -> 1.35 us  [carried(): behind_cells = lax.ppermute(last, 'span', onward)]
    ppermute x1, waiting for transfers between devices: 1.29 us -> 0.01 us  [carried(): ahead_cells = lax.ppermute(first, 'span', backward)]
    ppermute x1, starting transfers between devices: 3.32 us -> 2.09 us  [carried(): ahead_cells = lax.ppermute(first, 'span', backward)]
    pallas_call x1, Pallas kernels: 5.99 us -> 6.96 us  [carried(): pl.pallas_call(functools.partial(with_force, planes, halo), out_shape=(ar...]
  transfers between devices with their start and end apart: 8 -> 8, of which waited for: 5 -> 4; matrix products, arithmetic and copies ran while one was open for 0% -> 1% of each run, Pallas kernels for 11% -> 12%
where the time goes in v4:
time: 57.3 us; the launch traced here: 57 us
  starting transfers between devices  18.2 us (32%)
  waiting for transfers between devices  18.2 us (32%)
  Pallas kernels  13.9 us (24%)
  local copies, waits for them, and re-layouts  5.86 us (10%)
  between operations  0.74 us (1%)
    ppermute x1, waiting for transfers between devices, carried(): before = lax.ppermute(own_last, 'wall', upward)  13.6 us
    pallas_call x1, Pallas kernels, carried(): pl.pallas_call(functools.partial(with_force, planes, halo), out_shape=(ar...  6.96 us
    unnamed x16, local copies, waits for them, and re-layouts  5.1 us
    pallas_call x1, Pallas kernels, carried(): pl.pallas_call(functools.partial(before_force, planes, halo), out_shape=(...  3.89 us
    ppermute x1, starting transfers between devices, carried(): partner_1 = to_partner(speed)  3.62 us
    ppermute x1, starting transfers between devices, carried(): far_pack = to_partner(pack)  2.73 us
    ppermute x1, starting transfers between devices, carried(): after = lax.ppermute(own_first, 'wall', downward)  2.54 us
    ppermute x1, starting transfers between devices, carried(): partner_3 = to_partner(after_all(sent_3, pack, partner_2))  2.44 us
  transfers between devices with their start and end apart: 8, of which 4 were waited for; matrix products, arithmetic and copies ran while one was open for 1% of the time, Pallas kernels for 12%

profile of v4, /device:TPU:1, one launch (start us, length us, event | category | flops | bytes accessed | tf_op | source)
XLA Modules:
  0.0 57.0 jit_solution(16060331138855488162)
XLA Ops:
  0.6 3.6 %collective-permute-start.2 = (f32[48,32,128]{2,1,0:T(8,128)}, f32[48,32,128]{2,1,0:T(8,128)S(1)}, u32[]{:S(2)}, u32[]{:S(2)}) collective-permute-start(f32[48,32,128]{2,1,0:T(8,128)} %bitcast.17), channel_id=1, source_target_pairs={{0,28},{4,24},{8,20},{12,16},{16,12},{20,8},{24,4},{28,0},{1,29},{... | collective-permute-start | bytes 2359304 | tf_op jit(solution)/shard_map/ppermute | solution.py:561
  4.3 0.0 copy-start
  4.3 1.1 %copy-done = f32[3,1,16,32,128]{4,3,2,1,0:T(8,128)S(1)} copy-done((f32[3,1,16,32,128]{4,3,2,1,0:T(8,128)S(1)}, f32[3,1,16,32,128]{4,3,2,1,0:T(8,128)}, u32[]{:S(2)}) %copy-start) | copy-done | bytes 786456
  5.4 0.0 copy-start.2
  5.4 1.1 %copy-done.2 = f32[3,1,16,32,128]{4,3,2,1,0:T(8,128)S(1)} copy-done((f32[3,1,16,32,128]{4,3,2,1,0:T(8,128)S(1)}, f32[3,1,16,32,128]{4,3,2,1,0:T(8,128)}, u32[]{:S(2)}) %copy-start.2) | copy-done | bytes 786456
  6.5 0.0 copy-start.6
  6.5 0.7 %copy-done.6 = f32[32]{0:T(128)S(1)} copy-done((f32[32]{0:T(128)S(1)}, f32[32]{0:T(128)}, u32[]{:S(2)}) %copy-start.6) | copy-done | bytes 152
  7.2 0.0 copy-start.1
  7.2 0.1 edges.1
  7.3 2.1 %collective-permute-start = (f32[344,128]{1,0:T(8,128)S(1)}, f32[344,128]{1,0:T(8,128)S(1)}, u32[]{:S(2)}, u32[]{:S(2)}) collective-permute-start(f32[344,128]{1,0:T(8,128)S(1)} %get-tuple-element.25), channel_id=1, source_target_pairs={{0,4},{4,8},{8,12},{1,5},{5,9},{9,13},{2,6},{6,10},{10,14},{3,7},{... | collective-permute-start | bytes 528392 | tf_op jit(solution)/shard_map/ppermute | solution.py:589
  9.4 0.0 copy-start.3
  9.4 2.5 %collective-permute-start.1 = (f32[344,128]{1,0:T(8,128)S(1)}, f32[344,128]{1,0:T(8,128)S(1)}, u32[]{:S(2)}, u32[]{:S(2)}) collective-permute-start(f32[344,128]{1,0:T(8,128)S(1)} %get-tuple-element.26), channel_id=1, source_target_pairs={{4,0},{8,4},{12,8},{5,1},{9,5},{13,9},{6,2},{10,6},{14,10},{7,3},{... | collective-permute-start | bytes 528392 | tf_op jit(solution)/shard_map/ppermute | solution.py:590
  11.9 0.0 copy-done.1
  12.0 13.6 %collective-permute-done.before.refs_1_ = f32[344,128]{1,0:T(8,128)S(1)} collective-permute-done((f32[344,128]{1,0:T(8,128)S(1)}, f32[344,128]{1,0:T(8,128)S(1)}, u32[]{:S(2)}, u32[]{:S(2)}) %collective-permute-start) | collective-permute-done | bytes 176160 | tf_op jit(solution)/shard_map/ppermute | solution.py:589
  25.6 1.0 %collective-permute-done.1.after.refs_2_ = f32[344,128]{1,0:T(8,128)S(1)} collective-permute-done((f32[344,128]{1,0:T(8,128)S(1)}, f32[344,128]{1,0:T(8,128)S(1)}, u32[]{:S(2)}, u32[]{:S(2)}) %collective-permute-start.1) | collective-permute-done | bytes 176160 | tf_op jit(solution)/shard_map/ppermute | solution.py:590
  26.6 1.4 %collective-permute-start.5 = (f32[32,32,128]{2,1,0:T(8,128)S(1)}, f32[32,32,128]{2,1,0:T(8,128)S(1)}, u32[]{:S(2)}, u32[]{:S(2)}) collective-permute-start(f32[32,32,128]{2,1,0:T(8,128)S(1)} %hold.2), channel_id=1, source_target_pairs={{0,28},{4,24},{8,20},{12,16},{16,12},{20,8},{24,4},{28,0},{1,29},{... | collective-permute-start | bytes 1572872 | tf_op jit(solution)/shard_map/ppermute | solution.py:591
  28.0 0.0 collective-permute-done.2._.partner_1
  28.0 0.0 copy-done.3
  28.0 0.6 %edge_cells.1 = (f32[30,4,128]{2,1,0:T(4,128)S(1)}, f32[30,4,128]{2,1,0:T(4,128)S(1)}) custom-call(f32[48,32,128]{2,1,0:T(8,128)S(1)} %bitcast.20, f32[48,32,128]{2,1,0:T(8,128)S(1)} %bitcast.15, f32[344,128]{1,0:T(8,128)S(1)} %collective-permute-done.before.refs_1_, f32[344,128]{1,0:T(8,128)S(1)} %collective-permute-done.1.after.refs_2_, ...), custom_call_target="tpu_custom_call" | custom-call | tf_op jit(solution)/shard_map/edge_cells/pallas_call | solution.py:592
  28.7 0.0 copy-start.7
  28.7 1.3 %collective-permute-start.4 = (f32[30,4,128]{2,1,0:T(4,128)S(1)}, f32[30,4,128]{2,1,0:T(4,128)S(1)}, u32[]{:S(2)}, u32[]{:S(2)}) collective-permute-start(f32[30,4,128]{2,1,0:T(4,128)S(1)} %get-tuple-element.28), channel_id=1, source_target_pairs={{0,1},{1,2},{2,3},{3,0},{4,5},{5,6},{6,7},{7,4},{8,9},{9,10},{10,1... | collective-permute-start | bytes 184328 | tf_op jit(solution)/shard_map/ppermute | solution.py:610
  30.0 2.1 %collective-permute-start.3 = (f32[30,4,128]{2,1,0:T(4,128)S(1)}, f32[30,4,128]{2,1,0:T(4,128)S(1)}, u32[]{:S(2)}, u32[]{:S(2)}) collective-permute-start(f32[30,4,128]{2,1,0:T(4,128)S(1)} %get-tuple-element.27._), channel_id=1, source_target_pairs={{1,0},{2,1},{3,2},{0,3},{5,4},{6,5},{7,6},{4,7},{9,8},{10,9},{11,1... | collective-permute-start | bytes 184328 | tf_op jit(solution)/shard_map/ppermute | solution.py:611
  32.1 0.6 %own_tiles.1 = (f32[15,128,128]{2,1,0:T(8,128)S(1)}, f32[15,128,128]{2,1,0:T(8,128)S(1)}) custom-call(f32[48,32,128]{2,1,0:T(8,128)S(1)} %bitcast.21, f32[48,32,128]{2,1,0:T(8,128)S(1)} %bitcast.16, f32[344,128]{1,0:T(8,128)S(1)} %collective-permute-done.before.refs_1_, f32[344,128]{1,0:T(8,128)S(1)} %collective-permute-done.1.after.refs_2_, ...), custom_call_target="tpu_custom_call" | custom-call | tf_op jit(solution)/shard_map/own_tiles/pallas_call | solution.py:601
  32.8 0.0 copy-start.4
  32.8 1.0 %copy-done.4 = f32[15,128,128]{2,1,0:T(8,128)} copy-done((f32[15,128,128]{2,1,0:T(8,128)}, f32[15,128,128]{2,1,0:T(8,128)S(1)}, u32[]{:S(2)}) %copy-start.4) | copy-done | bytes 983064
  33.7 0.0 collective-permute-done.4.behind_cells
  33.8 0.0 collective-permute-done.3.ahead_cells
  33.8 0.0 copy-done.7
  33.8 0.1 bundle.1.refs_1_
  33.8 2.7 %collective-permute-start.7 = (f32[648,128]{1,0:T(8,128)S(1)}, f32[648,128]{1,0:T(8,128)S(1)}, u32[]{:S(2)}, u32[]{:S(2)}) collective-permute-start(f32[648,128]{1,0:T(8,128)S(1)} %bundle.1.refs_1_), channel_id=1, source_target_pairs={{0,28},{4,24},{8,20},{12,16},{16,12},{20,8},{24,4},{28,0},{1,29},{... | collective-permute-start | bytes 995336 | tf_op jit(solution)/shard_map/ppermute | solution.py:620
  36.6 0.7 %slice_bitcast_fusion.refs_0_ = f32[16,32,128]{2,1,0:T(8,128)} fusion(f32[3,1,16,32,128]{4,3,2,1,0:T(8,128)S(1)} %copy-done.1), kind=kLoop, calls=%fused_computation | loop fusion | bytes 524288 | tf_op jit(solution)/shard_map/slice | solution.py:563
  37.3 1.6 %collective-permute-done.5.refs_2_.partner_2 = f32[32,32,128]{2,1,0:T(8,128)S(1)} collective-permute-done((f32[32,32,128]{2,1,0:T(8,128)S(1)}, f32[32,32,128]{2,1,0:T(8,128)S(1)}, u32[]{:S(2)}, u32[]{:S(2)}) %collective-permute-start.5) | collective-permute-done | bytes 524320 | tf_op jit(solution)/shard_map/ppermute | solution.py:591
  38.9 2.4 %collective-permute-start.6 = (f32[16,32,128]{2,1,0:T(8,128)}, f32[16,32,128]{2,1,0:T(8,128)}, u32[]{:S(2)}, u32[]{:S(2)}) collective-permute-start(f32[16,32,128]{2,1,0:T(8,128)} %hold.3), channel_id=1, source_target_pairs={{0,28},{4,24},{8,20},{12,16},{16,12},{20,8},{24,4},{28,0},{1,29},{... | collective-permute-start | bytes 786440 | tf_op jit(solution)/shard_map/ppermute | solution.py:621
  41.3 0.1 pad_add_fusion.wall
  41.4 0.0 copy-start.5
  41.4 1.2 %copy-done.5 = f32[15,128,128]{2,1,0:T(8,128)S(1)} copy-done((f32[15,128,128]{2,1,0:T(8,128)S(1)}, f32[15,128,128]{2,1,0:T(8,128)}, u32[]{:S(2)}) %copy-start.5) | copy-done | bytes 983064
  42.6 1.5 %own_part.1 = (f32[15,152,128]{2,1,0:T(8,128)S(1)}, f32[15,152,128]{2,1,0:T(8,128)S(1)}, f32[15,152,128]{2,1,0:T(8,128)S(1)}, f32[45,152,128]{2,1,0:T(8,128)S(1)...) custom-call(s32[2]{0:T(128)S(1)} %pad_add_fusion.wall, f32[1,32]{1,0:T(1,128)S(1)} %bitcast.25, ...), custom_call_target="tpu_custom_call" | custom-call | tf_op jit(solution)/shard_map/own_part/pallas_call | solution.py:624
  44.1 1.9 %collective-permute-done.7.pack = f32[648,128]{1,0:T(8,128)S(1)} collective-permute-done((f32[648,128]{1,0:T(8,128)S(1)}, f32[648,128]{1,0:T(8,128)S(1)}, u32[]{:S(2)}, u32[]{:S(2)}) %collective-permute-start.7) | collective-permute-done | bytes 331808 | tf_op jit(solution)/shard_map/ppermute | solution.py:620
  46.1 3.9 %before_force.1 = (f32[15,152,128]{2,1,0:T(8,128)S(1)}, f32[15,152,128]{2,1,0:T(8,128)S(1)}, f32[15,152,128]{2,1,0:T(8,128)S(1)}, f32[15,152,128]{2,1,0:T(8,128)...) custom-call(f32[48,32,128]{2,1,0:T(8,128)S(1)} %collective-permute-d, ...), custom_call_target="tpu_custom_call" | custom-call | tf_op jit(solution)/shard_map/before_force/pallas_call | solution.py:634
  50.0 0.0 collective-permute-done.6.partner_3
  50.0 7.0 %with_force.1 = (f32[48,32,128]{2,1,0:T(8,128)}, f32[48,32,128]{2,1,0:T(8,128)}) custom-call(f32[16,32,128]{2,1,0:T(8,128)} %collective-permute-done.6.partner_3, f32[648,128]{1,0:T(8,128)S(1)} %collective-permute-done.7.pack, f32[15,152,128]{2,1,0:T(8,128)S(1)} %get-tuple-element.31.own_force, f32[5,8,128]{2,1,0:T(8,128)S(1)} %get-tuple-element.32.own_thick, ...), custom_call_target="tpu_custom_call" | custom-call | tf_op jit(solution)/shard_map/with_force/pallas_call | solution.py:646
  (3 shorter events, 0.0 us)
Async XLA Ops:
  0.6 27.4 %collective-permute-start.2 = (f32[48,32,128]{2,1,0:T(8,128)}, f32[48,32,128]{2,1,0:T(8,128)S(1)}, u32[]{:S(2)}, u32[]{:S(2)}) collective-permute-start(f32[48,32,128]{2,1,0:T(8,128)} %bitcast.17), channel_id=1, source_target_pairs={{0,28},{4,24},{8,20},{12,16},{16,12},{20,8},{24,4},{28,0},{1,29},{... | collective-permute-start | bytes 2359304 | tf_op jit(solution)/shard_map/ppermute | solution.py:561
  4.3 1.1 %copy-start = (f32[3,1,16,32,128]{4,3,2,1,0:T(8,128)S(1)}, f32[3,1,16,32,128]{4,3,2,1,0:T(8,128)}, u32[]{:S(2)}) copy-start(f32[3,1,16,32,128]{4,3,2,1,0:T(8,128)} %param.4) | copy-start | bytes 2359300
  5.4 1.1 %copy-start.2 = (f32[3,1,16,32,128]{4,3,2,1,0:T(8,128)S(1)}, f32[3,1,16,32,128]{4,3,2,1,0:T(8,128)}, u32[]{:S(2)}) copy-start(f32[3,1,16,32,128]{4,3,2,1,0:T(8,128)} %param.3) | copy-start | bytes 2359300
  6.5 0.7 %copy-start.6 = (f32[32]{0:T(128)S(1)}, f32[32]{0:T(128)}, u32[]{:S(2)}) copy-start(f32[32]{0:T(128)} %param.5) | copy-start | bytes 388
  7.2 4.8 %copy-start.1 = (f32[3,1,16,32,128]{4,3,2,1,0:T(8,128)S(1)}, f32[3,1,16,32,128]{4,3,2,1,0:T(8,128)}, u32[]{:S(2)}) copy-start(f32[3,1,16,32,128]{4,3,2,1,0:T(8,128)} %param.4) | copy-start | bytes 2359300
  7.3 18.3 %collective-permute-start = (f32[344,128]{1,0:T(8,128)S(1)}, f32[344,128]{1,0:T(8,128)S(1)}, u32[]{:S(2)}, u32[]{:S(2)}) collective-permute-start(f32[344,128]{1,0:T(8,128)S(1)} %get-tuple-element.25), channel_id=1, source_target_pairs={{0,4},{4,8},{8,12},{1,5},{5,9},{9,13},{2,6},{6,10},{10,14},{3,7},{... | collective-permute-start | bytes 528392 | tf_op jit(solution)/shard_map/ppermute | solution.py:589
  9.4 18.7 %copy-start.3 = (f32[3,1,16,32,128]{4,3,2,1,0:T(8,128)S(1)}, f32[3,1,16,32,128]{4,3,2,1,0:T(8,128)}, u32[]{:S(2)}) copy-start(f32[3,1,16,32,128]{4,3,2,1,0:T(8,128)} %param.3) | copy-start | bytes 2359300
  9.4 17.2 %collective-permute-start.1 = (f32[344,128]{1,0:T(8,128)S(1)}, f32[344,128]{1,0:T(8,128)S(1)}, u32[]{:S(2)}, u32[]{:S(2)}) collective-permute-start(f32[344,128]{1,0:T(8,128)S(1)} %get-tuple-element.26), channel_id=1, source_target_pairs={{4,0},{8,4},{12,8},{5,1},{9,5},{13,9},{6,2},{10,6},{14,10},{7,3},{... | collective-permute-start | bytes 528392 | tf_op jit(solution)/shard_map/ppermute | solution.py:590
  26.6 12.3 %collective-permute-start.5 = (f32[32,32,128]{2,1,0:T(8,128)S(1)}, f32[32,32,128]{2,1,0:T(8,128)S(1)}, u32[]{:S(2)}, u32[]{:S(2)}) collective-permute-start(f32[32,32,128]{2,1,0:T(8,128)S(1)} %hold.2), channel_id=1, source_target_pairs={{0,28},{4,24},{8,20},{12,16},{16,12},{20,8},{24,4},{28,0},{1,29},{... | collective-permute-start | bytes 1572872 | tf_op jit(solution)/shard_map/ppermute | solution.py:591
  28.7 5.1 %copy-start.7 = (f32[32]{0:T(128)S(1)}, f32[32]{0:T(128)}, u32[]{:S(2)}) copy-start(f32[32]{0:T(128)} %param.5) | copy-start | bytes 388
  28.7 5.1 %collective-permute-start.4 = (f32[30,4,128]{2,1,0:T(4,128)S(1)}, f32[30,4,128]{2,1,0:T(4,128)S(1)}, u32[]{:S(2)}, u32[]{:S(2)}) collective-permute-start(f32[30,4,128]{2,1,0:T(4,128)S(1)} %get-tuple-element.28), channel_id=1, source_target_pairs={{0,1},{1,2},{2,3},{3,0},{4,5},{5,6},{6,7},{7,4},{8,9},{9,10},{10,1... | collective-permute-start | bytes 184328 | tf_op jit(solution)/shard_map/ppermute | solution.py:610
  30.0 3.7 %collective-permute-start.3 = (f32[30,4,128]{2,1,0:T(4,128)S(1)}, f32[30,4,128]{2,1,0:T(4,128)S(1)}, u32[]{:S(2)}, u32[]{:S(2)}) collective-permute-start(f32[30,4,128]{2,1,0:T(4,128)S(1)} %get-tuple-element.27._), channel_id=1, source_target_pairs={{1,0},{2,1},{3,2},{0,3},{5,4},{6,5},{7,6},{4,7},{9,8},{10,9},{11,1... | collective-permute-start | bytes 184328 | tf_op jit(solution)/shard_map/ppermute | solution.py:611
  32.8 1.0 %copy-start.4 = (f32[15,128,128]{2,1,0:T(8,128)}, f32[15,128,128]{2,1,0:T(8,128)S(1)}, u32[]{:S(2)}) copy-start(f32[15,128,128]{2,1,0:T(8,128)S(1)} %get-tuple-element.30.speed_tiles) | copy-start | bytes 2949124
  33.8 12.3 %collective-permute-start.7 = (f32[648,128]{1,0:T(8,128)S(1)}, f32[648,128]{1,0:T(8,128)S(1)}, u32[]{:S(2)}, u32[]{:S(2)}) collective-permute-start(f32[648,128]{1,0:T(8,128)S(1)} %bundle.1.refs_1_), channel_id=1, source_target_pairs={{0,28},{4,24},{8,20},{12,16},{16,12},{20,8},{24,4},{28,0},{1,29},{... | collective-permute-start | bytes 995336 | tf_op jit(solution)/shard_map/ppermute | solution.py:620
  38.9 11.1 %collective-permute-start.6 = (f32[16,32,128]{2,1,0:T(8,128)}, f32[16,32,128]{2,1,0:T(8,128)}, u32[]{:S(2)}, u32[]{:S(2)}) collective-permute-start(f32[16,32,128]{2,1,0:T(8,128)} %hold.3), channel_id=1, source_target_pairs={{0,28},{4,24},{8,20},{12,16},{16,12},{20,8},{24,4},{28,0},{1,29},{... | collective-permute-start | bytes 786440 | tf_op jit(solution)/shard_map/ppermute | solution.py:621
  41.4 1.2 %copy-start.5 = (f32[15,128,128]{2,1,0:T(8,128)S(1)}, f32[15,128,128]{2,1,0:T(8,128)}, u32[]{:S(2)}) copy-start(f32[15,128,128]{2,1,0:T(8,128)} %copy-done.4) | copy-start | bytes 2949124

commit v5 on v4

--- a/solution.py
+++ b/solution.py
@@ -487,14 +487,24 @@
     close_far(far_open, far_force, own_open, inside, far_residual, own_next, 0, steps)
 
 
-def with_force(planes, halo, partner_3, pack,
+def with_force(planes, halo, partner_last, pack,
                own_force, own_thick, inside, far, own_residual, far_open, own_open, far_slopes, far_thick,
                far_force_1, far_residual_1, own_1,
                speed_out, residual_out,
                speed_buffer, residual_buffer, sems, rows, far_force_2, far_residual_2, own_2,
-               far_mirror, next_residual, next_own, next_far, own_slopes):
-    count = 3 * planes
+               far_mirror, next_residual, next_own, next_far, own_slopes, partner_3, fetch_sems):
     _, width, cells = partner_3.shape
+    share = partner_3.shape[0] // fetch_sems.shape[0]
+    fetches = [
+        pltpu.make_async_copy(
+            partner_last.at[pl.ds(index * share, share)], partner_3.at[pl.ds(index * share, share)], fetch_sems.at[index]
+        )
+        for index in range(fetch_sems.shape[0])
+    ]
+    for fetch in fetches:
+        fetch.start()
+    for fetch in fetches:
+        fetch.wait()
     depth = own_thick.shape[0]
     steps = (cells + 2 * halo) // SUBLANES
     turned_tiles(far_force_2, planes_of(partner_3), pack, 1, planes, halo, rows, range(2, 3))
@@ -646,12 +656,12 @@
     speed_out, residual_out = pl.pallas_call(
         functools.partial(with_force, planes, halo),
         out_shape=(arrays(count, width, cells), arrays(count, width, cells)),
-        in_specs=[whole] * 14,
+        in_specs=[any_place] + [whole] * 13,
         out_specs=[any_place] * 2,
         scratch_shapes=[out, out, pltpu.SemaphoreType.DMA((2, 3)), rows]
         + [pltpu.VMEM((depth, tall, LANES), jnp.float32)] * 3
         + [field] * 4
-        + [slope],
+        + [slope, pltpu.VMEM((count - cut, width, cells), jnp.float32), pltpu.SemaphoreType.DMA((8,))],
         compiler_params=grant(30),
         name="with_force",
     )(partner_3, far_pack, own_force, own_thick, inside, *early)

time: 57.3 us -> 57.3 us (level)
  no operation moved by 1% of the time
where the time goes in v5:
time: 57.3 us; the launch traced here: 56.9 us
  starting transfers between devices  18.2 us (32%)
  waiting for transfers between devices  18.2 us (32%)
  Pallas kernels  13.9 us (24%)
  local copies, waits for them, and re-layouts  5.86 us (10%)
  between operations  0.74 us (1%)
    ppermute x1, waiting for transfers between devices, carried(): before = lax.ppermute(own_last, 'wall', upward)  13.6 us
    pallas_call x1, Pallas kernels, carried(): pl.pallas_call(functools.partial(with_force, planes, halo), out_shape=(ar...  6.95 us
    unnamed x16, local copies, waits for them, and re-layouts  5.1 us
    pallas_call x1, Pallas kernels, carried(): pl.pallas_call(functools.partial(before_force, planes, halo), out_shape=(...  3.89 us
    ppermute x1, starting transfers between devices, carried(): partner_1 = to_partner(speed)  3.62 us
    ppermute x1, starting transfers between devices, carried(): far_pack = to_partner(pack)  2.73 us
    ppermute x1, starting transfers between devices, carried(): after = lax.ppermute(own_first, 'wall', downward)  2.54 us
    ppermute x1, starting transfers between devices, carried(): partner_3 = to_partner(after_all(sent_3, pack, partner_2))  2.44 us
  transfers between devices with their start and end apart: 8, of which 4 were waited for; matrix products, arithmetic and copies ran while one was open for 1% of the time, Pallas kernels for 12%

profile of v5, /device:TPU:1, one launch (start us, length us, event | category | flops | bytes accessed | tf_op | source)
XLA Modules:
  0.0 56.9 jit_solution(5210613769687126782)
XLA Ops:
  0.6 3.6 %collective-permute-start.2 = (f32[48,32,128]{2,1,0:T(8,128)}, f32[48,32,128]{2,1,0:T(8,128)S(1)}, u32[]{:S(2)}, u32[]{:S(2)}) collective-permute-start(f32[48,32,128]{2,1,0:T(8,128)} %bitcast.17), channel_id=1, source_target_pairs={{0,28},{4,24},{8,20},{12,16},{16,12},{20,8},{24,4},{28,0},{1,29},{... | collective-permute-start | bytes 2359304 | tf_op jit(solution)/shard_map/ppermute | solution.py:571
  4.3 0.0 copy-start
  4.3 1.1 %copy-done = f32[3,1,16,32,128]{4,3,2,1,0:T(8,128)S(1)} copy-done((f32[3,1,16,32,128]{4,3,2,1,0:T(8,128)S(1)}, f32[3,1,16,32,128]{4,3,2,1,0:T(8,128)}, u32[]{:S(2)}) %copy-start) | copy-done | bytes 786456
  5.4 0.0 copy-start.2
  5.4 1.1 %copy-done.2 = f32[3,1,16,32,128]{4,3,2,1,0:T(8,128)S(1)} copy-done((f32[3,1,16,32,128]{4,3,2,1,0:T(8,128)S(1)}, f32[3,1,16,32,128]{4,3,2,1,0:T(8,128)}, u32[]{:S(2)}) %copy-start.2) | copy-done | bytes 786456
  6.5 0.0 copy-start.6
  6.5 0.7 %copy-done.6 = f32[32]{0:T(128)S(1)} copy-done((f32[32]{0:T(128)S(1)}, f32[32]{0:T(128)}, u32[]{:S(2)}) %copy-start.6) | copy-done | bytes 152
  7.2 0.0 copy-start.1
  7.2 0.1 edges.1
  7.3 2.1 %collective-permute-start = (f32[344,128]{1,0:T(8,128)S(1)}, f32[344,128]{1,0:T(8,128)S(1)}, u32[]{:S(2)}, u32[]{:S(2)}) collective-permute-start(f32[344,128]{1,0:T(8,128)S(1)} %get-tuple-element.25), channel_id=1, source_target_pairs={{0,4},{4,8},{8,12},{1,5},{5,9},{9,13},{2,6},{6,10},{10,14},{3,7},{... | collective-permute-start | bytes 528392 | tf_op jit(solution)/shard_map/ppermute | solution.py:599
  9.4 0.0 copy-start.3
  9.4 2.5 %collective-permute-start.1 = (f32[344,128]{1,0:T(8,128)S(1)}, f32[344,128]{1,0:T(8,128)S(1)}, u32[]{:S(2)}, u32[]{:S(2)}) collective-permute-start(f32[344,128]{1,0:T(8,128)S(1)} %get-tuple-element.26), channel_id=1, source_target_pairs={{4,0},{8,4},{12,8},{5,1},{9,5},{13,9},{6,2},{10,6},{14,10},{7,3},{... | collective-permute-start | bytes 528392 | tf_op jit(solution)/shard_map/ppermute | solution.py:600
  11.9 0.0 copy-done.1
  12.0 13.6 %collective-permute-done.before.refs_1_ = f32[344,128]{1,0:T(8,128)S(1)} collective-permute-done((f32[344,128]{1,0:T(8,128)S(1)}, f32[344,128]{1,0:T(8,128)S(1)}, u32[]{:S(2)}, u32[]{:S(2)}) %collective-permute-start) | collective-permute-done | bytes 176160 | tf_op jit(solution)/shard_map/ppermute | solution.py:599
  25.6 1.0 %collective-permute-done.1.after.refs_2_ = f32[344,128]{1,0:T(8,128)S(1)} collective-permute-done((f32[344,128]{1,0:T(8,128)S(1)}, f32[344,128]{1,0:T(8,128)S(1)}, u32[]{:S(2)}, u32[]{:S(2)}) %collective-permute-start.1) | collective-permute-done | bytes 176160 | tf_op jit(solution)/shard_map/ppermute | solution.py:600
  26.6 1.4 %collective-permute-start.5 = (f32[32,32,128]{2,1,0:T(8,128)S(1)}, f32[32,32,128]{2,1,0:T(8,128)S(1)}, u32[]{:S(2)}, u32[]{:S(2)}) collective-permute-start(f32[32,32,128]{2,1,0:T(8,128)S(1)} %hold.2), channel_id=1, source_target_pairs={{0,28},{4,24},{8,20},{12,16},{16,12},{20,8},{24,4},{28,0},{1,29},{... | collective-permute-start | bytes 1572872 | tf_op jit(solution)/shard_map/ppermute | solution.py:601
  28.0 0.0 collective-permute-done.2._.partner_1
  28.0 0.0 copy-done.3
  28.0 0.6 %edge_cells.1 = (f32[30,4,128]{2,1,0:T(4,128)S(1)}, f32[30,4,128]{2,1,0:T(4,128)S(1)}) custom-call(f32[48,32,128]{2,1,0:T(8,128)S(1)} %bitcast.20, f32[48,32,128]{2,1,0:T(8,128)S(1)} %bitcast.15, f32[344,128]{1,0:T(8,128)S(1)} %collective-permute-done.before.refs_1_, f32[344,128]{1,0:T(8,128)S(1)} %collective-permute-done.1.after.refs_2_, ...), custom_call_target="tpu_custom_call" | custom-call | tf_op jit(solution)/shard_map/edge_cells/pallas_call | solution.py:602
  28.7 0.0 copy-start.7
  28.7 1.3 %collective-permute-start.4 = (f32[30,4,128]{2,1,0:T(4,128)S(1)}, f32[30,4,128]{2,1,0:T(4,128)S(1)}, u32[]{:S(2)}, u32[]{:S(2)}) collective-permute-start(f32[30,4,128]{2,1,0:T(4,128)S(1)} %get-tuple-element.28), channel_id=1, source_target_pairs={{0,1},{1,2},{2,3},{3,0},{4,5},{5,6},{6,7},{7,4},{8,9},{9,10},{10,1... | collective-permute-start | bytes 184328 | tf_op jit(solution)/shard_map/ppermute | solution.py:620
  30.0 2.1 %collective-permute-start.3 = (f32[30,4,128]{2,1,0:T(4,128)S(1)}, f32[30,4,128]{2,1,0:T(4,128)S(1)}, u32[]{:S(2)}, u32[]{:S(2)}) collective-permute-start(f32[30,4,128]{2,1,0:T(4,128)S(1)} %get-tuple-element.27._), channel_id=1, source_target_pairs={{1,0},{2,1},{3,2},{0,3},{5,4},{6,5},{7,6},{4,7},{9,8},{10,9},{11,1... | collective-permute-start | bytes 184328 | tf_op jit(solution)/shard_map/ppermute | solution.py:621
  32.1 0.6 %own_tiles.1 = (f32[15,128,128]{2,1,0:T(8,128)S(1)}, f32[15,128,128]{2,1,0:T(8,128)S(1)}) custom-call(f32[48,32,128]{2,1,0:T(8,128)S(1)} %bitcast.21, f32[48,32,128]{2,1,0:T(8,128)S(1)} %bitcast.16, f32[344,128]{1,0:T(8,128)S(1)} %collective-permute-done.before.refs_1_, f32[344,128]{1,0:T(8,128)S(1)} %collective-permute-done.1.after.refs_2_, ...), custom_call_target="tpu_custom_call" | custom-call | tf_op jit(solution)/shard_map/own_tiles/pallas_call | solution.py:611
  32.8 0.0 copy-start.4
  32.8 1.0 %copy-done.4 = f32[15,128,128]{2,1,0:T(8,128)} copy-done((f32[15,128,128]{2,1,0:T(8,128)}, f32[15,128,128]{2,1,0:T(8,128)S(1)}, u32[]{:S(2)}) %copy-start.4) | copy-done | bytes 983064
  33.7 0.0 collective-permute-done.4.behind_cells
  33.8 0.0 collective-permute-done.3.ahead_cells
  33.8 0.0 copy-done.7
  33.8 0.1 bundle.1.refs_1_
  33.8 2.7 %collective-permute-start.7 = (f32[648,128]{1,0:T(8,128)S(1)}, f32[648,128]{1,0:T(8,128)S(1)}, u32[]{:S(2)}, u32[]{:S(2)}) collective-permute-start(f32[648,128]{1,0:T(8,128)S(1)} %bundle.1.refs_1_), channel_id=1, source_target_pairs={{0,28},{4,24},{8,20},{12,16},{16,12},{20,8},{24,4},{28,0},{1,29},{... | collective-permute-start | bytes 995336 | tf_op jit(solution)/shard_map/ppermute | solution.py:630
  36.6 0.7 %slice_bitcast_fusion.refs_0_ = f32[16,32,128]{2,1,0:T(8,128)} fusion(f32[3,1,16,32,128]{4,3,2,1,0:T(8,128)S(1)} %copy-done.1), kind=kLoop, calls=%fused_computation | loop fusion | bytes 524288 | tf_op jit(solution)/shard_map/slice | solution.py:573
  37.3 1.6 %collective-permute-done.5.refs_2_.partner_2 = f32[32,32,128]{2,1,0:T(8,128)S(1)} collective-permute-done((f32[32,32,128]{2,1,0:T(8,128)S(1)}, f32[32,32,128]{2,1,0:T(8,128)S(1)}, u32[]{:S(2)}, u32[]{:S(2)}) %collective-permute-start.5) | collective-permute-done | bytes 524320 | tf_op jit(solution)/shard_map/ppermute | solution.py:601
  38.9 2.4 %collective-permute-start.6 = (f32[16,32,128]{2,1,0:T(8,128)}, f32[16,32,128]{2,1,0:T(8,128)}, u32[]{:S(2)}, u32[]{:S(2)}) collective-permute-start(f32[16,32,128]{2,1,0:T(8,128)} %hold.3), channel_id=1, source_target_pairs={{0,28},{4,24},{8,20},{12,16},{16,12},{20,8},{24,4},{28,0},{1,29},{... | collective-permute-start | bytes 786440 | tf_op jit(solution)/shard_map/ppermute | solution.py:631
  41.3 0.1 pad_add_fusion.wall
  41.4 0.0 copy-start.5
  41.4 1.2 %copy-done.5 = f32[15,128,128]{2,1,0:T(8,128)S(1)} copy-done((f32[15,128,128]{2,1,0:T(8,128)S(1)}, f32[15,128,128]{2,1,0:T(8,128)}, u32[]{:S(2)}) %copy-start.5) | copy-done | bytes 983064
  42.6 1.5 %own_part.1 = (f32[15,152,128]{2,1,0:T(8,128)S(1)}, f32[15,152,128]{2,1,0:T(8,128)S(1)}, f32[15,152,128]{2,1,0:T(8,128)S(1)}, f32[45,152,128]{2,1,0:T(8,128)S(1)...) custom-call(s32[2]{0:T(128)S(1)} %pad_add_fusion.wall, f32[1,32]{1,0:T(1,128)S(1)} %bitcast.25, ...), custom_call_target="tpu_custom_call" | custom-call | tf_op jit(solution)/shard_map/own_part/pallas_call | solution.py:634
  44.1 1.9 %collective-permute-done.7.pack = f32[648,128]{1,0:T(8,128)S(1)} collective-permute-done((f32[648,128]{1,0:T(8,128)S(1)}, f32[648,128]{1,0:T(8,128)S(1)}, u32[]{:S(2)}, u32[]{:S(2)}) %collective-permute-start.7) | collective-permute-done | bytes 331808 | tf_op jit(solution)/shard_map/ppermute | solution.py:630
  46.1 3.9 %before_force.1 = (f32[15,152,128]{2,1,0:T(8,128)S(1)}, f32[15,152,128]{2,1,0:T(8,128)S(1)}, f32[15,152,128]{2,1,0:T(8,128)S(1)}, f32[15,152,128]{2,1,0:T(8,128)...) custom-call(f32[48,32,128]{2,1,0:T(8,128)S(1)} %collective-permute-d, ...), custom_call_target="tpu_custom_call" | custom-call | tf_op jit(solution)/shard_map/before_force/pallas_call | solution.py:644
  50.0 0.0 collective-permute-done.6.partner_last
  50.0 7.0 %with_force.1 = (f32[48,32,128]{2,1,0:T(8,128)}, f32[48,32,128]{2,1,0:T(8,128)}) custom-call(f32[16,32,128]{2,1,0:T(8,128)} %collective-permute-done.6.partner_last, f32[648,128]{1,0:T(8,128)S(1)} %collective-permute-done.7.pack, f32[15,152,128]{2,1,0:T(8,128)S(1)} %get-tuple-element.31.own_force, f32[5,8,128]{2,1,0:T(8,128)S(1)} %get-tuple-element.32.own_thick, ...), custom_call_target="tpu_custom_call" | custom-call | tf_op jit(solution)/shard_map/with_force/pallas_call | solution.py:656
  (3 shorter events, 0.0 us)
Async XLA Ops:
  0.6 27.4 %collective-permute-start.2 = (f32[48,32,128]{2,1,0:T(8,128)}, f32[48,32,128]{2,1,0:T(8,128)S(1)}, u32[]{:S(2)}, u32[]{:S(2)}) collective-permute-start(f32[48,32,128]{2,1,0:T(8,128)} %bitcast.17), channel_id=1, source_target_pairs={{0,28},{4,24},{8,20},{12,16},{16,12},{20,8},{24,4},{28,0},{1,29},{... | collective-permute-start | bytes 2359304 | tf_op jit(solution)/shard_map/ppermute | solution.py:571
  4.3 1.1 %copy-start = (f32[3,1,16,32,128]{4,3,2,1,0:T(8,128)S(1)}, f32[3,1,16,32,128]{4,3,2,1,0:T(8,128)}, u32[]{:S(2)}) copy-start(f32[3,1,16,32,128]{4,3,2,1,0:T(8,128)} %param.4) | copy-start | bytes 2359300
  5.4 1.1 %copy-start.2 = (f32[3,1,16,32,128]{4,3,2,1,0:T(8,128)S(1)}, f32[3,1,16,32,128]{4,3,2,1,0:T(8,128)}, u32[]{:S(2)}) copy-start(f32[3,1,16,32,128]{4,3,2,1,0:T(8,128)} %param.3) | copy-start | bytes 2359300
  6.5 0.7 %copy-start.6 = (f32[32]{0:T(128)S(1)}, f32[32]{0:T(128)}, u32[]{:S(2)}) copy-start(f32[32]{0:T(128)} %param.5) | copy-start | bytes 388
  7.2 4.8 %copy-start.1 = (f32[3,1,16,32,128]{4,3,2,1,0:T(8,128)S(1)}, f32[3,1,16,32,128]{4,3,2,1,0:T(8,128)}, u32[]{:S(2)}) copy-start(f32[3,1,16,32,128]{4,3,2,1,0:T(8,128)} %param.4) | copy-start | bytes 2359300
  7.3 18.3 %collective-permute-start = (f32[344,128]{1,0:T(8,128)S(1)}, f32[344,128]{1,0:T(8,128)S(1)}, u32[]{:S(2)}, u32[]{:S(2)}) collective-permute-start(f32[344,128]{1,0:T(8,128)S(1)} %get-tuple-element.25), channel_id=1, source_target_pairs={{0,4},{4,8},{8,12},{1,5},{5,9},{9,13},{2,6},{6,10},{10,14},{3,7},{... | collective-permute-start | bytes 528392 | tf_op jit(solution)/shard_map/ppermute | solution.py:599
  9.4 18.7 %copy-start.3 = (f32[3,1,16,32,128]{4,3,2,1,0:T(8,128)S(1)}, f32[3,1,16,32,128]{4,3,2,1,0:T(8,128)}, u32[]{:S(2)}) copy-start(f32[3,1,16,32,128]{4,3,2,1,0:T(8,128)} %param.3) | copy-start | bytes 2359300
  9.4 17.2 %collective-permute-start.1 = (f32[344,128]{1,0:T(8,128)S(1)}, f32[344,128]{1,0:T(8,128)S(1)}, u32[]{:S(2)}, u32[]{:S(2)}) collective-permute-start(f32[344,128]{1,0:T(8,128)S(1)} %get-tuple-element.26), channel_id=1, source_target_pairs={{4,0},{8,4},{12,8},{5,1},{9,5},{13,9},{6,2},{10,6},{14,10},{7,3},{... | collective-permute-start | bytes 528392 | tf_op jit(solution)/shard_map/ppermute | solution.py:600
  26.6 12.3 %collective-permute-start.5 = (f32[32,32,128]{2,1,0:T(8,128)S(1)}, f32[32,32,128]{2,1,0:T(8,128)S(1)}, u32[]{:S(2)}, u32[]{:S(2)}) collective-permute-start(f32[32,32,128]{2,1,0:T(8,128)S(1)} %hold.2), channel_id=1, source_target_pairs={{0,28},{4,24},{8,20},{12,16},{16,12},{20,8},{24,4},{28,0},{1,29},{... | collective-permute-start | bytes 1572872 | tf_op jit(solution)/shard_map/ppermute | solution.py:601
  28.7 5.1 %copy-start.7 = (f32[32]{0:T(128)S(1)}, f32[32]{0:T(128)}, u32[]{:S(2)}) copy-start(f32[32]{0:T(128)} %param.5) | copy-start | bytes 388
  28.7 5.1 %collective-permute-start.4 = (f32[30,4,128]{2,1,0:T(4,128)S(1)}, f32[30,4,128]{2,1,0:T(4,128)S(1)}, u32[]{:S(2)}, u32[]{:S(2)}) collective-permute-start(f32[30,4,128]{2,1,0:T(4,128)S(1)} %get-tuple-element.28), channel_id=1, source_target_pairs={{0,1},{1,2},{2,3},{3,0},{4,5},{5,6},{6,7},{7,4},{8,9},{9,10},{10,1... | collective-permute-start | bytes 184328 | tf_op jit(solution)/shard_map/ppermute | solution.py:620
  30.0 3.7 %collective-permute-start.3 = (f32[30,4,128]{2,1,0:T(4,128)S(1)}, f32[30,4,128]{2,1,0:T(4,128)S(1)}, u32[]{:S(2)}, u32[]{:S(2)}) collective-permute-start(f32[30,4,128]{2,1,0:T(4,128)S(1)} %get-tuple-element.27._), channel_id=1, source_target_pairs={{1,0},{2,1},{3,2},{0,3},{5,4},{6,5},{7,6},{4,7},{9,8},{10,9},{11,1... | collective-permute-start | bytes 184328 | tf_op jit(solution)/shard_map/ppermute | solution.py:621
  32.8 1.0 %copy-start.4 = (f32[15,128,128]{2,1,0:T(8,128)}, f32[15,128,128]{2,1,0:T(8,128)S(1)}, u32[]{:S(2)}) copy-start(f32[15,128,128]{2,1,0:T(8,128)S(1)} %get-tuple-element.30.speed_tiles) | copy-start | bytes 2949124
  33.8 12.3 %collective-permute-start.7 = (f32[648,128]{1,0:T(8,128)S(1)}, f32[648,128]{1,0:T(8,128)S(1)}, u32[]{:S(2)}, u32[]{:S(2)}) collective-permute-start(f32[648,128]{1,0:T(8,128)S(1)} %bundle.1.refs_1_), channel_id=1, source_target_pairs={{0,28},{4,24},{8,20},{12,16},{16,12},{20,8},{24,4},{28,0},{1,29},{... | collective-permute-start | bytes 995336 | tf_op jit(solution)/shard_map/ppermute | solution.py:630
  38.9 11.1 %collective-permute-start.6 = (f32[16,32,128]{2,1,0:T(8,128)}, f32[16,32,128]{2,1,0:T(8,128)}, u32[]{:S(2)}, u32[]{:S(2)}) collective-permute-start(f32[16,32,128]{2,1,0:T(8,128)} %hold.3), channel_id=1, source_target_pairs={{0,28},{4,24},{8,20},{12,16},{16,12},{20,8},{24,4},{28,0},{1,29},{... | collective-permute-start | bytes 786440 | tf_op jit(solution)/shard_map/ppermute | solution.py:631
  41.4 1.2 %copy-start.5 = (f32[15,128,128]{2,1,0:T(8,128)S(1)}, f32[15,128,128]{2,1,0:T(8,128)}, u32[]{:S(2)}) copy-start(f32[15,128,128]{2,1,0:T(8,128)} %copy-done.4) | copy-start | bytes 2949124
